TPU v7x, 1024 devices: a whole 8x8x8 slice. The times are simulated.
1024 devices in a mesh: dp: 64 (over y, z), expert: 16 (over x, core).
Axes of the slice: x: 8, y: 8, z: 8, core: 2. Of those that a mesh axis runs over, the one named last changes fastest.
Arguments:
- image_tokens: bfloat16 [1024, 256, 640], P(('dp', 'expert'))
- text_tokens: bfloat16 [1024, 16, 640], P(('dp', 'expert'))
- text_counts: int32 [1024], P(('dp', 'expert')), may hold values from 3 to 16, as said below
- pair_labels: int32 [1024], P(('dp', 'expert')), may hold values from 0 to 1023, as said below
- image_expert: int32 [1024, 256], P(('dp', 'expert')), may hold values from 0 to 15
- image_rank: int32 [1024, 256], P(('dp', 'expert')), may hold values from 0 to 20, as said below
- image_keep: int32 [1024, 256], P(('dp', 'expert')), may hold values from 0 to 1, as said below
- text_expert: int32 [1024, 16], P(('dp', 'expert')), may hold values from 0 to 15
- text_rank: int32 [1024, 16], P(('dp', 'expert')), may hold values from 0 to 2, as said below
- text_keep: int32 [1024, 16], P(('dp', 'expert')), may hold values from 0 to 1, as said below
- image_gate: float32 [1024, 256], P(('dp', 'expert')), may hold values from 0.2 to 1
- text_gate: float32 [1024, 16], P(('dp', 'expert')), may hold values from 0.2 to 1
- w_in: bfloat16 [16, 640, 2560], P('expert'), may hold values from -0.25 to 0.25
- w_out: bfloat16 [16, 2560, 640], P('expert'), may hold values from -0.125 to 0.125
Outputs:
- image_out: bfloat16 [1024, 256, 640], P(('dp', 'expert'))
- text_out: bfloat16 [1024, 16, 640], P(('dp', 'expert'))
- image_grad: float32 [1024, 640], P(('dp', 'expert'))
- text_grad: float32 [1024, 640], P(('dp', 'expert'))
Inputs may be any that keep to these rules, and one draw needn't show every extreme that they name: `text_counts`: every text has at least 3 valid tokens. `pair_labels`: each text index appears once. `image_rank`: the token's place, in batch-priority order, among the image tokens of its pair routed to the same expert, and 20 for every place past 20. In every aligned group of 16 blocks some expert holds 20 image tokens and 2 text tokens from each block. `image_keep`: 1 exactly where image_rank < 20. `text_rank`: the token's place, in order of position, among the valid text tokens of its pair routed to the same expert, 2 past 2 and for tokens past text_counts. `text_keep`: 1 exactly where text_rank < 2.
All inputs are finite; a program needn't handle non-finite values.
Results may differ from a plain program's by a relative error of at most 0.02.
Values may be sent and summed in bfloat16 or wider, within the bound.
No kernel may reach another device: no remote copies, remote signals or barrier semaphores. Data moves between devices by JAX's collectives and lax.ppermute only.
A program may use at most 32 MiB of HBM per device.

v0:
```python
import jax
import jax.numpy as jnp
from jax import lax
from jax.sharding import PartitionSpec as P

logit_scale = 10.0


def normalize(pooled):
    return (pooled / jnp.sqrt(jnp.sum(pooled * pooled, axis=1, keepdims=True) + 1e-06)).astype(
        jnp.bfloat16
    )


def against(left, right):
    return lax.dot_general(
        left, right, (((1,), (1,)), ((), ())), preferred_element_type=jnp.float32
    )


def per_device(
    image_tokens,
    text_tokens,
    text_counts,
    pair_labels,
    image_expert,
    image_rank,
    image_keep,
    text_expert,
    text_rank,
    text_keep,
    image_gate,
    text_gate,
    w_in,
    w_out,
):
    pairs_here, img_tok, feat_width = image_tokens.shape
    txt_tok = text_tokens.shape[1]
    owners = lax.axis_size("expert")
    cap_img = 5 * pairs_here * img_tok // (4 * owners)
    slot_count = cap_img + 2 * pairs_here
    img_rows = pairs_here * img_tok
    tokens = jnp.concatenate(
        [
            image_tokens.reshape(img_rows, feat_width),
            text_tokens.reshape(pairs_here * txt_tok, feat_width),
        ],
        0,
    )
    target = jnp.concatenate(
        [
            image_expert.reshape(-1) * slot_count + image_rank.reshape(-1),
            text_expert.reshape(-1) * slot_count + cap_img + text_rank.reshape(-1),
        ]
    )
    keep_flags = jnp.concatenate([image_keep.reshape(-1), text_keep.reshape(-1)])
    gate_vals = jnp.concatenate([image_gate.reshape(-1), text_gate.reshape(-1)])
    columns = lax.broadcasted_iota(jnp.int32, (tokens.shape[0], owners * slot_count), 1)
    dispatch = ((columns == target[:, None]) & (keep_flags[:, None] == 1)).astype(jnp.bfloat16)
    packed = lax.dot_general(
        dispatch, tokens, (((0,), (0,)), ((), ())), preferred_element_type=jnp.float32
    )
    packed = packed.astype(jnp.bfloat16).reshape(owners, slot_count, feat_width)
    weight_in = w_in[0]
    weight_out = w_out[0]
    received = lax.all_to_all(packed, "expert", split_axis=0, concat_axis=0, tiled=True)
    source_count, item_count, _ = received.shape
    flat_rows = received.reshape(source_count * item_count, feat_width)
    hidden = jax.nn.gelu(
        jnp.dot(flat_rows, weight_in, preferred_element_type=jnp.float32), approximate=False
    ).astype(jnp.bfloat16)
    result = jnp.dot(hidden, weight_out, preferred_element_type=jnp.float32).astype(jnp.bfloat16)
    returned = lax.all_to_all(
        result.reshape(source_count, item_count, feat_width),
        "expert",
        split_axis=0,
        concat_axis=0,
        tiled=True,
    )
    picked = jnp.dot(
        dispatch,
        returned.reshape(owners * slot_count, feat_width),
        preferred_element_type=jnp.float32,
    )
    combined = tokens.astype(jnp.float32) + gate_vals[:, None] * picked
    image_part = combined[:img_rows].reshape(pairs_here, img_tok, feat_width)
    text_part = combined[img_rows:].reshape(pairs_here, txt_tok, feat_width)
    image_out = image_part.astype(jnp.bfloat16)
    text_out = text_part.astype(jnp.bfloat16)
    valid_flags = (
        lax.broadcasted_iota(jnp.int32, (pairs_here, txt_tok), 1) < text_counts[:, None]
    ).astype(jnp.float32)
    image_emb = normalize(jnp.mean(image_part, axis=1))
    text_emb = normalize(
        jnp.sum(text_part * valid_flags[:, :, None], axis=1)
        / text_counts.astype(jnp.float32)[:, None]
    )
    image_sent, label_sent = (
        lax.all_gather(image_emb.astype(jnp.float32), "expert", axis=0, tiled=True),
        lax.all_gather(pair_labels.astype(jnp.float32), "expert", axis=0, tiled=True),
    )
    image_rows = image_sent.astype(jnp.bfloat16)
    label_rows = label_sent.astype(jnp.int32)
    text_cols = lax.all_gather(text_emb, "dp", axis=0, tiled=True)
    col_count = text_cols.shape[0]
    exp_scores = jnp.exp(logit_scale * against(image_rows, text_cols))
    row_totals = lax.psum(jnp.sum(exp_scores, axis=1), "expert")
    column_totals = lax.psum(jnp.sum(exp_scores, axis=0), "dp")
    col_pos = lax.broadcasted_iota(jnp.int32, (1, col_count), 1)
    col_global = (
        col_pos // pairs_here * owners + lax.axis_index("expert")
    ) * pairs_here + col_pos % pairs_here
    matches = (label_rows[:, None] == col_global).astype(jnp.float32)
    scores = (
        exp_scores / row_totals[:, None] + exp_scores / column_totals[None, :] - 2.0 * matches
    ).astype(jnp.bfloat16)
    image_grad = lax.psum_scatter(
        jnp.dot(scores, text_cols, preferred_element_type=jnp.float32),
        "expert",
        scatter_dimension=0,
        tiled=True,
    )
    text_grad = lax.psum_scatter(
        lax.dot_general(
            scores, image_rows, (((0,), (0,)), ((), ())), preferred_element_type=jnp.float32
        ),
        "dp",
        scatter_dimension=0,
        tiled=True,
    )
    return (image_out, text_out, image_grad, text_grad)


def solution(mesh):
    return jax.shard_map(
        per_device,
        mesh=mesh,
        in_specs=(
            P(("dp", "expert"), None, None),
            P(("dp", "expert"), None, None),
            P(("dp", "expert")),
            P(("dp", "expert")),
            P(("dp", "expert"), None),
            P(("dp", "expert"), None),
            P(("dp", "expert"), None),
            P(("dp", "expert"), None),
            P(("dp", "expert"), None),
            P(("dp", "expert"), None),
            P(("dp", "expert"), None),
            P(("dp", "expert"), None),
            P("expert", None, None),
            P("expert", None, None),
        ),
        out_specs=(
            P(("dp", "expert"), None, None),
            P(("dp", "expert"), None, None),
            P(("dp", "expert"), None),
            P(("dp", "expert"), None),
        ),
        check_vma=False,
    )
```

profile of v0, /device:TPU:1, one launch (start us, length us, event | category | flops | bytes accessed | tf_op | source)
XLA Modules:
  0.0 487.6 jit_solution(12878135185409554494)
XLA Ops:
  7.2 0.0 copy-start
  7.2 0.9 add_compare_fusion
  8.0 0.8 add_bitcast_fusion
  8.9 0.7 multiply_add_fusion
  9.6 2.3 convolution_convert_fusion
  11.9 1.9 reshape.193
  13.8 34.9 %all_to_all.10 = bf16[16,22,640]{2,1,0:T(8,128)(2,1)} all-to-all(bf16[16,22,640]{2,1,0:T(8,128)(2,1)} %reshape.193), channel_id=1, replica_groups=mesh['dp'=64,'expert'=16] {'expert'}, dimensions={0} | all-to-all | bytes 901120 | tf_op jit(solution)/shard_map/all_to_all | solution.py:66
  48.7 1.9 reshape.194
  50.6 0.0 copy-done
  50.6 0.0 copy-start.2
  50.6 0.0 copy-start.3
  50.6 0.0 copy-start.4
  50.6 12.4 %fusion.49 = bf16[352,640]{1,0:T(8,128)(2,1)} fusion(bf16[1,2560,640]{2,1,0:T(8,128)(2,1)S(1)} %copy-done, bf16[352,640]{1,0:T(8,128)(2,1)} %reshape.194, bf16[1,640,2560]{2,1,0:T(8,128)(2,1)} %param.26), kind=kOutput, calls=%fused_computation.55 | convolution fusion | flops 2365665280 | bytes 7454720 | tf_op jit(solution)/shard_map/dot_general | solution.py:72
  63.1 1.9 reshape.195
  65.0 4.1 all-to-all-start.1
  69.1 0.0 all-reduce.6.cloned.1.call-start
  70.5 1.4 dynamic-slice.3
  71.8 1.4 fusion.108
  73.3 0.9 convert_dynamic-update-slice_fusion
  74.2 0.0 copy-done.2
  74.2 0.0 copy-done.3
  74.2 10.5 %all-to-all-done.1 = bf16[16,22,640]{2,1,0:T(8,128)(2,1)} async-done(((bf16[16,22,640]{2,1,0:T(8,128)(2,1)}), bf16[16,22,640]{2,1,0:T(8,128)(2,1)}, u32[]{:S(2)}, u32[]{:S(2)}) %all-to-all-start.1) | async-done | bytes 450592 | tf_op jit(solution)/shard_map/all_to_all | solution.py:73
  84.6 1.9 reshape.196
  86.6 0.0 copy-done.4
  86.6 1.5 fusion.48
  88.1 0.0 copy-start.1
  88.1 0.1 slice_reduce_fusion
  88.2 0.9 fusion.60
  89.1 0.0 copy-done.1
  89.1 0.1 multiply_reduce_fusion
  89.2 0.6 multiply_reduce_fusion.1
  90.5 0.6 multiply_reduce_fusion.2
  91.8 14.6 %all-gather.2 = bf16[16,1,640]{2,1,0:T(2,128)(2,1)S(1)} all-gather(bf16[1,1,640]{2,1,0:T(2,128)(2,1)S(1)} %reshape.204), channel_id=2, replica_groups=mesh['dp'=64,'expert'=16] {'expert'}, dimensions={0}, use_global_device_ids=true | all-gather | bytes 21760 | tf_op jit(solution)/shard_map/all_gather | solution.py:99
  106.4 41.2 %all-gather.3 = bf16[64,1,640]{2,1,0:T(2,128)(2,1)S(1)} all-gather(bf16[1,1,640]{2,1,0:T(2,128)(2,1)S(1)} %reshape.206), channel_id=3, replica_groups=mesh['dp'=64,'expert'=16] {'dp'}, dimensions={0}, use_global_device_ids=true | all-gather | bytes 83200 | tf_op jit(solution)/shard_map/all_gather | solution.py:104
  147.6 0.3 fusion.107
  147.8 35.5 %all-reduce.3 = (f32[16]{0:T(128)S(1)}, f32[16]{0:T(128)S(1)}) all-reduce(f32[16]{0:T(128)S(1)} %get-tuple-element.4, f32[16]{0:T(128)S(1)} %convert_dynamic-update-slice_fusion), channel_id=1, replica_groups=mesh['dp'=64,'expert'=16] {'expert'}, use_global_device_ids=true, to_apply=%region_5.0 | all-reduce | flops 32 | bytes 256 | tf_op jit(solution)/shard_map/psum | solution.py:107
  183.4 112.6 %psum.15 = f32[64]{0:T(128)S(1)} all-reduce(f32[64]{0:T(128)S(1)} %get-tuple-element.5), channel_id=1, replica_groups=mesh['dp'=64,'expert'=16] {'dp'}, use_global_device_ids=true, to_apply=%region_7.0 | all-reduce | flops 64 | bytes 512 | tf_op jit(solution)/shard_map/psum | solution.py:108
  296.0 0.2 fusion.65
  296.2 1.0 fusion.72
  297.1 0.0 all-reduce.6.cloned.1.call-update
  297.2 1.4 fusion.70
  298.6 71.4 %all-reduce.1 = f32[16,640]{1,0:T(8,128)S(1)} all-reduce(f32[16,640]{1,0:T(8,128)S(1)} %fusion.65), channel_id=4, replica_groups=mesh['dp'=64,'expert'=16] {'expert'}, use_global_device_ids=true, to_apply=%region_8.9.clone | all-reduce | flops 10240 | bytes 81920
  370.0 1.3 constant_dynamic-slice_fusion.1
  371.3 107.5 %all-reduce.6.cloned.1.call-done = f32[64,640]{1,0:T(8,128)} async-done(((f32[64,640]{1,0:T(8,128)}), f32[64,640]{1,0:T(8,128)}) %all-reduce.6.cloned.1.call-update) | async-done | bytes 163856
  478.8 2.0 constant_dynamic-slice_fusion
  (10 shorter events, 0.1 us)
Async XLA Ops:
  7.2 43.5 %copy-start = (bf16[1,2560,640]{2,1,0:T(8,128)(2,1)S(1)}, bf16[1,2560,640]{2,1,0:T(8,128)(2,1)}, u32[]{:S(2)}) copy-start(bf16[1,2560,640]{2,1,0:T(8,128)(2,1)} %param.27) | copy-start | bytes 9830404
  50.6 23.5 %copy-start.2 = (f32[1,256]{1,0:T(1,128)S(1)}, f32[1,256]{1,0:T(1,128)}, u32[]{:S(2)}) copy-start(f32[1,256]{1,0:T(1,128)} %param.24) | copy-start | bytes 3076
  50.6 23.6 %copy-start.3 = (f32[1,16]{1,0:T(1,128)S(1)}, f32[1,16]{1,0:T(1,128)}, u32[]{:S(2)}) copy-start(f32[1,16]{1,0:T(1,128)} %param.25) | copy-start | bytes 196
  50.6 36.0 %copy-start.4 = (bf16[1,16,640]{2,1,0:T(8,128)(2,1)S(1)}, bf16[1,16,640]{2,1,0:T(8,128)(2,1)}, u32[]{:S(2)}) copy-start(bf16[1,16,640]{2,1,0:T(8,128)(2,1)} %param.15) | copy-start | bytes 61444
  65.0 19.6 %all-to-all-start.1 = ((bf16[16,22,640]{2,1,0:T(8,128)(2,1)}), bf16[16,22,640]{2,1,0:T(8,128)(2,1)}, u32[]{:S(2)}, u32[]{:S(2)}) async-start(bf16[16,22,640]{2,1,0:T(8,128)(2,1)} %reshape.195), calls=%async_computation.1 | async-start | bytes 983040 | tf_op jit(solution)/shard_map/all_to_all | solution.py:73
  69.1 409.6 %all-reduce.6.cloned.1.call-start = ((), (), s32[]{:S(2)}) async-start(), calls=%async_computation.2 | async-start | bytes 327680
  88.1 1.0 copy-start.1
Sparse Core Ops, SparseCore 0:
  297.3 181.4 all-reduce.5
where the time goes:
time: 492 us; the launch traced here: 488 us
  blocking collectives  310 us (63%)
  waiting for transfers between devices  118 us (24%)
  matrix products  17.7 us (4%)
  between operations  16.9 us (3%)
  local copies, waits for them, and re-layouts  16.1 us (3%)
    psum x1, blocking collectives, per_device(): column_totals = lax.psum(jnp.sum(exp_scores, axis=0), 'dp')  113 us
    unnamed x2, waiting for transfers between devices  108 us
    unnamed x1, blocking collectives  71.4 us
    all_gather x1, blocking collectives, per_device(): text_cols = lax.all_gather(text_emb, 'dp', axis=0, tiled=True)  41.2 us
    psum x1, blocking collectives, per_device(): row_totals = lax.psum(jnp.sum(exp_scores, axis=1), 'expert')  35.5 us
    all_to_all x1, blocking collectives, per_device(): lax.all_to_all(packed, 'expert', split_axis=0, concat_axis=0, tiled=True)  34.9 us
    all_gather x1, blocking collectives, per_device(): lax.all_gather(image_emb.astype(jnp.float32), 'expert', axis=0, tiled=True)  14.6 us
    dot_general x1, matrix products, per_device(): jnp.dot(hidden, weight_out, preferred_element_type=jnp.float32)  12.4 us
  transfers between devices with their start and end apart: 2, of which 2 were waited for; matrix products, arithmetic and copies ran while one was open for 1% of the time, Pallas kernels for 0%

commit v1 on v0

v1 whole, which is shorter than its diff:
```python
import jax
import jax.numpy as jnp
import numpy as np
from jax import lax
from jax.experimental import pallas as pl
from jax.experimental.pallas import tpu as pltpu
from jax.sharding import PartitionSpec as P

logit_scale = 10.0
f32, bf16, i32 = jnp.float32, jnp.bfloat16, jnp.int32
NT = (((1,), (1,)), ((), ()))
TN = (((0,), (0,)), ((), ()))
NN = (((1,), (0,)), ((), ()))


def dot(left, right, dims=NN):
    return lax.dot_general(left, right, dims, preferred_element_type=f32)


def iota(shape, dim):
    return lax.broadcasted_iota(i32, shape, dim)


def one_hot(mask):
    return jnp.where(mask, 1.0, 0.0).astype(bf16)


def three_parts(value):
    high = value.astype(bf16)
    rest = value - high.astype(f32)
    middle = rest.astype(bf16)
    low = (rest - middle.astype(f32)).astype(bf16)
    return high, middle, low


class Sizes:
    def __init__(self, owners, lines, img_tok, txt_tok, feat):
        self.owners, self.lines = owners, lines
        self.cores = 2
        self.nx = owners // self.cores
        self.ny = 1 << ((lines.bit_length() - 1 + 1) // 2)
        self.nz = lines // self.ny
        self.img_tok, self.txt_tok, self.feat = img_tok, txt_tok, feat
        self.cap = 5 * img_tok // (4 * owners)
        self.slots = self.cap + 2
        self.stride = -(-(self.slots + 2) // 8) * 8
        self.rows = owners * self.stride
        self.half = self.nx * lines
        self.pairs = owners * lines


def slot_masks(sz, img_expert, img_rank, img_keep, txt_expert, txt_rank, txt_keep):
    img_target = img_expert * sz.stride + img_rank
    txt_target = txt_expert * sz.stride + sz.cap + txt_rank
    img_target = jnp.where(img_keep == 1, img_target, -1)
    txt_target = jnp.where(txt_keep == 1, txt_target, -1)
    return (
        one_hot(iota((sz.rows, sz.img_tok), 0) == img_target),
        one_hot(iota((sz.rows, sz.txt_tok), 0) == txt_target),
    )


def dispatch_kernel(sz, count_ref, label_ref, ie, ir, ik, te, tr, tk, ig, tg, img, txt, packed, means):
    img_mask, txt_mask = slot_masks(sz, ie[...], ir[...], ik[...], te[...], tr[...], tk[...])
    count = count_ref[0]
    count_f = jnp.full((1, 1), count, i32).astype(f32)
    label = label_ref[0]
    img_weight = jnp.where(ik[...] == 1, ig[...], 0.0) * (1.0 / sz.img_tok)
    valid = iota((1, sz.txt_tok), 1) < count
    txt_weight = jnp.where((tk[...] == 1) & valid, tg[...], 0.0) / count_f
    img_place = one_hot(iota((128, sz.img_tok), 0) == ir[...])
    txt_place = one_hot(iota((128, sz.txt_tok), 0) == tr[...] + sz.cap)
    img_at = iota((sz.owners, sz.img_tok), 0) == ie[...]
    txt_at = iota((sz.owners, sz.txt_tok), 0) == te[...]
    tables = []
    for img_part, txt_part in zip(three_parts(img_weight), three_parts(txt_weight)):
        img_side = jnp.where(img_at, img_part.astype(f32), 0.0).astype(bf16)
        txt_side = jnp.where(txt_at, txt_part.astype(f32), 0.0).astype(bf16)
        tables.append(dot(img_side, img_place, NT) + dot(txt_side, txt_place, NT))
    pad = sz.feat - 3 * 128
    if pad:
        tables.append(jnp.zeros((sz.owners, pad), f32))
    weights = jnp.concatenate(tables, 1).astype(bf16)
    lane = iota((sz.owners, sz.feat), 1)
    label_row = jnp.where(
        lane < 128,
        (label >> 5).astype(f32),
        jnp.where(lane < 256, (label & 31).astype(f32), 0.0),
    ).astype(bf16)
    row = iota((sz.rows, sz.owners), 0)
    block = iota((sz.rows, sz.owners), 1) * sz.stride
    out = dot(img_mask, img[...]) + dot(txt_mask, txt[...])
    out = out + dot(one_hot(row == block + sz.slots), weights)
    out = out + dot(one_hot(row == block + sz.slots + 1), label_row)
    packed[...] = out.astype(bf16)
    img_mean = dot(jnp.ones((8, sz.img_tok), bf16), img[...]) * (1.0 / sz.img_tok)
    counted = one_hot(iota((8, sz.txt_tok), 1) < count)
    txt_mean = dot(counted, txt[...]) / count_f
    means[...] = jnp.where(iota((8, sz.feat), 0) == 0, img_mean, txt_mean)


def gelu(x):
    return 0.5 * x * (1.0 + lax.erf(x * np.float32(np.sqrt(0.5))))


def expert_kernel(sz, chunk, x_ref, w_in, w_out, means, rows_ref, pool_ref, label_ref, total):
    step = pl.program_id(0)

    @pl.when(step == 0)
    def _():
        total[...] = jnp.zeros_like(total)

    x = x_ref[...]
    width = w_in.shape[1]
    part = None
    for at in range(0, width, chunk):
        hidden = gelu(dot(x, w_in[:, at : at + chunk])).astype(bf16)
        term = dot(hidden, w_out[at : at + chunk, :])
        part = term if part is None else part + term
    total[...] += part

    @pl.when(step == pl.num_programs(0) - 1)
    def _():
        out = total[...].astype(bf16)
        rows_ref[...] = out
        count = 2 * sz.owners
        r = iota((count, sz.rows), 0)
        c = iota((count, sz.rows), 1)
        magic = -(-65536 // sz.stride)
        assert all((v * magic) >> 16 == v // sz.stride for v in range(sz.rows))
        block = (c * magic) >> 16
        place = c - block * sz.stride
        is_txt = (r & sz.nx) > 0
        source = (r & (sz.nx - 1)) * sz.cores + jnp.where(r >= 2 * sz.nx, 1, 0)
        held = dot(one_hot(c == source * sz.stride + sz.slots), x)
        lane = iota((128, sz.rows), 1)
        lane_place = lane - ((lane * magic) >> 16) * sz.stride
        spread = one_hot(iota((128, sz.rows), 0) == lane_place)
        own = (block == source) & (
            jnp.where(is_txt, 1, 0) == jnp.where(place >= sz.cap, 1, 0)
        ) & (place < sz.slots)
        pool = jnp.zeros((count, sz.feat), f32)
        for part_at in range(3):
            piece = held[:, part_at * 128 : (part_at + 1) * 128].astype(bf16)
            weight = jnp.where(own, dot(piece, spread), 0.0).astype(bf16)
            pool = pool + dot(weight, out)
        me = lax.axis_index("expert")
        line = lax.axis_index("dp")
        my_x, my_core = me >> 1, me & 1
        row = iota((count, sz.feat), 0)
        my_row = my_core * (2 * sz.nx) + my_x
        pool = pool + jnp.where(row == my_row, means[0:1, :], 0.0)
        pool = pool + jnp.where(row == my_row + sz.nx, means[1:2, :], 0.0)
        pool_ref[...] = pool
        r8 = iota((sz.nx, sz.rows), 0)
        c8 = iota((sz.nx, sz.rows), 1)
        labels = dot(one_hot(c8 == (r8 * sz.cores + my_core) * sz.stride + sz.slots + 1), x)
        lane = iota((sz.nx, sz.feat), 1)
        label_ref[...] = jnp.where((lane == line) | (lane == line + 128), labels, 0.0).astype(bf16)


def normalize_kernel(sz, mine, theirs, label, out):
    pooled = mine[...] + theirs[...]
    norm = jnp.sqrt(jnp.sum(pooled * pooled, axis=1, keepdims=True) + 1e-06)
    out[...] = jnp.concatenate([(pooled / norm).astype(bf16), label[...]], 0)


def combine_kernel(sz, ie, ir, ik, te, tr, tk, ig, tg, img, txt, returned, img_out, txt_out):
    img_mask, txt_mask = slot_masks(sz, ie[...], ir[...], ik[...], te[...], tr[...], tk[...])
    back = returned[...]
    for mask, gate, tokens, out in ((img_mask, ig, img, img_out), (txt_mask, tg, txt, txt_out)):
        count = tokens.shape[0]
        picked = dot(mask, back, TN)
        column = jnp.transpose(jnp.broadcast_to(gate[...], (128, count)))[:, 0:1]
        out[...] = (tokens[...].astype(f32) + column * picked).astype(bf16)


def reverse(value, width):
    bits = [((value >> b) & 1) << (width - 1 - b) for b in range(width)]
    out = bits[0]
    for b in bits[1:]:
        out = out | b
    return out


def merge_kernel(count, held, got, out):
    out[...] = jnp.concatenate(
        [
            held[:count, :],
            got[:count, :],
            held[count : 2 * count, :],
            got[count : 2 * count, :],
            held[2 * count :, :] + got[2 * count :, :],
        ],
        0,
    )


def head_kernel(sz, label_ref, mine_held, mine_got, theirs_held, theirs_got, img_grad, txt_grad, column_scores):
    half = sz.half
    tile = half // 2
    me = lax.axis_index("expert")
    line = lax.axis_index("dp")
    my_x, my_core = me >> 1, me & 1
    y_bits, z_bits = sz.ny.bit_length() - 1, sz.nz.bit_length() - 1
    pair = line * sz.owners + me

    def position(other_line, other_x, other_core):
        apart_y = reverse((other_line >> z_bits) ^ (line >> z_bits), y_bits)
        apart_z = reverse((other_line & (sz.nz - 1)) ^ (line & (sz.nz - 1)), z_bits)
        block = jnp.where(
            other_core == 0, apart_y | (apart_z << y_bits), apart_z | (apart_y << z_bits)
        )
        return jnp.where(other_core == my_core, 0, half) + block * sz.nx + other_x

    parts = (mine_held, mine_got, theirs_held, theirs_got)
    width = column_scores.shape[1]
    column_totals = [jnp.zeros((1, tile), f32) for _ in parts]
    row_totals = []
    strip = []
    for a, left in enumerate(parts):
        images = left[:tile, :]
        sums = jnp.zeros((tile, 1), f32)
        for b, right in enumerate(parts):
            scores = jnp.exp(logit_scale * dot(images, right[tile : 2 * tile, :], NT))
            sums = sums + jnp.sum(scores, axis=1, keepdims=True)
            column_totals[b] = column_totals[b] + jnp.sum(scores, axis=0, keepdims=True)
            if b == 0:
                column_scores[a * tile : (a + 1) * tile, :] = scores[:, :width]
            if a == 0:
                strip.append(scores[: sz.nx, :])
        row_totals.append(sums)

    label = label_ref[0]
    owner = label & (sz.owners - 1)
    target = position(label >> (sz.owners.bit_length() - 1), owner >> 1, owner & 1)
    grad = jnp.zeros((sz.nx, sz.feat), f32)
    for b, right in enumerate(parts):
        match = jnp.where(iota((sz.nx, tile), 1) + b * tile == target, 2.0, 0.0)
        scores = strip[b] / row_totals[0][: sz.nx] + strip[b] / column_totals[b] - match
        grad = grad + dot(scores.astype(bf16), right[tile : 2 * tile, :])
    chosen = iota((sz.nx, sz.feat), 0) == my_x
    img_grad[...] = jnp.sum(jnp.where(chosen, grad, 0.0), axis=0, keepdims=True)

    lane = iota((sz.nx, 128), 1)
    sub = iota((sz.nx, 128), 0)
    found_line = jnp.zeros((1, 1), i32)
    found_x = jnp.zeros((1, 1), i32)
    found_theirs = jnp.zeros((1, 1), i32)
    high, low = (pair >> 5).astype(f32), (pair & 31).astype(f32)
    for b in range(2):
        held, got = parts[2 * b], parts[2 * b + 1]
        names = held[2 * tile :, 0:256].astype(f32) + got[2 * tile :, 0:256].astype(f32)
        hit = (names[:, :128] == high) & (names[:, 128:] == low) & (lane < sz.lines)

        def total(value):
            value = jnp.where(hit, value, 0.0)
            return jnp.sum(jnp.sum(value, axis=0, keepdims=True), axis=1, keepdims=True).astype(i32)

        found_line = found_line + total(lane.astype(f32))
        found_x = found_x + total(sub.astype(f32))
        if b == 1:
            found_theirs = total(jnp.ones((sz.nx, 128), f32))
    found_core = jnp.where(found_theirs > 0, 1 - my_core, my_core)
    named = position(found_line, found_x, found_core)
    grad = jnp.zeros((width, sz.feat), f32)
    for a, left in enumerate(parts):
        rows = column_scores[a * tile : (a + 1) * tile, :]
        match = jnp.where(iota((tile, width), 0) + a * tile == named, 2.0, 0.0)
        scores = rows / row_totals[a] + rows / column_totals[0][:, :width] - match
        grad = grad + dot(scores.astype(bf16), left[:tile, :], TN)
    txt_grad[...] = jnp.sum(jnp.where(chosen, grad[: sz.nx], 0.0), axis=0, keepdims=True)


def call(kernel, out_shape, in_specs=None, cost=None, limit=24, **kw):
    if cost is not None:
        kw["cost_estimate"] = pl.CostEstimate(flops=cost[0], bytes_accessed=cost[1], transcendentals=cost[2])
    if in_specs is not None:
        kw["in_specs"] = in_specs
    return pl.pallas_call(
        kernel,
        out_shape=out_shape,
        compiler_params=pltpu.CompilerParams(vmem_limit_bytes=limit << 20),
        **kw,
    )


def bind(kernel, *head):
    def bound(*refs):
        return kernel(*head, *refs)

    return bound


def swap(value, sz, partner):
    pairs = []
    for y in range(sz.ny):
        for z in range(sz.nz):
            for x in range(sz.nx):
                for core in range(sz.cores):
                    py, pz, px, pcore = partner(y, z, x, core)
                    rank = ((y * sz.nz + z) * sz.nx + x) * sz.cores + core
                    pairs.append((rank, ((py * sz.nz + pz) * sz.nx + px) * sz.cores + pcore))
    return lax.ppermute(value, ("dp", "expert"), pairs)


def masks(count):
    out = []
    while count > 1:
        count //= 2
        out.append(count)
    return out


def per_device(
    image_tokens,
    text_tokens,
    text_counts,
    pair_labels,
    image_expert,
    image_rank,
    image_keep,
    text_expert,
    text_rank,
    text_keep,
    image_gate,
    text_gate,
    w_in,
    w_out,
):
    _, img_tok, feat = image_tokens.shape
    txt_tok = text_tokens.shape[1]
    sz = Sizes(lax.axis_size("expert"), lax.axis_size("dp"), img_tok, txt_tok, feat)
    ff = w_in.shape[2]
    img, txt = image_tokens[0], text_tokens[0]
    routes = (image_expert, image_rank, image_keep, text_expert, text_rank, text_keep)
    gates = (image_gate, text_gate)
    vmem = pl.BlockSpec(memory_space=pltpu.VMEM)
    smem = pl.BlockSpec(memory_space=pltpu.SMEM)
    packed, means = call(
        bind(dispatch_kernel, sz),
        (
            jax.ShapeDtypeStruct((sz.rows, feat), bf16),
            jax.ShapeDtypeStruct((8, feat), f32),
        ),
        in_specs=[smem, smem] + [vmem] * 10,
        name="dispatch",
    )(text_counts, pair_labels, *routes, *gates, img, txt)

    def exchange(rows):
        rows = rows.reshape(sz.owners, sz.stride, feat)
        rows = lax.all_to_all(rows, "expert", split_axis=0, concat_axis=0, tiled=True)
        return rows.reshape(sz.rows, feat)

    received = exchange(packed)
    block = min(512, ff)
    whole = lambda shape: pl.BlockSpec(shape, lambda i: (0, 0))
    rows, pools, labels = call(
        bind(expert_kernel, sz, min(256, block)),
        (
            jax.ShapeDtypeStruct((sz.rows, feat), bf16),
            jax.ShapeDtypeStruct((2 * sz.owners, feat), f32),
            jax.ShapeDtypeStruct((sz.nx, feat), bf16),
        ),
        grid=(ff // block,),
        in_specs=[
            whole((sz.rows, feat)),
            pl.BlockSpec((feat, block), lambda i: (0, i)),
            pl.BlockSpec((block, feat), lambda i: (i, 0)),
            whole((8, feat)),
        ],
        out_specs=[
            whole((sz.rows, feat)),
            whole((2 * sz.owners, feat)),
            whole((sz.nx, feat)),
        ],
        scratch_shapes=[pltpu.VMEM((sz.rows, feat), f32)],
        name="expert",
    )(received, w_in[0], w_out[0], means)

    core = lax.axis_index("expert") & 1
    per_core = 2 * sz.nx
    mine = lax.dynamic_slice_in_dim(pools, core * per_core, per_core, 0)
    others = lax.dynamic_slice_in_dim(pools, (1 - core) * per_core, per_core, 0)
    theirs = swap(others, sz, lambda y, z, x, c: (y, z, x, 1 - c))
    for mask in masks(sz.nx):
        mine = mine + theirs
        theirs = swap(mine, sz, lambda y, z, x, c: (y, z, x ^ mask, c))
    held = call(
        bind(normalize_kernel, sz),
        jax.ShapeDtypeStruct((3 * sz.nx, feat), bf16),
        name="normalize",
    )(mine, theirs, labels)

    rows, held = lax.optimization_barrier((rows, held))
    returned = exchange(rows)
    img_out, txt_out = call(
        bind(combine_kernel, sz),
        (
            jax.ShapeDtypeStruct((img_tok, feat), bf16),
            jax.ShapeDtypeStruct((txt_tok, feat), bf16),
        ),
        cost=(2 * sz.rows * (img_tok + txt_tok) * feat, 4 * sz.rows * feat, 0),
        name="combine",
    )(*routes, *gates, img, txt, returned)

    def across(value):
        return swap(value, sz, lambda y, z, x, c: (y, z, x, 1 - c))

    count = sz.nx
    for second in (False, True):
        for y_mask, z_mask in zip(masks(sz.ny), masks(sz.nz)):

            def partner(y, z, x, c):
                if (c == 0) != second:
                    return (y ^ y_mask, z, x, c)
                return (y, z ^ z_mask, x, c)

            got = swap(held, sz, partner)
            if 2 * count < sz.half:
                held = call(
                    bind(merge_kernel, count),
                    jax.ShapeDtypeStruct((4 * count + sz.nx, feat), bf16),
                    name="merge",
                )(held, got)
            count *= 2
    img_grad, txt_grad = call(
        bind(head_kernel, sz),
        (
            jax.ShapeDtypeStruct((1, feat), f32),
            jax.ShapeDtypeStruct((1, feat), f32),
        ),
        in_specs=[smem] + [vmem] * 4,
        scratch_shapes=[pltpu.VMEM((2 * sz.half, min(128, sz.half // 2)), f32)],
        name="head",
    )(pair_labels, held, got, across(held), across(got))
    return (img_out[None], txt_out[None], img_grad, txt_grad)


def solution(mesh):
    both = ("dp", "expert")
    return jax.shard_map(
        per_device,
        mesh=mesh,
        in_specs=(
            P(both, None, None),
            P(both, None, None),
            P(both),
            P(both),
            P(both, None),
            P(both, None),
            P(both, None),
            P(both, None),
            P(both, None),
            P(both, None),
            P(both, None),
            P(both, None),
            P("expert", None, None),
            P("expert", None, None),
        ),
        out_specs=(
            P(both, None, None),
            P(both, None, None),
            P(both, None),
            P(both, None),
        ),
        check_vma=False,
    )
```

time: 492 us -> 159 us (0.32)
  blocking collectives: 310 us -> 0 us
  starting transfers between devices: 4.17 us -> 74.5 us
  waiting for transfers between devices: 118 us -> 57.9 us
  matrix products: 17.7 us -> 0 us
  between operations: 16.9 us -> 2.2 us
  Pallas kernels: 0 us -> 12.2 us
  local copies, waits for them, and re-layouts: 16.1 us -> 10.9 us
    psum x2 -> x0, blocking collectives: 148 us -> none  [the longest x1 113 us: per_device(): column_totals = lax.psum(jnp.sum(exp_scores, axis=0), 'dp')]
    unnamed x2 -> x0, waiting for transfers between devices: 108 us -> none
    unnamed x1 -> x0, blocking collectives: 71.4 us -> none
    all_gather x2 -> x0, blocking collectives: 55.8 us -> none  [the longest x1 41.2 us: per_device(): text_cols = lax.all_gather(text_emb, 'dp', axis=0, tiled=True)]
    ppermute x0 -> x12, starting transfers between devices: none -> 44.3 us  [swap(): return lax.ppermute(value, ('dp', 'expert'), pairs)]
    all_to_all x1 -> x0, blocking collectives: 34.9 us -> none  [per_device(): lax.all_to_all(packed, 'expert', split_axis=0, concat_axis=0, tiled=True)]
    ppermute x0 -> x12, waiting for transfers between devices: none -> 32.8 us  [swap(): return lax.ppermute(value, ('dp', 'expert'), pairs)]
    all_to_all x1 -> x2, starting transfers between devices: 4.13 us -> 30.2 us  [exchange(): lax.all_to_all(rows, 'expert', split_axis=0, concat_axis=0, tiled=True)]
  transfers between devices with their start and end apart: 2 -> 14, of which waited for: 2 -> 11; matrix products, arithmetic and copies ran while one was open for 1% -> 0% of each run, Pallas kernels for 0% -> 1%
where the time goes in v1:
time: 159 us; the launch traced here: 158 us
  starting transfers between devices  74.5 us (47%)
  waiting for transfers between devices  57.9 us (36%)
  Pallas kernels  12.2 us (8%)
  local copies, waits for them, and re-layouts  10.9 us (7%)
  between operations  2.2 us (1%)
    ppermute x12, starting transfers between devices, swap(): return lax.ppermute(value, ('dp', 'expert'), pairs)  44.3 us
    ppermute x12, waiting for transfers between devices, swap(): return lax.ppermute(value, ('dp', 'expert'), pairs)  32.8 us
    all_to_all x2, starting transfers between devices, exchange(): lax.all_to_all(rows, 'expert', split_axis=0, concat_axis=0, tiled=True)  30.2 us
    all_to_all x2, waiting for transfers between devices, exchange(): lax.all_to_all(rows, 'expert', split_axis=0, concat_axis=0, tiled=True)  25.1 us
    unnamed x44, local copies, waits for them, and re-layouts  10.9 us
    pallas_call x1, Pallas kernels, per_device(): call(bind(expert_kernel, sz, min(256, block)), (jax.ShapeDtypeStruct((sz....  6.32 us
  transfers between devices with their start and end apart: 14, of which 11 were waited for; matrix products, arithmetic and copies ran while one was open for 0% of the time, Pallas kernels for 1%

profile of v1, /device:TPU:1, one launch (start us, length us, event | category | flops | bytes accessed | tf_op | source)
XLA Modules:
  0.0 157.8 jit_solution(6597480187145738910)
XLA Ops:
  1.9 0.0 copy-start.2
  1.9 1.0 copy-done.2
  2.9 0.0 copy-start.4
  2.9 0.7 copy-done.4
  3.6 0.7 copy-done.6
  4.3 0.7 copy-done.8
  5.0 0.7 copy-done.10
  5.7 0.7 copy-done.12
  6.3 0.7 copy-done.14
  7.0 0.7 copy-done.16
  7.7 0.7 copy-done.18
  8.3 0.7 copy-done.20
  9.0 1.5 dispatch.1
  10.5 17.5 %all-to-all-start = ((bf16[16,24,640]{2,1,0:T(8,128)(2,1)}), bf16[16,24,640]{2,1,0:T(8,128)(2,1)S(1)}, u32[]{:S(2)}, u32[]{:S(2)}) async-start(bf16[16,24,640]{2,1,0:T(8,128)(2,1)} %bitcast.2), calls=%async_computation | async-start | bytes 983040 | tf_op jit(solution)/shard_map/all_to_all | solution.py:352
  28.0 16.7 %all-to-all-done = bf16[16,24,640]{2,1,0:T(8,128)(2,1)S(1)} async-done(((bf16[16,24,640]{2,1,0:T(8,128)(2,1)}), bf16[16,24,640]{2,1,0:T(8,128)(2,1)S(1)}, u32[]{:S(2)}, u32[]{:S(2)}) %all-to-all-start) | async-done | bytes 491552 | tf_op jit(solution)/shard_map/all_to_all | solution.py:352
  44.7 1.9 %copy-done = bf16[1,640,2560]{2,1,0:T(8,128)(2,1)S(1)} copy-done((bf16[1,640,2560]{2,1,0:T(8,128)(2,1)S(1)}, bf16[1,640,2560]{2,1,0:T(8,128)(2,1)}, u32[]{:S(2)}) %copy-start) | copy-done | bytes 3276824
  46.6 1.9 %copy-done.1 = bf16[1,2560,640]{2,1,0:T(8,128)(2,1)S(1)} copy-done((bf16[1,2560,640]{2,1,0:T(8,128)(2,1)S(1)}, bf16[1,2560,640]{2,1,0:T(8,128)(2,1)}, u32[]{:S(2)}) %copy-start.1) | copy-done | bytes 3276824
  48.5 6.3 %expert.1 = (bf16[384,640]{1,0:T(8,128)(2,1)}, f32[32,640]{1,0:T(8,128)S(1)}, bf16[8,640]{1,0:T(8,128)(2,1)S(1)}) custom-call(bf16[384,640]{1,0:T(8,128)(2,1)S(1)} %bitcast.13, bf16[640,2560]{1,0:T(8,128)(2,1)S(1)} %bitcast.10, bf16[2560,640]{1,0:T(8,128)(2,1)S(1)} %bitcast.11, f32[8,640]{1,0:T(8,128)S(1)} %get-tuple-element.16.refs_3_), custom_call_target="tpu_custom_call" | custom-call | tf_op jit(solution)/shard_map/expert/pallas_call | solution.py:358
  54.9 0.0 copy-start.11
  54.9 0.0 copy-start.13
  54.9 0.0 copy-start.15
  54.9 0.0 copy-start.17
  54.9 0.0 copy-start.19
  54.9 0.0 copy-start.21
  55.0 2.1 %collective-permute-start = (f32[16,640]{1,0:T(8,128)S(1)}, f32[16,640]{1,0:T(8,128)S(1)}, u32[]{:S(2)}, u32[]{:S(2)}) collective-permute-start(f32[16,640]{1,0:T(8,128)S(1)} %constant_dynamic-slice_fusion), channel_id=1, source_target_pairs={{0,1},{1,0},{2,3},{3,2},{4,5},{5,4},{6,7},{7,6},{8,9},{9,8},{10,11... | collective-permute-start | bytes 122888 | tf_op jit(solution)/shard_map/ppermute | solution.py:304
  57.0 1.2 collective-permute-done
  58.2 2.9 %collective-permute-start.1 = (f32[16,640]{1,0:T(8,128)S(1)}, f32[16,640]{1,0:T(8,128)S(1)}, u32[]{:S(2)}, u32[]{:S(2)}) collective-permute-start(f32[16,640]{1,0:T(8,128)S(1)} %dynamic-slice_add_fusion), channel_id=1, source_target_pairs={{0,8},{1,9},{2,10},{3,11},{4,12},{5,13},{6,14},{7,15},{8,0},{9,1},... | collective-permute-start | bytes 122888 | tf_op jit(solution)/shard_map/ppermute | solution.py:304
  61.1 7.2 %collective-permute-done.1 = f32[16,640]{1,0:T(8,128)S(1)} collective-permute-done((f32[16,640]{1,0:T(8,128)S(1)}, f32[16,640]{1,0:T(8,128)S(1)}, u32[]{:S(2)}, u32[]{:S(2)}) %collective-permute-start.1) | collective-permute-done | bytes 40992 | tf_op jit(solution)/shard_map/ppermute | solution.py:304
  68.3 1.9 %collective-permute-start.2 = (f32[16,640]{1,0:T(8,128)S(1)}, f32[16,640]{1,0:T(8,128)S(1)}, u32[]{:S(2)}, u32[]{:S(2)}) collective-permute-start(f32[16,640]{1,0:T(8,128)S(1)} %add.18), channel_id=1, source_target_pairs={{0,4},{1,5},{2,6},{3,7},{4,0},{5,1},{6,2},{7,3},{8,12},{9,13},{10,... | collective-permute-start | bytes 122888 | tf_op jit(solution)/shard_map/ppermute | solution.py:304
  70.2 3.7 %collective-permute-done.2 = f32[16,640]{1,0:T(8,128)S(1)} collective-permute-done((f32[16,640]{1,0:T(8,128)S(1)}, f32[16,640]{1,0:T(8,128)S(1)}, u32[]{:S(2)}, u32[]{:S(2)}) %collective-permute-start.2) | collective-permute-done | bytes 40992 | tf_op jit(solution)/shard_map/ppermute | solution.py:304
  73.9 1.9 %collective-permute-start.3 = (f32[16,640]{1,0:T(8,128)S(1)}, f32[16,640]{1,0:T(8,128)S(1)}, u32[]{:S(2)}, u32[]{:S(2)}) collective-permute-start(f32[16,640]{1,0:T(8,128)S(1)} %add.19.refs_0_), channel_id=1, source_target_pairs={{0,2},{1,3},{2,0},{3,1},{4,6},{5,7},{6,4},{7,5},{8,10},{9,11},{10,... | collective-permute-start | bytes 122888 | tf_op jit(solution)/shard_map/ppermute | solution.py:304
  75.9 2.8 %collective-permute-done.3.refs_1_ = f32[16,640]{1,0:T(8,128)S(1)} collective-permute-done((f32[16,640]{1,0:T(8,128)S(1)}, f32[16,640]{1,0:T(8,128)S(1)}, u32[]{:S(2)}, u32[]{:S(2)}) %collective-permute-start.3) | collective-permute-done | bytes 40992 | tf_op jit(solution)/shard_map/ppermute | solution.py:304
  78.7 0.1 normalize.1.refs_0_
  78.8 5.0 %collective-permute-start.4 = (bf16[24,640]{1,0:T(8,128)(2,1)S(1)}, bf16[24,640]{1,0:T(8,128)(2,1)S(1)}, u32[]{:S(2)}, u32[]{:S(2)}) collective-permute-start(bf16[24,640]{1,0:T(8,128)(2,1)S(1)} %normalize.1.refs_0_), channel_id=1, source_target_pairs={{0,512},{1,65},{2,514},{3,67},{4,516},{5,69},{6,518},{7,71},{8,520... | collective-permute-start | bytes 92168 | tf_op jit(solution)/shard_map/ppermute | solution.py:304
  83.8 3.5 %collective-permute-done.4.refs_1_ = bf16[24,640]{1,0:T(8,128)(2,1)S(1)} collective-permute-done((bf16[24,640]{1,0:T(8,128)(2,1)S(1)}, bf16[24,640]{1,0:T(8,128)(2,1)S(1)}, u32[]{:S(2)}, u32[]{:S(2)}) %collective-permute-start.4) | collective-permute-done | bytes 30752 | tf_op jit(solution)/shard_map/ppermute | solution.py:304
  87.3 3.6 %collective-permute-start.5 = (bf16[40,640]{1,0:T(8,128)(2,1)S(1)}, bf16[40,640]{1,0:T(8,128)(2,1)S(1)}, u32[]{:S(2)}, u32[]{:S(2)}) collective-permute-start(bf16[40,640]{1,0:T(8,128)(2,1)S(1)} %merge.5.refs_0_), channel_id=1, source_target_pairs={{0,256},{1,33},{2,258},{3,35},{4,260},{5,37},{6,262},{7,39},{8,264... | collective-permute-start | bytes 153608 | tf_op jit(solution)/shard_map/ppermute | solution.py:304
  90.9 2.2 %collective-permute-done.5.refs_1_ = bf16[40,640]{1,0:T(8,128)(2,1)S(1)} collective-permute-done((bf16[40,640]{1,0:T(8,128)(2,1)S(1)}, bf16[40,640]{1,0:T(8,128)(2,1)S(1)}, u32[]{:S(2)}, u32[]{:S(2)}) %collective-permute-start.5) | collective-permute-done | bytes 51232 | tf_op jit(solution)/shard_map/ppermute | solution.py:304
  93.1 3.3 %collective-permute-start.6 = (bf16[72,640]{1,0:T(8,128)(2,1)S(1)}, bf16[72,640]{1,0:T(8,128)(2,1)S(1)}, u32[]{:S(2)}, u32[]{:S(2)}) collective-permute-start(bf16[72,640]{1,0:T(8,128)(2,1)S(1)} %merge.6.refs_0_), channel_id=1, source_target_pairs={{0,128},{1,17},{2,130},{3,19},{4,132},{5,21},{6,134},{7,23},{8,136... | collective-permute-start | bytes 276488 | tf_op jit(solution)/shard_map/ppermute | solution.py:304
  96.4 2.0 %collective-permute-done.6.refs_1_ = bf16[72,640]{1,0:T(8,128)(2,1)S(1)} collective-permute-done((bf16[72,640]{1,0:T(8,128)(2,1)S(1)}, bf16[72,640]{1,0:T(8,128)(2,1)S(1)}, u32[]{:S(2)}, u32[]{:S(2)}) %collective-permute-start.6) | collective-permute-done | bytes 92192 | tf_op jit(solution)/shard_map/ppermute | solution.py:304
  98.4 7.9 %collective-permute-start.7 = (bf16[136,640]{1,0:T(8,128)(2,1)S(1)}, bf16[136,640]{1,0:T(8,128)(2,1)S(1)}, u32[]{:S(2)}, u32[]{:S(2)}) collective-permute-start(bf16[136,640]{1,0:T(8,128)(2,1)S(1)} %merge.7.refs_0_), channel_id=1, source_target_pairs={{0,64},{1,513},{2,66},{3,515},{4,68},{5,517},{6,70},{7,519},{8,72}... | collective-permute-start | bytes 522248 | tf_op jit(solution)/shard_map/ppermute | solution.py:304
  106.3 2.9 %collective-permute-done.7.refs_1_ = bf16[136,640]{1,0:T(8,128)(2,1)S(1)} collective-permute-done((bf16[136,640]{1,0:T(8,128)(2,1)S(1)}, bf16[136,640]{1,0:T(8,128)(2,1)S(1)}, u32[]{:S(2)}, u32[]{:S(2)}) %collective-permute-start.7) | collective-permute-done | bytes 174112 | tf_op jit(solution)/shard_map/ppermute | solution.py:304
  109.2 5.7 %collective-permute-start.8 = (bf16[264,640]{1,0:T(8,128)(2,1)S(1)}, bf16[264,640]{1,0:T(8,128)(2,1)S(1)}, u32[]{:S(2)}, u32[]{:S(2)}) collective-permute-start(bf16[264,640]{1,0:T(8,128)(2,1)S(1)} %merge.8.refs_0_), channel_id=1, source_target_pairs={{0,32},{1,257},{2,34},{3,259},{4,36},{5,261},{6,38},{7,263},{8,40}... | collective-permute-start | bytes 1013768 | tf_op jit(solution)/shard_map/ppermute | solution.py:304
  114.9 7.3 %collective-permute-done.8.refs_1_ = bf16[264,640]{1,0:T(8,128)(2,1)S(1)} collective-permute-done((bf16[264,640]{1,0:T(8,128)(2,1)S(1)}, bf16[264,640]{1,0:T(8,128)(2,1)S(1)}, u32[]{:S(2)}, u32[]{:S(2)}) %collective-permute-start.8) | collective-permute-done | bytes 337952 | tf_op jit(solution)/shard_map/ppermute | solution.py:304
  122.3 0.1 merge.9.refs_1_
  122.3 1.9 %collective-permute-start.9 = (bf16[520,640]{1,0:T(8,128)(2,1)S(1)}, bf16[520,640]{1,0:T(8,128)(2,1)S(1)}, u32[]{:S(2)}, u32[]{:S(2)}) collective-permute-start(bf16[520,640]{1,0:T(8,128)(2,1)S(1)} %merge.9.refs_1_), channel_id=1, source_target_pairs={{0,16},{1,129},{2,18},{3,131},{4,20},{5,133},{6,22},{7,135},{8,24}... | collective-permute-start | bytes 1996808 | tf_op jit(solution)/shard_map/ppermute | solution.py:304
  124.3 12.7 %all-to-all-start.1 = ((bf16[16,24,640]{2,1,0:T(8,128)(2,1)}), bf16[16,24,640]{2,1,0:T(8,128)(2,1)S(1)}, u32[]{:S(2)}, u32[]{:S(2)}) async-start(bf16[16,24,640]{2,1,0:T(8,128)(2,1)} %bitcast.6), calls=%async_computation.1 | async-start | bytes 983040 | tf_op jit(solution)/shard_map/all_to_all | solution.py:352
  136.9 2.1 %collective-permute-start.10 = (bf16[520,640]{1,0:T(8,128)(2,1)S(1)}, bf16[520,640]{1,0:T(8,128)(2,1)S(1)}, u32[]{:S(2)}, u32[]{:S(2)}) collective-permute-start(bf16[520,640]{1,0:T(8,128)(2,1)S(1)} %merge.9.refs_1_), channel_id=1, source_target_pairs={{0,1},{1,0},{2,3},{3,2},{4,5},{5,4},{6,7},{7,6},{8,9},{9,8},{10,11... | collective-permute-start | bytes 1996808 | tf_op jit(solution)/shard_map/ppermute | solution.py:304
  139.0 0.0 collective-permute-done.9.refs_2_
  139.1 6.1 %collective-permute-start.11 = (bf16[520,640]{1,0:T(8,128)(2,1)S(1)}, bf16[520,640]{1,0:T(8,128)(2,1)S(1)}, u32[]{:S(2)}, u32[]{:S(2)}) collective-permute-start(bf16[520,640]{1,0:T(8,128)(2,1)S(1)} %collective-permute-done.9.refs_2_), channel_id=1, source_target_pairs={{0,1},{1,0},{2,3},{3,2},{4,5},{5,4},{6,7},{7,6},{8,9},{9,8},{10,11... | collective-permute-start | bytes 1996808 | tf_op jit(solution)/shard_map/ppermute | solution.py:304
  145.1 8.5 %all-to-all-done.1 = bf16[16,24,640]{2,1,0:T(8,128)(2,1)S(1)} async-done(((bf16[16,24,640]{2,1,0:T(8,128)(2,1)}), bf16[16,24,640]{2,1,0:T(8,128)(2,1)S(1)}, u32[]{:S(2)}, u32[]{:S(2)}) %all-to-all-start.1) | async-done | bytes 491552 | tf_op jit(solution)/shard_map/all_to_all | solution.py:352
  153.6 0.0 copy-done.3
  153.6 0.0 copy-done.5
  153.6 0.0 copy-done.7
  153.6 0.0 copy-done.9
  153.6 0.0 copy-done.11
  153.6 0.0 copy-done.13
  153.6 0.0 copy-done.15
  153.6 0.0 copy-done.17
  153.6 0.0 copy-done.19
  153.6 0.0 copy-done.21
  153.7 1.1 combine.1
  154.8 0.0 collective-permute-done.10.refs_3_
  154.8 0.0 collective-permute-done.11.refs_4_
  154.8 3.0 %head.1 = (f32[1,640]{1,0:T(1,128)}, f32[1,640]{1,0:T(1,128)}) custom-call(s32[1]{0:T(128)S(6)} %copy.19.refs_1_.refs_0_, bf16[520,640]{1,0:T(8,128)(2,1)S(1)} %merge.9.refs_1_, bf16[520,640]{1,0:T(8,128)(2,1)S(1)} %collective-permute-done.9.refs_2_, bf16[520,640]{1,0:T(8,128)(2,1)S(1)} %collective-permute-done.10.refs_3_, ...), custom_call_target="tpu_custom_call" | custom-call | tf_op jit(solution)/shard_map/head/pallas_call | solution.py:427
  (22 shorter events, 0.1 us)
Async XLA Ops:
  1.9 1.0 copy-start.2
  2.9 0.7 copy-start.4
  3.6 0.7 copy-start.6
  4.3 0.7 copy-start.8
  5.0 0.7 copy-start.10
  5.7 0.7 copy-start.12
  6.3 0.7 copy-start.14
  7.0 0.7 copy-start.16
  7.7 0.7 copy-start.18
  8.3 0.7 copy-start.20
  10.5 34.2 %all-to-all-start = ((bf16[16,24,640]{2,1,0:T(8,128)(2,1)}), bf16[16,24,640]{2,1,0:T(8,128)(2,1)S(1)}, u32[]{:S(2)}, u32[]{:S(2)}) async-start(bf16[16,24,640]{2,1,0:T(8,128)(2,1)} %bitcast.2), calls=%async_computation | async-start | bytes 983040 | tf_op jit(solution)/shard_map/all_to_all | solution.py:352
  44.7 1.9 %copy-start = (bf16[1,640,2560]{2,1,0:T(8,128)(2,1)S(1)}, bf16[1,640,2560]{2,1,0:T(8,128)(2,1)}, u32[]{:S(2)}) copy-start(bf16[1,640,2560]{2,1,0:T(8,128)(2,1)} %param.26) | copy-start | bytes 9830404
  46.6 1.9 %copy-start.1 = (bf16[1,2560,640]{2,1,0:T(8,128)(2,1)S(1)}, bf16[1,2560,640]{2,1,0:T(8,128)(2,1)}, u32[]{:S(2)}) copy-start(bf16[1,2560,640]{2,1,0:T(8,128)(2,1)} %param.27) | copy-start | bytes 9830404
  54.8 98.7 %copy-start.3 = (bf16[1,256,640]{2,1,0:T(8,128)(2,1)S(1)}, bf16[1,256,640]{2,1,0:T(8,128)(2,1)}, u32[]{:S(2)}) copy-start(bf16[1,256,640]{2,1,0:T(8,128)(2,1)} %param.14) | copy-start | bytes 983044
  54.8 98.7 %copy-start.5 = (bf16[1,16,640]{2,1,0:T(8,128)(2,1)S(1)}, bf16[1,16,640]{2,1,0:T(8,128)(2,1)}, u32[]{:S(2)}) copy-start(bf16[1,16,640]{2,1,0:T(8,128)(2,1)} %param.15) | copy-start | bytes 61444
  54.9 98.7 %copy-start.7 = (s32[1,256]{1,0:T(1,128)S(1)}, s32[1,256]{1,0:T(1,128)}, u32[]{:S(2)}) copy-start(s32[1,256]{1,0:T(1,128)} %refs_0_.3) | copy-start | bytes 3076
  54.9 98.7 %copy-start.9 = (s32[1,256]{1,0:T(1,128)S(1)}, s32[1,256]{1,0:T(1,128)}, u32[]{:S(2)}) copy-start(s32[1,256]{1,0:T(1,128)} %refs_1_.2) | copy-start | bytes 3076
  54.9 98.7 %copy-start.11 = (s32[1,256]{1,0:T(1,128)S(1)}, s32[1,256]{1,0:T(1,128)}, u32[]{:S(2)}) copy-start(s32[1,256]{1,0:T(1,128)} %refs_2_.3) | copy-start | bytes 3076
  54.9 98.7 %copy-start.13 = (f32[1,256]{1,0:T(1,128)S(1)}, f32[1,256]{1,0:T(1,128)}, u32[]{:S(2)}) copy-start(f32[1,256]{1,0:T(1,128)} %refs_6_.3) | copy-start | bytes 3076
  54.9 98.7 %copy-start.15 = (s32[1,16]{1,0:T(1,128)S(1)}, s32[1,16]{1,0:T(1,128)}, u32[]{:S(2)}) copy-start(s32[1,16]{1,0:T(1,128)} %refs_3_.3) | copy-start | bytes 196
  54.9 98.7 %copy-start.17 = (s32[1,16]{1,0:T(1,128)S(1)}, s32[1,16]{1,0:T(1,128)}, u32[]{:S(2)}) copy-start(s32[1,16]{1,0:T(1,128)} %refs_4_.3) | copy-start | bytes 196
  54.9 98.7 %copy-start.19 = (s32[1,16]{1,0:T(1,128)S(1)}, s32[1,16]{1,0:T(1,128)}, u32[]{:S(2)}) copy-start(s32[1,16]{1,0:T(1,128)} %refs_5_.3) | copy-start | bytes 196
  54.9 98.7 %copy-start.21 = (f32[1,16]{1,0:T(1,128)S(1)}, f32[1,16]{1,0:T(1,128)}, u32[]{:S(2)}) copy-start(f32[1,16]{1,0:T(1,128)} %refs_7_.3) | copy-start | bytes 196
  55.0 3.2 %collective-permute-start = (f32[16,640]{1,0:T(8,128)S(1)}, f32[16,640]{1,0:T(8,128)S(1)}, u32[]{:S(2)}, u32[]{:S(2)}) collective-permute-start(f32[16,640]{1,0:T(8,128)S(1)} %constant_dynamic-slice_fusion), channel_id=1, source_target_pairs={{0,1},{1,0},{2,3},{3,2},{4,5},{5,4},{6,7},{7,6},{8,9},{9,8},{10,11... | collective-permute-start | bytes 122888 | tf_op jit(solution)/shard_map/ppermute | solution.py:304
  58.2 10.1 %collective-permute-start.1 = (f32[16,640]{1,0:T(8,128)S(1)}, f32[16,640]{1,0:T(8,128)S(1)}, u32[]{:S(2)}, u32[]{:S(2)}) collective-permute-start(f32[16,640]{1,0:T(8,128)S(1)} %dynamic-slice_add_fusion), channel_id=1, source_target_pairs={{0,8},{1,9},{2,10},{3,11},{4,12},{5,13},{6,14},{7,15},{8,0},{9,1},... | collective-permute-start | bytes 122888 | tf_op jit(solution)/shard_map/ppermute | solution.py:304
  68.3 5.6 %collective-permute-start.2 = (f32[16,640]{1,0:T(8,128)S(1)}, f32[16,640]{1,0:T(8,128)S(1)}, u32[]{:S(2)}, u32[]{:S(2)}) collective-permute-start(f32[16,640]{1,0:T(8,128)S(1)} %add.18), channel_id=1, source_target_pairs={{0,4},{1,5},{2,6},{3,7},{4,0},{5,1},{6,2},{7,3},{8,12},{9,13},{10,... | collective-permute-start | bytes 122888 | tf_op jit(solution)/shard_map/ppermute | solution.py:304
  73.9 4.7 %collective-permute-start.3 = (f32[16,640]{1,0:T(8,128)S(1)}, f32[16,640]{1,0:T(8,128)S(1)}, u32[]{:S(2)}, u32[]{:S(2)}) collective-permute-start(f32[16,640]{1,0:T(8,128)S(1)} %add.19.refs_0_), channel_id=1, source_target_pairs={{0,2},{1,3},{2,0},{3,1},{4,6},{5,7},{6,4},{7,5},{8,10},{9,11},{10,... | collective-permute-start | bytes 122888 | tf_op jit(solution)/shard_map/ppermute | solution.py:304
  78.8 8.5 %collective-permute-start.4 = (bf16[24,640]{1,0:T(8,128)(2,1)S(1)}, bf16[24,640]{1,0:T(8,128)(2,1)S(1)}, u32[]{:S(2)}, u32[]{:S(2)}) collective-permute-start(bf16[24,640]{1,0:T(8,128)(2,1)S(1)} %normalize.1.refs_0_), channel_id=1, source_target_pairs={{0,512},{1,65},{2,514},{3,67},{4,516},{5,69},{6,518},{7,71},{8,520... | collective-permute-start | bytes 92168 | tf_op jit(solution)/shard_map/ppermute | solution.py:304
  87.3 5.8 %collective-permute-start.5 = (bf16[40,640]{1,0:T(8,128)(2,1)S(1)}, bf16[40,640]{1,0:T(8,128)(2,1)S(1)}, u32[]{:S(2)}, u32[]{:S(2)}) collective-permute-start(bf16[40,640]{1,0:T(8,128)(2,1)S(1)} %merge.5.refs_0_), channel_id=1, source_target_pairs={{0,256},{1,33},{2,258},{3,35},{4,260},{5,37},{6,262},{7,39},{8,264... | collective-permute-start | bytes 153608 | tf_op jit(solution)/shard_map/ppermute | solution.py:304
  93.1 5.3 %collective-permute-start.6 = (bf16[72,640]{1,0:T(8,128)(2,1)S(1)}, bf16[72,640]{1,0:T(8,128)(2,1)S(1)}, u32[]{:S(2)}, u32[]{:S(2)}) collective-permute-start(bf16[72,640]{1,0:T(8,128)(2,1)S(1)} %merge.6.refs_0_), channel_id=1, source_target_pairs={{0,128},{1,17},{2,130},{3,19},{4,132},{5,21},{6,134},{7,23},{8,136... | collective-permute-start | bytes 276488 | tf_op jit(solution)/shard_map/ppermute | solution.py:304
  98.4 10.8 %collective-permute-start.7 = (bf16[136,640]{1,0:T(8,128)(2,1)S(1)}, bf16[136,640]{1,0:T(8,128)(2,1)S(1)}, u32[]{:S(2)}, u32[]{:S(2)}) collective-permute-start(bf16[136,640]{1,0:T(8,128)(2,1)S(1)} %merge.7.refs_0_), channel_id=1, source_target_pairs={{0,64},{1,513},{2,66},{3,515},{4,68},{5,517},{6,70},{7,519},{8,72}... | collective-permute-start | bytes 522248 | tf_op jit(solution)/shard_map/ppermute | solution.py:304
  109.2 13.0 %collective-permute-start.8 = (bf16[264,640]{1,0:T(8,128)(2,1)S(1)}, bf16[264,640]{1,0:T(8,128)(2,1)S(1)}, u32[]{:S(2)}, u32[]{:S(2)}) collective-permute-start(bf16[264,640]{1,0:T(8,128)(2,1)S(1)} %merge.8.refs_0_), channel_id=1, source_target_pairs={{0,32},{1,257},{2,34},{3,259},{4,36},{5,261},{6,38},{7,263},{8,40}... | collective-permute-start | bytes 1013768 | tf_op jit(solution)/shard_map/ppermute | solution.py:304
  122.3 16.7 %collective-permute-start.9 = (bf16[520,640]{1,0:T(8,128)(2,1)S(1)}, bf16[520,640]{1,0:T(8,128)(2,1)S(1)}, u32[]{:S(2)}, u32[]{:S(2)}) collective-permute-start(bf16[520,640]{1,0:T(8,128)(2,1)S(1)} %merge.9.refs_1_), channel_id=1, source_target_pairs={{0,16},{1,129},{2,18},{3,131},{4,20},{5,133},{6,22},{7,135},{8,24}... | collective-permute-start | bytes 1996808 | tf_op jit(solution)/shard_map/ppermute | solution.py:304
  124.3 29.3 %all-to-all-start.1 = ((bf16[16,24,640]{2,1,0:T(8,128)(2,1)}), bf16[16,24,640]{2,1,0:T(8,128)(2,1)S(1)}, u32[]{:S(2)}, u32[]{:S(2)}) async-start(bf16[16,24,640]{2,1,0:T(8,128)(2,1)} %bitcast.6), calls=%async_computation.1 | async-start | bytes 983040 | tf_op jit(solution)/shard_map/all_to_all | solution.py:352
  136.9 17.9 %collective-permute-start.10 = (bf16[520,640]{1,0:T(8,128)(2,1)S(1)}, bf16[520,640]{1,0:T(8,128)(2,1)S(1)}, u32[]{:S(2)}, u32[]{:S(2)}) collective-permute-start(bf16[520,640]{1,0:T(8,128)(2,1)S(1)} %merge.9.refs_1_), channel_id=1, source_target_pairs={{0,1},{1,0},{2,3},{3,2},{4,5},{5,4},{6,7},{7,6},{8,9},{9,8},{10,11... | collective-permute-start | bytes 1996808 | tf_op jit(solution)/shard_map/ppermute | solution.py:304
  139.1 15.7 %collective-permute-start.11 = (bf16[520,640]{1,0:T(8,128)(2,1)S(1)}, bf16[520,640]{1,0:T(8,128)(2,1)S(1)}, u32[]{:S(2)}, u32[]{:S(2)}) collective-permute-start(bf16[520,640]{1,0:T(8,128)(2,1)S(1)} %collective-permute-done.9.refs_2_), channel_id=1, source_target_pairs={{0,1},{1,0},{2,3},{3,2},{4,5},{5,4},{6,7},{7,6},{8,9},{9,8},{10,11... | collective-permute-start | bytes 1996808 | tf_op jit(solution)/shard_map/ppermute | solution.py:304

commit v2 on v1

v2 whole, which is shorter than its diff:
```python
import jax
import jax.numpy as jnp
import numpy as np
from jax import lax
from jax.experimental import pallas as pl
from jax.experimental.pallas import tpu as pltpu
from jax.sharding import PartitionSpec as P

logit_scale = 10.0
f32, bf16, i32 = jnp.float32, jnp.bfloat16, jnp.int32
NT = (((1,), (1,)), ((), ()))
TN = (((0,), (0,)), ((), ()))
NN = (((1,), (0,)), ((), ()))


def dot(left, right, dims=NN):
    return lax.dot_general(left, right, dims, preferred_element_type=f32)


def divided(value, by, limit):
    magic = -(-65536 // by)
    assert all((v * magic) >> 16 == v // by for v in range(limit))
    return (value * magic) >> 16


def iota(shape, dim):
    return lax.broadcasted_iota(i32, shape, dim)


def one_hot(mask):
    return jnp.where(mask, 1.0, 0.0).astype(bf16)


def three_parts(value):
    high = value.astype(bf16)
    rest = value - high.astype(f32)
    middle = rest.astype(bf16)
    low = (rest - middle.astype(f32)).astype(bf16)
    return high, middle, low


class Sizes:
    def __init__(self, owners, lines, img_tok, txt_tok, feat):
        self.owners, self.lines = owners, lines
        self.cores = 2
        self.nx = owners // self.cores
        self.ny = 1 << ((lines.bit_length() - 1 + 1) // 2)
        self.nz = lines // self.ny
        self.img_tok, self.txt_tok, self.feat = img_tok, txt_tok, feat
        self.cap = 5 * img_tok // (4 * owners)
        self.slots = self.cap + 2
        self.stride = -(-(self.slots + 2) // 8) * 8
        self.rows = owners * self.stride
        self.back = self.stride + 2 * self.nx
        self.half = self.nx * lines
        self.pairs = owners * lines


def slot_masks(sz, stride, img_expert, img_rank, img_keep, txt_expert, txt_rank, txt_keep):
    img_target = img_expert * stride + img_rank
    txt_target = txt_expert * stride + sz.cap + txt_rank
    img_target = jnp.where(img_keep == 1, img_target, -1)
    txt_target = jnp.where(txt_keep == 1, txt_target, -1)
    return (
        one_hot(iota((sz.owners * stride, sz.img_tok), 0) == img_target),
        one_hot(iota((sz.owners * stride, sz.txt_tok), 0) == txt_target),
    )


def dispatch_kernel(sz, count_ref, label_ref, ie, ir, ik, te, tr, tk, ig, tg, img, txt, packed, means):
    img_mask, txt_mask = slot_masks(sz, sz.stride, ie[...], ir[...], ik[...], te[...], tr[...], tk[...])
    count = count_ref[0]
    count_f = jnp.full((1, 1), count, i32).astype(f32)
    label = label_ref[0]
    img_weight = jnp.where(ik[...] == 1, ig[...], 0.0) * (1.0 / sz.img_tok)
    valid = iota((1, sz.txt_tok), 1) < count
    txt_weight = jnp.where((tk[...] == 1) & valid, tg[...], 0.0) / count_f
    img_place = one_hot(iota((128, sz.img_tok), 0) == ir[...])
    txt_place = one_hot(iota((128, sz.txt_tok), 0) == tr[...] + sz.cap)
    img_at = iota((sz.owners, sz.img_tok), 0) == ie[...]
    txt_at = iota((sz.owners, sz.txt_tok), 0) == te[...]
    tables = []
    for img_part, txt_part in zip(three_parts(img_weight), three_parts(txt_weight)):
        img_side = jnp.where(img_at, img_part.astype(f32), 0.0).astype(bf16)
        txt_side = jnp.where(txt_at, txt_part.astype(f32), 0.0).astype(bf16)
        tables.append(dot(img_side, img_place, NT) + dot(txt_side, txt_place, NT))
    pad = sz.feat - 3 * 128
    if pad:
        tables.append(jnp.zeros((sz.owners, pad), f32))
    weights = jnp.concatenate(tables, 1).astype(bf16)
    lane = iota((sz.owners, sz.feat), 1)
    label_row = jnp.where(
        lane < 128,
        (label >> 5).astype(f32),
        jnp.where(lane < 256, (label & 31).astype(f32), 0.0),
    ).astype(bf16)
    row = iota((sz.rows, sz.owners), 0)
    block = iota((sz.rows, sz.owners), 1) * sz.stride
    out = dot(img_mask, img[...]) + dot(txt_mask, txt[...])
    out = out + dot(one_hot(row == block + sz.slots), weights)
    out = out + dot(one_hot(row == block + sz.slots + 1), label_row)
    packed[...] = out.astype(bf16)
    img_mean = dot(jnp.ones((8, sz.img_tok), bf16), img[...]) * (1.0 / sz.img_tok)
    counted = one_hot(iota((8, sz.txt_tok), 1) < count)
    txt_mean = dot(counted, txt[...]) / count_f
    means[...] = jnp.where(iota((8, sz.feat), 0) == 0, img_mean, txt_mean)


def gelu(x):
    return 0.5 * x * (1.0 + lax.erf(x * np.float32(np.sqrt(0.5))))


def expert_kernel(sz, chunk, x_ref, w_in, w_out, means, back_ref, label_ref, total):
    step = pl.program_id(0)

    @pl.when(step == 0)
    def _():
        total[...] = jnp.zeros_like(total)

    x = x_ref[...]
    width = w_in.shape[1]
    part = None
    for at in range(0, width, chunk):
        hidden = gelu(dot(x, w_in[:, at : at + chunk])).astype(bf16)
        term = dot(hidden, w_out[at : at + chunk, :])
        part = term if part is None else part + term
    total[...] += part

    @pl.when(step == pl.num_programs(0) - 1)
    def _():
        out = total[...].astype(bf16)
        count = 2 * sz.owners
        r = iota((count, sz.rows), 0)
        c = iota((count, sz.rows), 1)
        block = divided(c, sz.stride, sz.rows)
        place = c - block * sz.stride
        is_txt = (r & sz.nx) > 0
        source = (r & (sz.nx - 1)) * sz.cores + jnp.where(r >= 2 * sz.nx, 1, 0)
        held = dot(one_hot(c == source * sz.stride + sz.slots), x)
        lane = iota((128, sz.rows), 1)
        lane_place = lane - divided(lane, sz.stride, sz.rows) * sz.stride
        spread = one_hot(iota((128, sz.rows), 0) == lane_place)
        own = (block == source) & (
            jnp.where(is_txt, 1, 0) == jnp.where(place >= sz.cap, 1, 0)
        ) & (place < sz.slots)
        pool = jnp.zeros((count, sz.feat), f32)
        for part_at in range(3):
            piece = held[:, part_at * 128 : (part_at + 1) * 128].astype(bf16)
            weight = jnp.where(own, dot(piece, spread), 0.0).astype(bf16)
            pool = pool + dot(weight, out)
        me = lax.axis_index("expert")
        line = lax.axis_index("dp")
        my_x, my_core = me >> 1, me & 1
        row = iota((count, sz.feat), 0)
        my_row = my_core * (2 * sz.nx) + my_x
        pool = pool + jnp.where(row == my_row, means[0:1, :], 0.0)
        pool = pool + jnp.where(row == my_row + sz.nx, means[1:2, :], 0.0)
        lost = pool - pool.astype(bf16).astype(f32)
        img_lost = jnp.sum(jnp.where(row == my_row, lost, 0.0), axis=0, keepdims=True)
        txt_lost = jnp.sum(jnp.where(row == my_row + sz.nx, lost, 0.0), axis=0, keepdims=True)
        spare = iota((sz.stride, sz.feat), 0)
        blocks = []
        for e in range(sz.owners):
            kept = total[e * sz.stride : (e + 1) * sz.stride, :]
            kept = jnp.where(spare == sz.slots, img_lost, kept)
            blocks.append(jnp.where(spare == sz.slots + 1, txt_lost, kept))
            half = (e % sz.cores) * 2 * sz.nx
            blocks.append(pool[half : half + 2 * sz.nx, :])
        back_ref[...] = jnp.concatenate(blocks, 0).astype(bf16)
        r8 = iota((sz.nx, sz.rows), 0)
        c8 = iota((sz.nx, sz.rows), 1)
        labels = dot(one_hot(c8 == (r8 * sz.cores + my_core) * sz.stride + sz.slots + 1), x)
        lane = iota((sz.nx, sz.feat), 1)
        label_ref[...] = jnp.where((lane == line) | (lane == line + 128), labels, 0.0).astype(bf16)


def normalize_kernel(sz, back, label, out, copies):
    my_core = lax.axis_index("expert") & 1
    shape = (2 * sz.nx, sz.owners * sz.back)
    r, c = iota(shape, 0), iota(shape, 1)
    owner = divided(c, sz.back, shape[1])
    place = c - owner * sz.back
    spare = jnp.where(r >= sz.nx, sz.slots + 1, sz.slots)
    left = (place == spare) & (owner == (r & (sz.nx - 1)) * sz.cores + my_core)
    pooled = dot(one_hot((place == sz.stride + r) | left), back[...])
    norm = jnp.sqrt(jnp.sum(pooled * pooled, axis=1, keepdims=True) + 1e-06)
    block = jnp.concatenate([(pooled / norm).astype(bf16), label[...]], 0)
    out[...] = block
    for at in range(0, copies.shape[0], block.shape[0]):
        copies[at : at + block.shape[0], :] = block


def combine_kernel(sz, ie, ir, ik, te, tr, tk, ig, tg, img, txt, returned, img_out, txt_out):
    img_mask, txt_mask = slot_masks(sz, sz.back, ie[...], ir[...], ik[...], te[...], tr[...], tk[...])
    back = returned[...]
    for mask, gate, tokens, out in ((img_mask, ig, img, img_out), (txt_mask, tg, txt, txt_out)):
        count = tokens.shape[0]
        picked = dot(mask, back, TN)
        column = jnp.transpose(jnp.broadcast_to(gate[...], (128, count)))[:, 0:1]
        out[...] = (tokens[...].astype(f32) + column * picked).astype(bf16)


def merge_kernel(sz, got, copies):
    size = 3 * sz.nx
    count = got.shape[0] // size
    pieces = [got[b * size : b * size + sz.nx, :] for b in range(count)]
    pieces += [got[b * size + sz.nx : b * size + 2 * sz.nx, :] for b in range(count)]
    labels = jnp.zeros((sz.nx, sz.feat), f32)
    for b in range(count):
        labels = labels + got[b * size + 2 * sz.nx : (b + 1) * size, :].astype(f32)
    block = jnp.concatenate(pieces + [labels.astype(bf16)], 0)
    for at in range(0, copies.shape[0], block.shape[0]):
        copies[at : at + block.shape[0], :] = block


def head_kernel(sz, label_ref, own, mine, theirs, img_grad, txt_grad, images, texts):
    half = sz.half
    me = lax.axis_index("expert")
    line = lax.axis_index("dp")
    my_x, my_core = me >> 1, me & 1
    z_bits = sz.nz.bit_length() - 1
    pair = line * sz.owners + me

    def position(line, x, core):
        y, z = line >> z_bits, line & (sz.nz - 1)
        block = jnp.where(core == 0, z * sz.ny + y, y * sz.nz + z)
        return jnp.where(core == my_core, 0, half) + block * sz.nx + x

    blocks = sz.nz
    each = half // blocks
    size = 2 * each + sz.nx
    names = []
    for a, got in enumerate((mine, theirs)):
        table = jnp.zeros((sz.nx, 256), f32)
        for b in range(blocks):
            at, to = b * size, a * half + b * each
            images[to : to + each, :] = got[at : at + each, :]
            texts[to : to + each, :] = got[at + each : at + 2 * each, :]
            table = table + got[at + 2 * each : at + size, 0:256].astype(f32)
        names.append(table)

    total = 2 * half
    row_scores = jnp.exp(logit_scale * dot(own[: sz.nx, :], texts[...], NT))
    column_scores = jnp.exp(logit_scale * dot(images[...], own[sz.nx : 2 * sz.nx, :], NT))
    tile = min(256, total)
    column_totals = jnp.zeros((1, total), f32)
    row_totals = []
    for at in range(0, total, tile):
        scores = jnp.exp(logit_scale * dot(images[at : at + tile, :], texts[...], NT))
        row_totals.append(jnp.sum(scores, axis=1, keepdims=True))
        column_totals = column_totals + jnp.sum(scores, axis=0, keepdims=True)

    label = label_ref[0]
    owner = label & (sz.owners - 1)
    target = position(label >> (sz.owners.bit_length() - 1), owner >> 1, owner & 1)
    match = jnp.where(iota((sz.nx, total), 1) == target, 2.0, 0.0)
    own_rows = jnp.sum(row_scores, axis=1, keepdims=True)
    scores = row_scores / own_rows + row_scores / column_totals - match
    grad = dot(scores.astype(bf16), texts[...])
    chosen = iota((sz.nx, sz.feat), 0) == my_x
    img_grad[...] = jnp.sum(jnp.where(chosen, grad, 0.0), axis=0, keepdims=True)

    lane = iota((sz.nx, 128), 1)
    sub = iota((sz.nx, 128), 0)
    high, low = (pair >> 5).astype(f32), (pair & 31).astype(f32)
    found = []
    for table in names:
        hit = (table[:, :128] == high) & (table[:, 128:] == low) & (lane < sz.lines)

        def summed(value):
            value = jnp.where(hit, value, 0.0)
            return jnp.sum(jnp.sum(value, axis=0, keepdims=True), axis=1, keepdims=True)

        found.append([summed(v) for v in (lane.astype(f32), sub.astype(f32), jnp.ones((sz.nx, 128), f32))])
    found_line = (found[0][0] + found[1][0]).astype(i32)
    found_x = (found[0][1] + found[1][1]).astype(i32)
    found_core = jnp.where(found[1][2] > 0.5, 1 - my_core, my_core)
    named = position(found_line, found_x, found_core)
    own_columns = jnp.sum(column_scores, axis=0, keepdims=True)
    grad = jnp.zeros((sz.nx, sz.feat), f32)
    for t, at in enumerate(range(0, total, tile)):
        rows = column_scores[at : at + tile, :]
        match = jnp.where(iota((tile, sz.nx), 0) + at == named, 2.0, 0.0)
        scores = rows / row_totals[t] + rows / own_columns - match
        grad = grad + dot(scores.astype(bf16), images[at : at + tile, :], TN)
    txt_grad[...] = jnp.sum(jnp.where(chosen, grad, 0.0), axis=0, keepdims=True)


def call(kernel, out_shape, in_specs=None, cost=None, limit=24, **kw):
    if cost is not None:
        kw["cost_estimate"] = pl.CostEstimate(flops=cost[0], bytes_accessed=cost[1], transcendentals=cost[2])
    if in_specs is not None:
        kw["in_specs"] = in_specs
    return pl.pallas_call(
        kernel,
        out_shape=out_shape,
        compiler_params=pltpu.CompilerParams(vmem_limit_bytes=limit << 20),
        **kw,
    )


def bind(kernel, *head):
    def bound(*refs):
        return kernel(*head, *refs)

    return bound


def rank_of(sz, y, z, x, core):
    return ((y * sz.nz + z) * sz.nx + x) * sz.cores + core


def split_groups(sz, first):
    groups = []
    for core in range(sz.cores):
        along_y = (core == 0) == first
        for fixed in range(sz.nz if along_y else sz.ny):
            for x in range(sz.nx):
                if along_y:
                    groups.append([rank_of(sz, y, fixed, x, core) for y in range(sz.ny)])
                else:
                    groups.append([rank_of(sz, fixed, z, x, core) for z in range(sz.nz)])
    return groups


def per_device(
    image_tokens,
    text_tokens,
    text_counts,
    pair_labels,
    image_expert,
    image_rank,
    image_keep,
    text_expert,
    text_rank,
    text_keep,
    image_gate,
    text_gate,
    w_in,
    w_out,
):
    _, img_tok, feat = image_tokens.shape
    txt_tok = text_tokens.shape[1]
    sz = Sizes(lax.axis_size("expert"), lax.axis_size("dp"), img_tok, txt_tok, feat)
    ff = w_in.shape[2]
    img, txt = image_tokens[0], text_tokens[0]
    routes = (image_expert, image_rank, image_keep, text_expert, text_rank, text_keep)
    gates = (image_gate, text_gate)
    vmem = pl.BlockSpec(memory_space=pltpu.VMEM)
    smem = pl.BlockSpec(memory_space=pltpu.SMEM)

    def whole(shape):
        return pl.BlockSpec(shape, lambda i: (0, 0))

    packed, means = call(
        bind(dispatch_kernel, sz),
        (
            jax.ShapeDtypeStruct((sz.rows, feat), bf16),
            jax.ShapeDtypeStruct((8, feat), f32),
        ),
        grid=(1,),
        in_specs=[smem, smem]
        + [whole((1, img_tok))] * 3
        + [whole((1, txt_tok))] * 3
        + [whole((1, img_tok)), whole((1, txt_tok))]
        + [whole((img_tok, feat)), whole((txt_tok, feat))],
        out_specs=[whole((sz.rows, feat)), whole((8, feat))],
        limit=56,
        name="dispatch",
    )(text_counts, pair_labels, *routes, *gates, img, txt)

    def exchange(rows, count, axes="expert", groups=None):
        rows = rows.reshape(count, rows.shape[0] // count, feat)
        rows = lax.all_to_all(
            rows, axes, split_axis=0, concat_axis=0, tiled=True, axis_index_groups=groups
        )
        return rows.reshape(-1, feat)

    received = exchange(packed, sz.owners)
    block = min(512, ff)
    back_rows = sz.owners * sz.back
    rows, labels = call(
        bind(expert_kernel, sz, min(256, block)),
        (
            jax.ShapeDtypeStruct((back_rows, feat), bf16),
            jax.ShapeDtypeStruct((sz.nx, feat), bf16),
        ),
        grid=(ff // block,),
        in_specs=[
            whole((sz.rows, feat)),
            pl.BlockSpec((feat, block), lambda i: (0, i)),
            pl.BlockSpec((block, feat), lambda i: (i, 0)),
            whole((8, feat)),
        ],
        out_specs=[whole((back_rows, feat)), whole((sz.nx, feat))],
        scratch_shapes=[pltpu.VMEM((sz.rows, feat), f32)],
        limit=56,
        name="expert",
    )(received, w_in[0], w_out[0], means)
    returned = exchange(rows, sz.owners)

    size = 3 * sz.nx
    own, copies = call(
        bind(normalize_kernel, sz),
        (
            jax.ShapeDtypeStruct((size, feat), bf16),
            jax.ShapeDtypeStruct((sz.ny * size, feat), bf16),
        ),
        name="normalize",
    )(returned, labels)
    both = ("dp", "expert")
    got = exchange(copies, sz.ny, both, split_groups(sz, True))
    size = 2 * sz.ny * sz.nx + sz.nx
    copies = call(
        bind(merge_kernel, sz),
        jax.ShapeDtypeStruct((sz.nz * size, feat), bf16),
        name="merge",
    )(got)
    mine = exchange(copies, sz.nz, both, split_groups(sz, False))
    pairs = [(r, r ^ 1) for r in range(sz.pairs)]
    theirs = lax.ppermute(mine, both, pairs)
    img_out, txt_out = call(
        bind(combine_kernel, sz),
        (
            jax.ShapeDtypeStruct((img_tok, feat), bf16),
            jax.ShapeDtypeStruct((txt_tok, feat), bf16),
        ),
        cost=(2 * back_rows * (img_tok + txt_tok) * feat, 4 * back_rows * feat, 0),
        name="combine",
    )(*routes, *gates, img, txt, returned)
    img_grad, txt_grad = call(
        bind(head_kernel, sz),
        (
            jax.ShapeDtypeStruct((1, feat), f32),
            jax.ShapeDtypeStruct((1, feat), f32),
        ),
        in_specs=[smem] + [vmem] * 3,
        scratch_shapes=[pltpu.VMEM((sz.pairs, feat), bf16)] * 2,
        name="head",
    )(pair_labels, own, mine, theirs)
    return (img_out[None], txt_out[None], img_grad, txt_grad)


def solution(mesh):
    both = ("dp", "expert")
    return jax.shard_map(
        per_device,
        mesh=mesh,
        in_specs=(
            P(both, None, None),
            P(both, None, None),
            P(both),
            P(both),
            P(both, None),
            P(both, None),
            P(both, None),
            P(both, None),
            P(both, None),
            P(both, None),
            P(both, None),
            P(both, None),
            P("expert", None, None),
            P("expert", None, None),
        ),
        out_specs=(
            P(both, None, None),
            P(both, None, None),
            P(both, None),
            P(both, None),
        ),
        check_vma=False,
    )
```

time: 159 us -> 131 us (0.82)
  blocking collectives: 0 us -> 106 us
  starting transfers between devices: 74.5 us -> 4.45 us
  waiting for transfers between devices: 57.9 us -> 1.41 us
  local copies, waits for them, and re-layouts: 10.9 us -> 0.07 us
  Pallas kernels: 12.2 us -> 16.3 us
    all_to_all x0 -> x4, blocking collectives: none -> 106 us  [exchange(): lax.all_to_all(rows, axes, split_axis=0, concat_axis=0, tiled=True, axis_...]
    ppermute x12 -> x1, starting transfers between devices: 44.3 us -> 4.45 us  [per_device(): theirs = lax.ppermute(mine, both, pairs)]
    ppermute x12 -> x1, waiting for transfers between devices: 32.8 us -> 1.41 us  [per_device(): theirs = lax.ppermute(mine, both, pairs)]
    all_to_all x2 -> x0, starting transfers between devices: 30.2 us -> none  [exchange(): lax.all_to_all(rows, 'expert', split_axis=0, concat_axis=0, tiled=True)]
    all_to_all x2 -> x0, waiting for transfers between devices: 25.1 us -> none  [exchange(): lax.all_to_all(rows, 'expert', split_axis=0, concat_axis=0, tiled=True)]
    unnamed x44 -> x22, local copies, waits for them, and re-layouts: 10.9 us -> 0.07 us
    pallas_call x7 -> x3, Pallas kernels: 6.54 us -> 8.93 us  [the longest x1 8.48 us: per_device(): call(bind(expert_kernel, sz, min(256, block)), (jax.ShapeDtypeStruct((bac...]
  transfers between devices with their start and end apart: 14 -> 1, of which waited for: 11 -> 1; matrix products, arithmetic and copies ran while one was open for 0% -> 0% of each run, Pallas kernels for 1% -> 1%
where the time goes in v2:
time: 131 us; the launch traced here: 130 us
  blocking collectives  106 us (81%)
  Pallas kernels  16.3 us (12%)
  starting transfers between devices  4.45 us (3%)
  between operations  2.1 us (2%)
  waiting for transfers between devices  1.41 us (1%)
    all_to_all x4, blocking collectives, exchange(): lax.all_to_all(rows, axes, split_axis=0, concat_axis=0, tiled=True, axis_...  106 us
    pallas_call x1, Pallas kernels, per_device(): call(bind(expert_kernel, sz, min(256, block)), (jax.ShapeDtypeStruct((bac...  8.48 us
    ppermute x1, starting transfers between devices, per_device(): theirs = lax.ppermute(mine, both, pairs)  4.45 us
    pallas_call x1, Pallas kernels, per_device(): call(bind(head_kernel, sz), (jax.ShapeDtypeStruct((1, feat), f32), jax.Sh...  3.46 us
    pallas_call x1, Pallas kernels, per_device(): call(bind(dispatch_kernel, sz), (jax.ShapeDtypeStruct((sz.rows, feat), bf...  2.65 us
  transfers between devices with their start and end apart: 1, of which 1 were waited for; matrix products, arithmetic and copies ran while one was open for 0% of the time, Pallas kernels for 1%

profile of v2, /device:TPU:1, one launch (start us, length us, event | category | flops | bytes accessed | tf_op | source)
XLA Modules:
  0.0 129.9 jit_solution(15012265339845708989)
XLA Ops:
  1.9 2.7 %dispatch.1 = (bf16[384,640]{1,0:T(8,128)(2,1)}, f32[8,640]{1,0:T(8,128)}) custom-call(s32[1]{0:T(128)S(6)} %copy.18.refs_0_, s32[1]{0:T(128)S(6)} %copy.19.refs_1_.refs_0_, s32[1,256]{1,0:T(1,128)} %refs_0_.3, s32[1,256]{1,0:T(1,128)} %refs_1_.2, s32[1,256]{1,0:T(1,128)} %refs_2_.3, s32[1,16]{1,0:T(1,128)} %refs_3_.3, s32[1,16]{1,0:T(1,128)} %refs_4_.3, ...), custom_call_target="tpu_custom_call" | custom-call | tf_op jit(solution)/shard_map/dispatch/pallas_call | solution.py:355
  4.6 34.9 %all_to_all.20 = bf16[16,24,640]{2,1,0:T(8,128)(2,1)} all-to-all(bf16[16,24,640]{2,1,0:T(8,128)(2,1)} %bitcast.29), channel_id=1, replica_groups=mesh['dp'=64,'expert'=16] {'expert'}, dimensions={0} | all-to-all | bytes 983040 | tf_op jit(solution)/shard_map/all_to_all | solution.py:374
  39.5 8.5 %expert.1 = (bf16[640,640]{1,0:T(8,128)(2,1)}, bf16[8,640]{1,0:T(8,128)(2,1)}) custom-call(bf16[384,640]{1,0:T(8,128)(2,1)} %bitcast.27, bf16[640,2560]{1,0:T(8,128)(2,1)} %bitcast.25, bf16[2560,640]{1,0:T(8,128)(2,1)} %bitcast.26, f32[8,640]{1,0:T(8,128)} %get-tuple-element.15.refs_3_), custom_call_target="tpu_custom_call" | custom-call | tf_op jit(solution)/shard_map/expert/pallas_call | solution.py:382
  47.9 0.0 copy-start.2
  47.9 26.6 %all_to_all.21 = bf16[16,40,640]{2,1,0:T(8,128)(2,1)S(1)} all-to-all(bf16[16,40,640]{2,1,0:T(8,128)(2,1)} %bitcast.28), channel_id=1, replica_groups=mesh['dp'=64,'expert'=16] {'expert'}, dimensions={0} | all-to-all | bytes 1638400 | tf_op jit(solution)/shard_map/all_to_all | solution.py:374
  74.6 0.0 copy-done.2
  74.6 0.3 normalize.1
  74.9 15.4 %all_to_all.22 = bf16[8,24,640]{2,1,0:T(8,128)(2,1)S(1)} all-to-all(bf16[8,24,640]{2,1,0:T(8,128)(2,1)S(1)} %bitcast.22), channel_id=1, replica_groups={{0,128,256,384,512,640,768,896},{2,130,258,386,514,642,770,898},{4,132,..., dimensions={0} | all-to-all | bytes 491520 | tf_op jit(solution)/shard_map/all_to_all | solution.py:374
  90.4 0.1 merge.1
  90.5 0.0 copy-start
  90.5 0.0 copy-start.1
  90.5 0.0 copy-start.3
  90.5 0.0 copy-start.4
  90.5 0.0 copy-start.5
  90.5 0.0 copy-start.6
  90.5 0.0 copy-start.7
  90.6 0.0 copy-start.8
  90.6 0.0 copy-start.9
  90.6 0.0 copy-start.10
  90.6 28.7 %all_to_all.23 = bf16[8,136,640]{2,1,0:T(8,128)(2,1)S(1)} all-to-all(bf16[8,136,640]{2,1,0:T(8,128)(2,1)S(1)} %bitcast.16), channel_id=1, replica_groups={{0,16,32,48,64,80,96,112},{2,18,34,50,66,82,98,114},{4,20,36,52,68,84,1..., dimensions={0} | all-to-all | bytes 2785280 | tf_op jit(solution)/shard_map/all_to_all | solution.py:374
  119.3 4.5 %collective-permute-start = (bf16[1088,640]{1,0:T(8,128)(2,1)S(1)}, bf16[1088,640]{1,0:T(8,128)(2,1)S(1)}, u32[]{:S(2)}, u32[]{:S(2)}) collective-permute-start(bf16[1088,640]{1,0:T(8,128)(2,1)S(1)} %bitcast.17), channel_id=1, source_target_pairs={{0,1},{1,0},{2,3},{3,2},{4,5},{5,4},{6,7},{7,6},{8,9},{9,8},{10,11... | collective-permute-start | bytes 4177928 | tf_op jit(solution)/shard_map/ppermute | solution.py:421
  123.7 0.0 copy-done
  123.7 0.0 copy-done.1
  123.7 0.0 copy-done.3
  123.8 0.0 copy-done.4
  123.8 0.0 copy-done.5
  123.8 0.0 copy-done.6
  123.8 0.0 copy-done.7
  123.8 0.0 copy-done.8
  123.8 0.0 copy-done.9
  123.8 0.0 copy-done.10
  123.8 1.2 combine.1
  125.1 1.4 %collective-permute-done.refs_3_ = bf16[1088,640]{1,0:T(8,128)(2,1)S(1)} collective-permute-done((bf16[1088,640]{1,0:T(8,128)(2,1)S(1)}, bf16[1088,640]{1,0:T(8,128)(2,1)S(1)}, u32[]{:S(2)}, u32[]{:S(2)}) %collective-permute-start) | collective-permute-done | bytes 1392672 | tf_op jit(solution)/shard_map/ppermute | solution.py:421
  126.5 3.5 %head.1 = (f32[1,640]{1,0:T(1,128)}, f32[1,640]{1,0:T(1,128)}) custom-call(s32[1]{0:T(128)S(6)} %copy.19.refs_1_.refs_0_, bf16[24,640]{1,0:T(8,128)(2,1)S(1)} %get-tuple-element.20.refs_1_, bf16[1088,640]{1,0:T(8,128)(2,1)S(1)} %bitcast.18, bf16[1088,640]{1,0:T(8,128)(2,1)S(1)} %collective-permute-done.refs_3_), custom_call_target="tpu_custom_call" | custom-call | tf_op jit(solution)/shard_map/head/pallas_call | solution.py:431
Async XLA Ops:
  47.9 26.6 %copy-start.2 = (bf16[8,640]{1,0:T(8,128)(2,1)S(1)}, bf16[8,640]{1,0:T(8,128)(2,1)}, u32[]{:S(2)}) copy-start(bf16[8,640]{1,0:T(8,128)(2,1)} %get-tuple-element.19.refs_1_) | copy-start | bytes 30724
  90.5 33.2 %copy-start = (bf16[1,256,640]{2,1,0:T(8,128)(2,1)S(1)}, bf16[1,256,640]{2,1,0:T(8,128)(2,1)}, u32[]{:S(2)}) copy-start(bf16[1,256,640]{2,1,0:T(8,128)(2,1)} %param.14) | copy-start | bytes 983044
  90.5 33.2 %copy-start.1 = (bf16[1,16,640]{2,1,0:T(8,128)(2,1)S(1)}, bf16[1,16,640]{2,1,0:T(8,128)(2,1)}, u32[]{:S(2)}) copy-start(bf16[1,16,640]{2,1,0:T(8,128)(2,1)} %param.15) | copy-start | bytes 61444
  90.5 33.2 %copy-start.3 = (s32[1,256]{1,0:T(1,128)S(1)}, s32[1,256]{1,0:T(1,128)}, u32[]{:S(2)}) copy-start(s32[1,256]{1,0:T(1,128)} %refs_0_.3) | copy-start | bytes 3076
  90.5 33.2 %copy-start.4 = (s32[1,256]{1,0:T(1,128)S(1)}, s32[1,256]{1,0:T(1,128)}, u32[]{:S(2)}) copy-start(s32[1,256]{1,0:T(1,128)} %refs_1_.2) | copy-start | bytes 3076
  90.5 33.2 %copy-start.5 = (s32[1,256]{1,0:T(1,128)S(1)}, s32[1,256]{1,0:T(1,128)}, u32[]{:S(2)}) copy-start(s32[1,256]{1,0:T(1,128)} %refs_2_.3) | copy-start | bytes 3076
  90.5 33.2 %copy-start.6 = (f32[1,256]{1,0:T(1,128)S(1)}, f32[1,256]{1,0:T(1,128)}, u32[]{:S(2)}) copy-start(f32[1,256]{1,0:T(1,128)} %refs_6_.3) | copy-start | bytes 3076
  90.5 33.2 %copy-start.7 = (s32[1,16]{1,0:T(1,128)S(1)}, s32[1,16]{1,0:T(1,128)}, u32[]{:S(2)}) copy-start(s32[1,16]{1,0:T(1,128)} %refs_3_.3) | copy-start | bytes 196
  90.6 33.2 %copy-start.8 = (s32[1,16]{1,0:T(1,128)S(1)}, s32[1,16]{1,0:T(1,128)}, u32[]{:S(2)}) copy-start(s32[1,16]{1,0:T(1,128)} %refs_4_.3) | copy-start | bytes 196
  90.6 33.2 %copy-start.9 = (s32[1,16]{1,0:T(1,128)S(1)}, s32[1,16]{1,0:T(1,128)}, u32[]{:S(2)}) copy-start(s32[1,16]{1,0:T(1,128)} %refs_5_.3) | copy-start | bytes 196
  90.6 33.2 %copy-start.10 = (f32[1,16]{1,0:T(1,128)S(1)}, f32[1,16]{1,0:T(1,128)}, u32[]{:S(2)}) copy-start(f32[1,16]{1,0:T(1,128)} %refs_7_.3) | copy-start | bytes 196
  119.3 7.2 %collective-permute-start = (bf16[1088,640]{1,0:T(8,128)(2,1)S(1)}, bf16[1088,640]{1,0:T(8,128)(2,1)S(1)}, u32[]{:S(2)}, u32[]{:S(2)}) collective-permute-start(bf16[1088,640]{1,0:T(8,128)(2,1)S(1)} %bitcast.17), channel_id=1, source_target_pairs={{0,1},{1,0},{2,3},{3,2},{4,5},{5,4},{6,7},{7,6},{8,9},{9,8},{10,11... | collective-permute-start | bytes 4177928 | tf_op jit(solution)/shard_map/ppermute | solution.py:421

commit v3 on v2

--- a/solution.py
+++ b/solution.py
@@ -51,7 +51,9 @@
         self.slots = self.cap + 2
         self.stride = -(-(self.slots + 2) // 8) * 8
         self.rows = owners * self.stride
-        self.back = self.stride + 2 * self.nx
+        self.per = self.nx // 2
+        self.part = 2 * self.per
+        self.back = self.stride + self.part
         self.half = self.nx * lines
         self.pairs = owners * lines
 
@@ -67,7 +69,18 @@
     )
 
 
-def dispatch_kernel(sz, count_ref, label_ref, ie, ir, ik, te, tr, tk, ig, tg, img, txt, packed, means):
+def dispatch_kernel(sz, count_ref, label_ref, *refs):
+    sources, (packed, means, weights_ref) = refs[:11], refs[11:14]
+    held, sems = refs[14:24], refs[24]
+    copies = [
+        pltpu.make_async_copy(source, target, sems.at[i])
+        for i, (source, target) in enumerate(zip(sources, held + (weights_ref,)))
+    ]
+    for copy in copies:
+        copy.start()
+    for copy in copies[:10]:
+        copy.wait()
+    ie, ir, ik, te, tr, tk, ig, tg, img, txt = held
     img_mask, txt_mask = slot_masks(sz, sz.stride, ie[...], ir[...], ik[...], te[...], tr[...], tk[...])
     count = count_ref[0]
     count_f = jnp.full((1, 1), count, i32).astype(f32)
@@ -104,84 +117,82 @@
     counted = one_hot(iota((8, sz.txt_tok), 1) < count)
     txt_mean = dot(counted, txt[...]) / count_f
     means[...] = jnp.where(iota((8, sz.feat), 0) == 0, img_mean, txt_mean)
+    copies[10].wait()
+
+
+def source_of(sz, r):
+    bits = sz.per.bit_length() - 1
+    parity, core = (r >> (bits + 1)) & 1, r >> (bits + 2)
+    return ((r & (sz.per - 1)) * 2 + parity) * sz.cores + core
 
 
 def gelu(x):
     return 0.5 * x * (1.0 + lax.erf(x * np.float32(np.sqrt(0.5))))
 
 
-def expert_kernel(sz, chunk, x_ref, w_in, w_out, means, back_ref, label_ref, total):
-    step = pl.program_id(0)
-
-    @pl.when(step == 0)
-    def _():
-        total[...] = jnp.zeros_like(total)
-
+def expert_kernel(sz, x_ref, w_in, w_out_source, means, back_ref, label_ref, w_out, sem):
+    copy = pltpu.make_async_copy(w_out_source, w_out, sem)
+    copy.start()
     x = x_ref[...]
-    width = w_in.shape[1]
-    part = None
-    for at in range(0, width, chunk):
-        hidden = gelu(dot(x, w_in[:, at : at + chunk])).astype(bf16)
-        term = dot(hidden, w_out[at : at + chunk, :])
-        part = term if part is None else part + term
-    total[...] += part
-
-    @pl.when(step == pl.num_programs(0) - 1)
-    def _():
-        out = total[...].astype(bf16)
-        count = 2 * sz.owners
-        r = iota((count, sz.rows), 0)
-        c = iota((count, sz.rows), 1)
-        block = divided(c, sz.stride, sz.rows)
-        place = c - block * sz.stride
-        is_txt = (r & sz.nx) > 0
-        source = (r & (sz.nx - 1)) * sz.cores + jnp.where(r >= 2 * sz.nx, 1, 0)
-        held = dot(one_hot(c == source * sz.stride + sz.slots), x)
-        lane = iota((128, sz.rows), 1)
-        lane_place = lane - divided(lane, sz.stride, sz.rows) * sz.stride
-        spread = one_hot(iota((128, sz.rows), 0) == lane_place)
-        own = (block == source) & (
-            jnp.where(is_txt, 1, 0) == jnp.where(place >= sz.cap, 1, 0)
-        ) & (place < sz.slots)
-        pool = jnp.zeros((count, sz.feat), f32)
-        for part_at in range(3):
-            piece = held[:, part_at * 128 : (part_at + 1) * 128].astype(bf16)
-            weight = jnp.where(own, dot(piece, spread), 0.0).astype(bf16)
-            pool = pool + dot(weight, out)
-        me = lax.axis_index("expert")
-        line = lax.axis_index("dp")
-        my_x, my_core = me >> 1, me & 1
-        row = iota((count, sz.feat), 0)
-        my_row = my_core * (2 * sz.nx) + my_x
-        pool = pool + jnp.where(row == my_row, means[0:1, :], 0.0)
-        pool = pool + jnp.where(row == my_row + sz.nx, means[1:2, :], 0.0)
-        lost = pool - pool.astype(bf16).astype(f32)
-        img_lost = jnp.sum(jnp.where(row == my_row, lost, 0.0), axis=0, keepdims=True)
-        txt_lost = jnp.sum(jnp.where(row == my_row + sz.nx, lost, 0.0), axis=0, keepdims=True)
-        spare = iota((sz.stride, sz.feat), 0)
-        blocks = []
-        for e in range(sz.owners):
-            kept = total[e * sz.stride : (e + 1) * sz.stride, :]
-            kept = jnp.where(spare == sz.slots, img_lost, kept)
-            blocks.append(jnp.where(spare == sz.slots + 1, txt_lost, kept))
-            half = (e % sz.cores) * 2 * sz.nx
-            blocks.append(pool[half : half + 2 * sz.nx, :])
-        back_ref[...] = jnp.concatenate(blocks, 0).astype(bf16)
-        r8 = iota((sz.nx, sz.rows), 0)
-        c8 = iota((sz.nx, sz.rows), 1)
-        labels = dot(one_hot(c8 == (r8 * sz.cores + my_core) * sz.stride + sz.slots + 1), x)
-        lane = iota((sz.nx, sz.feat), 1)
-        label_ref[...] = jnp.where((lane == line) | (lane == line + 128), labels, 0.0).astype(bf16)
+    hidden = gelu(dot(x, w_in[...])).astype(bf16)
+    copy.wait()
+    total = dot(hidden, w_out[...])
+    out = total.astype(bf16)
+    me = lax.axis_index("expert")
+    line = lax.axis_index("dp")
+    my_x, my_core = me >> 1, me & 1
+    count = 2 * sz.owners
+    r = iota((count, sz.rows), 0)
+    c = iota((count, sz.rows), 1)
+    block = divided(c, sz.stride, sz.rows)
+    place = c - block * sz.stride
+    is_txt = r & sz.per
+    source = source_of(sz, r)
+    held = dot(one_hot(c == source * sz.stride + sz.slots), x)
+    lane = iota((128, sz.rows), 1)
+    lane_place = lane - divided(lane, sz.stride, sz.rows) * sz.stride
+    spread = one_hot(iota((128, sz.rows), 0) == lane_place)
+    own = (block == source) & (
+        jnp.where(is_txt > 0, 1, 0) == jnp.where(place >= sz.cap, 1, 0)
+    ) & (place < sz.slots)
+    pool = jnp.zeros((count, sz.feat), f32)
+    for part_at in range(3):
+        piece = held[:, part_at * 128 : (part_at + 1) * 128].astype(bf16)
+        weight = jnp.where(own, dot(piece, spread), 0.0).astype(bf16)
+        pool = pool + dot(weight, out)
+    row = iota((count, sz.feat), 0)
+    my_row = (my_core * 2 + (my_x & 1)) * sz.part + (my_x >> 1)
+    pool = pool + jnp.where(row == my_row, means[0:1, :], 0.0)
+    pool = pool + jnp.where(row == my_row + sz.per, means[1:2, :], 0.0)
+    lost = pool - pool.astype(bf16).astype(f32)
+    img_lost = jnp.sum(jnp.where(row == my_row, lost, 0.0), axis=0, keepdims=True)
+    txt_lost = jnp.sum(jnp.where(row == my_row + sz.per, lost, 0.0), axis=0, keepdims=True)
+    spare = iota((sz.stride, sz.feat), 0)
+    blocks = []
+    for e in range(sz.owners):
+        kept = total[e * sz.stride : (e + 1) * sz.stride, :]
+        kept = jnp.where(spare == sz.slots, img_lost, kept)
+        blocks.append(jnp.where(spare == sz.slots + 1, txt_lost, kept))
+        group = (e % sz.cores) * 2 + (e // sz.cores) % 2
+        blocks.append(pool[group * sz.part : (group + 1) * sz.part, :])
+    back_ref[...] = jnp.concatenate(blocks, 0).astype(bf16)
+    r8 = iota((sz.nx, sz.rows), 0)
+    c8 = iota((sz.nx, sz.rows), 1)
+    wanted = (c8 == (r8 * sz.cores + my_core) * sz.stride + sz.slots + 1) & ((r8 & 1) == (my_x & 1))
+    labels = dot(one_hot(wanted), x)
+    lane = iota((sz.nx, sz.feat), 1)
+    label_ref[...] = jnp.where((lane == line) | (lane == line + 128), labels, 0.0).astype(bf16)
 
 
 def normalize_kernel(sz, back, label, out, copies):
-    my_core = lax.axis_index("expert") & 1
-    shape = (2 * sz.nx, sz.owners * sz.back)
+    me = lax.axis_index("expert")
+    group = (me & 1) * 2 + ((me >> 1) & 1)
+    shape = (sz.part, sz.owners * sz.back)
     r, c = iota(shape, 0), iota(shape, 1)
     owner = divided(c, sz.back, shape[1])
     place = c - owner * sz.back
-    spare = jnp.where(r >= sz.nx, sz.slots + 1, sz.slots)
-    left = (place == spare) & (owner == (r & (sz.nx - 1)) * sz.cores + my_core)
+    spare = jnp.where(r >= sz.per, sz.slots + 1, sz.slots)
+    left = (place == spare) & (owner == source_of(sz, r + group * sz.part))
     pooled = dot(one_hot((place == sz.stride + r) | left), back[...])
     norm = jnp.sqrt(jnp.sum(pooled * pooled, axis=1, keepdims=True) + 1e-06)
     block = jnp.concatenate([(pooled / norm).astype(bf16), label[...]], 0)
@@ -201,14 +212,19 @@
 
 
 def merge_kernel(sz, got, copies):
-    size = 3 * sz.nx
-    count = got.shape[0] // size
-    pieces = [got[b * size : b * size + sz.nx, :] for b in range(count)]
-    pieces += [got[b * size + sz.nx : b * size + 2 * sz.nx, :] for b in range(count)]
-    labels = jnp.zeros((sz.nx, sz.feat), f32)
-    for b in range(count):
-        labels = labels + got[b * size + 2 * sz.nx : (b + 1) * size, :].astype(f32)
-    block = jnp.concatenate(pieces + [labels.astype(bf16)], 0)
+    size = sz.part + sz.nx
+    members = got.shape[0] // size
+    count = members * sz.per
+    bits = sz.per.bit_length() - 1
+    shape = (2 * count + sz.nx, got.shape[0])
+    r, c = iota(shape, 0), iota(shape, 1)
+    is_txt = jnp.where(r >= count, 1, 0)
+    pair = r - is_txt * count
+    place = (pair >> bits) * size + is_txt * sz.per + (pair & (sz.per - 1))
+    is_label = r >= 2 * count
+    label = (c & (size - 1)) == r - 2 * count + sz.part
+    chosen = (is_label & label) | (jnp.logical_not(is_label) & (c == place))
+    block = dot(one_hot(chosen), got[...]).astype(bf16)
     for at in range(0, copies.shape[0], block.shape[0]):
         copies[at : at + block.shape[0], :] = block
 
@@ -224,7 +240,8 @@
     def position(line, x, core):
         y, z = line >> z_bits, line & (sz.nz - 1)
         block = jnp.where(core == 0, z * sz.ny + y, y * sz.nz + z)
-        return jnp.where(core == my_core, 0, half) + block * sz.nx + x
+        place = (block * 2 + (x & 1)) * sz.per + (x >> 1)
+        return jnp.where(core == my_core, 0, half) + place
 
     blocks = sz.nz
     each = half // blocks
@@ -240,8 +257,9 @@
         names.append(table)
 
     total = 2 * half
-    row_scores = jnp.exp(logit_scale * dot(own[: sz.nx, :], texts[...], NT))
-    column_scores = jnp.exp(logit_scale * dot(images[...], own[sz.nx : 2 * sz.nx, :], NT))
+    near = own[: sz.part, :]
+    row_scores = jnp.exp(logit_scale * dot(near, texts[...], NT))
+    column_scores = jnp.exp(logit_scale * dot(images[...], near, NT))
     tile = min(256, total)
     column_totals = jnp.zeros((1, total), f32)
     row_totals = []
@@ -253,12 +271,12 @@
     label = label_ref[0]
     owner = label & (sz.owners - 1)
     target = position(label >> (sz.owners.bit_length() - 1), owner >> 1, owner & 1)
-    match = jnp.where(iota((sz.nx, total), 1) == target, 2.0, 0.0)
+    match = jnp.where(iota((sz.part, total), 1) == target, 2.0, 0.0)
     own_rows = jnp.sum(row_scores, axis=1, keepdims=True)
     scores = row_scores / own_rows + row_scores / column_totals - match
     grad = dot(scores.astype(bf16), texts[...])
-    chosen = iota((sz.nx, sz.feat), 0) == my_x
-    img_grad[...] = jnp.sum(jnp.where(chosen, grad, 0.0), axis=0, keepdims=True)
+    own_row = iota((sz.part, sz.feat), 0) - (my_x >> 1)
+    img_grad[...] = jnp.sum(jnp.where(own_row == 0, grad, 0.0), axis=0, keepdims=True)
 
     lane = iota((sz.nx, 128), 1)
     sub = iota((sz.nx, 128), 0)
@@ -277,13 +295,13 @@
     found_core = jnp.where(found[1][2] > 0.5, 1 - my_core, my_core)
     named = position(found_line, found_x, found_core)
     own_columns = jnp.sum(column_scores, axis=0, keepdims=True)
-    grad = jnp.zeros((sz.nx, sz.feat), f32)
+    grad = jnp.zeros((sz.part, sz.feat), f32)
     for t, at in enumerate(range(0, total, tile)):
         rows = column_scores[at : at + tile, :]
-        match = jnp.where(iota((tile, sz.nx), 0) + at == named, 2.0, 0.0)
+        match = jnp.where(iota((tile, sz.part), 0) + at == named, 2.0, 0.0)
         scores = rows / row_totals[t] + rows / own_columns - match
         grad = grad + dot(scores.astype(bf16), images[at : at + tile, :], TN)
-    txt_grad[...] = jnp.sum(jnp.where(chosen, grad, 0.0), axis=0, keepdims=True)
+    txt_grad[...] = jnp.sum(jnp.where(own_row == sz.per, grad, 0.0), axis=0, keepdims=True)
 
 
 def call(kernel, out_shape, in_specs=None, cost=None, limit=24, **kw):
@@ -311,15 +329,17 @@
 
 
 def split_groups(sz, first):
+    width = 2 if first else 1
     groups = []
     for core in range(sz.cores):
         along_y = (core == 0) == first
         for fixed in range(sz.nz if along_y else sz.ny):
-            for x in range(sz.nx):
-                if along_y:
-                    groups.append([rank_of(sz, y, fixed, x, core) for y in range(sz.ny)])
-                else:
-                    groups.append([rank_of(sz, fixed, z, x, core) for z in range(sz.nz)])
+            for x in range(0, sz.nx, width):
+                group = []
+                for moving in range(sz.ny if along_y else sz.nz):
+                    y, z = (moving, fixed) if along_y else (fixed, moving)
+                    group += [rank_of(sz, y, z, x + b, core) for b in range(width)]
+                groups.append(group)
     return groups
 
 
@@ -342,7 +362,6 @@
     _, img_tok, feat = image_tokens.shape
     txt_tok = text_tokens.shape[1]
     sz = Sizes(lax.axis_size("expert"), lax.axis_size("dp"), img_tok, txt_tok, feat)
-    ff = w_in.shape[2]
     img, txt = image_tokens[0], text_tokens[0]
     routes = (image_expert, image_rank, image_keep, text_expert, text_rank, text_keep)
     gates = (image_gate, text_gate)
@@ -352,22 +371,30 @@
     def whole(shape):
         return pl.BlockSpec(shape, lambda i: (0, 0))
 
-    packed, means = call(
+    hbm = pl.BlockSpec(memory_space=pltpu.HBM)
+
+    def in_hbm(value):
+        return pltpu.with_memory_space_constraint(value, pltpu.HBM)
+
+    ff = w_in.shape[2]
+    counts, keys = (1, img_tok), (1, txt_tok)
+    packed, means, w_in_held = call(
         bind(dispatch_kernel, sz),
         (
             jax.ShapeDtypeStruct((sz.rows, feat), bf16),
             jax.ShapeDtypeStruct((8, feat), f32),
-        ),
-        grid=(1,),
-        in_specs=[smem, smem]
-        + [whole((1, img_tok))] * 3
-        + [whole((1, txt_tok))] * 3
-        + [whole((1, img_tok)), whole((1, txt_tok))]
-        + [whole((img_tok, feat)), whole((txt_tok, feat))],
-        out_specs=[whole((sz.rows, feat)), whole((8, feat))],
-        limit=56,
+            jax.ShapeDtypeStruct((feat, ff), bf16),
+        ),
+        in_specs=[smem, smem] + [hbm] * 11,
+        out_specs=[vmem] * 3,
+        scratch_shapes=[pltpu.VMEM(counts, i32)] * 3
+        + [pltpu.VMEM(keys, i32)] * 3
+        + [pltpu.VMEM(counts, f32), pltpu.VMEM(keys, f32)]
+        + [pltpu.VMEM((img_tok, feat), bf16), pltpu.VMEM((txt_tok, feat), bf16)]
+        + [pltpu.SemaphoreType.DMA((11,))],
+        limit=16,
         name="dispatch",
-    )(text_counts, pair_labels, *routes, *gates, img, txt)
+    )(text_counts, pair_labels, *[in_hbm(v) for v in (*routes, *gates, img, txt, w_in[0])])
 
     def exchange(rows, count, axes="expert", groups=None):
         rows = rows.reshape(count, rows.shape[0] // count, feat)
@@ -377,39 +404,31 @@
         return rows.reshape(-1, feat)
 
     received = exchange(packed, sz.owners)
-    block = min(512, ff)
     back_rows = sz.owners * sz.back
     rows, labels = call(
-        bind(expert_kernel, sz, min(256, block)),
+        bind(expert_kernel, sz),
         (
             jax.ShapeDtypeStruct((back_rows, feat), bf16),
             jax.ShapeDtypeStruct((sz.nx, feat), bf16),
         ),
-        grid=(ff // block,),
-        in_specs=[
-            whole((sz.rows, feat)),
-            pl.BlockSpec((feat, block), lambda i: (0, i)),
-            pl.BlockSpec((block, feat), lambda i: (i, 0)),
-            whole((8, feat)),
-        ],
-        out_specs=[whole((back_rows, feat)), whole((sz.nx, feat))],
-        scratch_shapes=[pltpu.VMEM((sz.rows, feat), f32)],
-        limit=56,
+        in_specs=[vmem, vmem, hbm, vmem],
+        scratch_shapes=[pltpu.VMEM((ff, feat), bf16), pltpu.SemaphoreType.DMA],
+        limit=28,
         name="expert",
-    )(received, w_in[0], w_out[0], means)
+    )(received, w_in_held, w_out[0], means)
     returned = exchange(rows, sz.owners)
 
-    size = 3 * sz.nx
+    size = sz.part + sz.nx
     own, copies = call(
         bind(normalize_kernel, sz),
         (
             jax.ShapeDtypeStruct((size, feat), bf16),
-            jax.ShapeDtypeStruct((sz.ny * size, feat), bf16),
+            jax.ShapeDtypeStruct((2 * sz.ny * size, feat), bf16),
         ),
         name="normalize",
     )(returned, labels)
     both = ("dp", "expert")
-    got = exchange(copies, sz.ny, both, split_groups(sz, True))
+    got = exchange(copies, 2 * sz.ny, both, split_groups(sz, True))
     size = 2 * sz.ny * sz.nx + sz.nx
     copies = call(
         bind(merge_kernel, sz),

time: 131 us -> 124 us (0.947)
  blocking collectives: 106 us -> 102 us
  Pallas kernels: 16.3 us -> 12.6 us
    all_to_all x4, blocking collectives: 106 us -> 102 us  [exchange(): lax.all_to_all(rows, axes, split_axis=0, concat_axis=0, tiled=True, axis_...]
    pallas_call x1, Pallas kernels: 8.48 us -> 5.11 us  [per_device(): call(bind(expert_kernel, sz), (jax.ShapeDtypeStruct((back_rows, feat), bf...]
where the time goes in v3:
time: 124 us
  blocking collectives  102 us (82%)
  Pallas kernels  12.6 us (10%)
  starting transfers between devices  5.11 us (4%)
  between operations  2.44 us (2%)
  waiting for transfers between devices  1.51 us (1%)
    all_to_all x4, blocking collectives, exchange(): lax.all_to_all(rows, axes, split_axis=0, concat_axis=0, tiled=True, axis_...  102 us
    ppermute x1, starting transfers between devices, per_device(): theirs = lax.ppermute(mine, both, pairs)  5.11 us
    pallas_call x1, Pallas kernels, per_device(): call(bind(expert_kernel, sz), (jax.ShapeDtypeStruct((back_rows, feat), bf...  5.11 us
    pallas_call x1, Pallas kernels, per_device(): call(bind(head_kernel, sz), (jax.ShapeDtypeStruct((1, feat), f32), jax.Sh...  3.47 us
  transfers between devices with their start and end apart: 1, of which 1 were waited for; matrix products, arithmetic and copies ran while one was open for 0% of the time, Pallas kernels for 1%

profile of v3, /device:TPU:1, one launch (start us, length us, event | category | flops | bytes accessed | tf_op | source)
XLA Modules:
  0.0 123.5 jit_solution(14910097424474481573)
XLA Ops:
  0.6 0.0 copy-start
  2.2 2.3 %dispatch.1 = (bf16[384,640]{1,0:T(8,128)(2,1)S(1)}, f32[8,640]{1,0:T(8,128)S(1)}, bf16[640,2560]{1,0:T(8,128)(2,1)S(1)}) custom-call(s32[1]{0:T(128)S(6)} %copy.18.refs_0_, s32[1]{0:T(128)S(6)} %copy.19.refs_1_.refs_0_, s32[1,256]{1,0:T(1,128)} %refs_0_.3, s32[1,256]{1,0:T(1,128)} %refs_1_.2, s32[1,256]{1,0:T(1,128)} %refs_2_.3, s32[1,16]{1,0:T(1,128)} %refs_3_.3, ...), custom_call_target="tpu_custom_call" | custom-call | tf_op jit(solution)/shard_map/dispatch/pallas_call | solution.py:381
  4.5 33.3 %all_to_all.20 = bf16[16,24,640]{2,1,0:T(8,128)(2,1)S(1)} all-to-all(bf16[16,24,640]{2,1,0:T(8,128)(2,1)S(1)} %bitcast.25), channel_id=1, replica_groups=mesh['dp'=64,'expert'=16] {'expert'}, dimensions={0} | all-to-all | bytes 983040 | tf_op jit(solution)/shard_map/all_to_all | solution.py:401
  37.8 0.0 copy-done
  37.8 5.1 %expert.1 = (bf16[512,640]{1,0:T(8,128)(2,1)S(1)}, bf16[8,640]{1,0:T(8,128)(2,1)S(1)}) custom-call(bf16[384,640]{1,0:T(8,128)(2,1)S(1)} %bitcast.20, bf16[640,2560]{1,0:T(8,128)(2,1)S(1)} %get-tuple-element.16.refs_1_, bf16[2560,640]{1,0:T(8,128)(2,1)S(1)} %bitcast.19, f32[8,640]{1,0:T(8,128)S(1)} %get-tuple-element.17.refs_3_), custom_call_target="tpu_custom_call" | custom-call | tf_op jit(solution)/shard_map/expert/pallas_call | solution.py:408
  42.9 0.0 copy-start.1
  42.9 0.0 copy-start.2
  42.9 0.0 copy-start.3
  42.9 0.0 copy-start.4
  42.9 0.0 copy-start.5
  42.9 0.0 copy-start.6
  43.0 0.0 copy-start.7
  43.0 0.0 copy-start.8
  43.0 0.0 copy-start.9
  43.0 0.0 copy-start.10
  43.0 23.1 %all_to_all.21 = bf16[16,32,640]{2,1,0:T(8,128)(2,1)S(1)} all-to-all(bf16[16,32,640]{2,1,0:T(8,128)(2,1)S(1)} %bitcast.24), channel_id=1, replica_groups=mesh['dp'=64,'expert'=16] {'expert'}, dimensions={0} | all-to-all | bytes 1310720 | tf_op jit(solution)/shard_map/all_to_all | solution.py:401
  66.1 0.3 normalize.1
  66.4 17.0 %all_to_all.22 = bf16[16,16,640]{2,1,0:T(8,128)(2,1)S(1)} all-to-all(bf16[16,16,640]{2,1,0:T(8,128)(2,1)S(1)} %bitcast.26), channel_id=1, replica_groups={{0,2,128,130,256,258,384,386,512,514,640,642,768,770,896,898},{4,6,132,..., dimensions={0} | all-to-all | bytes 655360 | tf_op jit(solution)/shard_map/all_to_all | solution.py:401
  83.4 0.3 merge.1
  83.7 28.5 %all_to_all.23 = bf16[8,136,640]{2,1,0:T(8,128)(2,1)S(1)} all-to-all(bf16[8,136,640]{2,1,0:T(8,128)(2,1)S(1)} %bitcast.18), channel_id=1, replica_groups={{0,16,32,48,64,80,96,112},{2,18,34,50,66,82,98,114},{4,20,36,52,68,84,1..., dimensions={0} | all-to-all | bytes 2785280 | tf_op jit(solution)/shard_map/all_to_all | solution.py:401
  112.2 5.1 %collective-permute-start = (bf16[1088,640]{1,0:T(8,128)(2,1)S(1)}, bf16[1088,640]{1,0:T(8,128)(2,1)S(1)}, u32[]{:S(2)}, u32[]{:S(2)}) collective-permute-start(bf16[1088,640]{1,0:T(8,128)(2,1)S(1)} %bitcast.16), channel_id=1, source_target_pairs={{0,1},{1,0},{2,3},{3,2},{4,5},{5,4},{6,7},{7,6},{8,9},{9,8},{10,11... | collective-permute-start | bytes 4177928 | tf_op jit(solution)/shard_map/ppermute | solution.py:440
  117.3 0.0 copy-done.1
  117.3 0.0 copy-done.2
  117.3 0.0 copy-done.3
  117.3 0.0 copy-done.4
  117.3 0.0 copy-done.5
  117.3 0.0 copy-done.6
  117.3 0.0 copy-done.7
  117.4 0.0 copy-done.8
  117.4 0.0 copy-done.9
  117.4 0.0 copy-done.10
  117.4 1.1 combine.1
  118.5 1.5 %collective-permute-done.refs_3_ = bf16[1088,640]{1,0:T(8,128)(2,1)S(1)} collective-permute-done((bf16[1088,640]{1,0:T(8,128)(2,1)S(1)}, bf16[1088,640]{1,0:T(8,128)(2,1)S(1)}, u32[]{:S(2)}, u32[]{:S(2)}) %collective-permute-start) | collective-permute-done | bytes 1392672 | tf_op jit(solution)/shard_map/ppermute | solution.py:440
  120.0 3.5 %head.1 = (f32[1,640]{1,0:T(1,128)}, f32[1,640]{1,0:T(1,128)}) custom-call(s32[1]{0:T(128)S(6)} %copy.19.refs_1_.refs_0_, bf16[16,640]{1,0:T(8,128)(2,1)S(1)} %get-tuple-element.22.refs_1_, bf16[1088,640]{1,0:T(8,128)(2,1)S(1)} %bitcast.17, bf16[1088,640]{1,0:T(8,128)(2,1)S(1)} %collective-permute-done.refs_3_), custom_call_target="tpu_custom_call" | custom-call | tf_op jit(solution)/shard_map/head/pallas_call | solution.py:450
Async XLA Ops:
  0.6 37.1 %copy-start = (bf16[1,2560,640]{2,1,0:T(8,128)(2,1)S(1)}, bf16[1,2560,640]{2,1,0:T(8,128)(2,1)}, u32[]{:S(2)}) copy-start(bf16[1,2560,640]{2,1,0:T(8,128)(2,1)} %param.27) | copy-start | bytes 9830404
  42.9 74.4 %copy-start.1 = (bf16[1,256,640]{2,1,0:T(8,128)(2,1)S(1)}, bf16[1,256,640]{2,1,0:T(8,128)(2,1)}, u32[]{:S(2)}) copy-start(bf16[1,256,640]{2,1,0:T(8,128)(2,1)} %param.14) | copy-start | bytes 983044
  42.9 74.4 %copy-start.2 = (bf16[1,16,640]{2,1,0:T(8,128)(2,1)S(1)}, bf16[1,16,640]{2,1,0:T(8,128)(2,1)}, u32[]{:S(2)}) copy-start(bf16[1,16,640]{2,1,0:T(8,128)(2,1)} %param.15) | copy-start | bytes 61444
  42.9 74.4 %copy-start.3 = (s32[1,256]{1,0:T(1,128)S(1)}, s32[1,256]{1,0:T(1,128)}, u32[]{:S(2)}) copy-start(s32[1,256]{1,0:T(1,128)} %refs_0_.3) | copy-start | bytes 3076
  42.9 74.4 %copy-start.4 = (s32[1,256]{1,0:T(1,128)S(1)}, s32[1,256]{1,0:T(1,128)}, u32[]{:S(2)}) copy-start(s32[1,256]{1,0:T(1,128)} %refs_1_.2) | copy-start | bytes 3076
  42.9 74.4 %copy-start.5 = (s32[1,256]{1,0:T(1,128)S(1)}, s32[1,256]{1,0:T(1,128)}, u32[]{:S(2)}) copy-start(s32[1,256]{1,0:T(1,128)} %refs_2_.3) | copy-start | bytes 3076
  42.9 74.4 %copy-start.6 = (f32[1,256]{1,0:T(1,128)S(1)}, f32[1,256]{1,0:T(1,128)}, u32[]{:S(2)}) copy-start(f32[1,256]{1,0:T(1,128)} %refs_6_.3) | copy-start | bytes 3076
  43.0 74.4 %copy-start.7 = (s32[1,16]{1,0:T(1,128)S(1)}, s32[1,16]{1,0:T(1,128)}, u32[]{:S(2)}) copy-start(s32[1,16]{1,0:T(1,128)} %refs_3_.3) | copy-start | bytes 196
  43.0 74.4 %copy-start.8 = (s32[1,16]{1,0:T(1,128)S(1)}, s32[1,16]{1,0:T(1,128)}, u32[]{:S(2)}) copy-start(s32[1,16]{1,0:T(1,128)} %refs_4_.3) | copy-start | bytes 196
  43.0 74.4 %copy-start.9 = (s32[1,16]{1,0:T(1,128)S(1)}, s32[1,16]{1,0:T(1,128)}, u32[]{:S(2)}) copy-start(s32[1,16]{1,0:T(1,128)} %refs_5_.3) | copy-start | bytes 196
  43.0 74.4 %copy-start.10 = (f32[1,16]{1,0:T(1,128)S(1)}, f32[1,16]{1,0:T(1,128)}, u32[]{:S(2)}) copy-start(f32[1,16]{1,0:T(1,128)} %refs_7_.3) | copy-start | bytes 196
  112.2 7.9 %collective-permute-start = (bf16[1088,640]{1,0:T(8,128)(2,1)S(1)}, bf16[1088,640]{1,0:T(8,128)(2,1)S(1)}, u32[]{:S(2)}, u32[]{:S(2)}) collective-permute-start(bf16[1088,640]{1,0:T(8,128)(2,1)S(1)} %bitcast.16), channel_id=1, source_target_pairs={{0,1},{1,0},{2,3},{3,2},{4,5},{5,4},{6,7},{7,6},{8,9},{9,8},{10,11... | collective-permute-start | bytes 4177928 | tf_op jit(solution)/shard_map/ppermute | solution.py:440

commit v4 on v3

--- a/solution.py
+++ b/solution.py
@@ -82,9 +82,8 @@
         copy.wait()
     ie, ir, ik, te, tr, tk, ig, tg, img, txt = held
     img_mask, txt_mask = slot_masks(sz, sz.stride, ie[...], ir[...], ik[...], te[...], tr[...], tk[...])
-    count = count_ref[0]
+    count, label = count_ref[0], label_ref[0]
     count_f = jnp.full((1, 1), count, i32).astype(f32)
-    label = label_ref[0]
     img_weight = jnp.where(ik[...] == 1, ig[...], 0.0) * (1.0 / sz.img_tok)
     valid = iota((1, sz.txt_tok), 1) < count
     txt_weight = jnp.where((tk[...] == 1) & valid, tg[...], 0.0) / count_f
@@ -92,11 +91,11 @@
     txt_place = one_hot(iota((128, sz.txt_tok), 0) == tr[...] + sz.cap)
     img_at = iota((sz.owners, sz.img_tok), 0) == ie[...]
     txt_at = iota((sz.owners, sz.txt_tok), 0) == te[...]
-    tables = []
-    for img_part, txt_part in zip(three_parts(img_weight), three_parts(txt_weight)):
-        img_side = jnp.where(img_at, img_part.astype(f32), 0.0).astype(bf16)
-        txt_side = jnp.where(txt_at, txt_part.astype(f32), 0.0).astype(bf16)
-        tables.append(dot(img_side, img_place, NT) + dot(txt_side, txt_place, NT))
+    img_side = [jnp.where(img_at, part.astype(f32), 0.0) for part in three_parts(img_weight)]
+    txt_side = [jnp.where(txt_at, part.astype(f32), 0.0) for part in three_parts(txt_weight)]
+    table = dot(jnp.concatenate(img_side, 0).astype(bf16), img_place, NT)
+    table = table + dot(jnp.concatenate(txt_side, 0).astype(bf16), txt_place, NT)
+    tables = [table[at * sz.owners : (at + 1) * sz.owners] for at in range(3)]
     pad = sz.feat - 3 * 128
     if pad:
         tables.append(jnp.zeros((sz.owners, pad), f32))
@@ -148,18 +147,24 @@
     place = c - block * sz.stride
     is_txt = r & sz.per
     source = source_of(sz, r)
-    held = dot(one_hot(c == source * sz.stride + sz.slots), x)
+    r8 = iota((sz.nx, sz.rows), 0)
+    c8 = iota((sz.nx, sz.rows), 1)
+    wanted = (c8 == (r8 * sz.cores + my_core) * sz.stride + sz.slots + 1) & ((r8 & 1) == (my_x & 1))
+    weighing = jnp.where(c == source * sz.stride + sz.slots, 1.0, 0.0)
+    labelling = jnp.where(wanted, 1.0, 0.0)
+    held = dot(jnp.concatenate([weighing, labelling], 0).astype(bf16), x)
+    labels = held[count:, :]
     lane = iota((128, sz.rows), 1)
     lane_place = lane - divided(lane, sz.stride, sz.rows) * sz.stride
     spread = one_hot(iota((128, sz.rows), 0) == lane_place)
     own = (block == source) & (
         jnp.where(is_txt > 0, 1, 0) == jnp.where(place >= sz.cap, 1, 0)
     ) & (place < sz.slots)
-    pool = jnp.zeros((count, sz.feat), f32)
-    for part_at in range(3):
-        piece = held[:, part_at * 128 : (part_at + 1) * 128].astype(bf16)
-        weight = jnp.where(own, dot(piece, spread), 0.0).astype(bf16)
-        pool = pool + dot(weight, out)
+    pieces = [held[:count, at : at + 128] for at in (0, 128, 256)]
+    weight = dot(jnp.concatenate(pieces, 0).astype(bf16), spread)
+    weight = jnp.where(jnp.concatenate([own] * 3, 0), weight, 0.0)
+    pool = dot(weight.astype(bf16), out)
+    pool = pool[:count] + pool[count : 2 * count] + pool[2 * count :]
     row = iota((count, sz.feat), 0)
     my_row = (my_core * 2 + (my_x & 1)) * sz.part + (my_x >> 1)
     pool = pool + jnp.where(row == my_row, means[0:1, :], 0.0)
@@ -176,10 +181,6 @@
         group = (e % sz.cores) * 2 + (e // sz.cores) % 2
         blocks.append(pool[group * sz.part : (group + 1) * sz.part, :])
     back_ref[...] = jnp.concatenate(blocks, 0).astype(bf16)
-    r8 = iota((sz.nx, sz.rows), 0)
-    c8 = iota((sz.nx, sz.rows), 1)
-    wanted = (c8 == (r8 * sz.cores + my_core) * sz.stride + sz.slots + 1) & ((r8 & 1) == (my_x & 1))
-    labels = dot(one_hot(wanted), x)
     lane = iota((sz.nx, sz.feat), 1)
     label_ref[...] = jnp.where((lane == line) | (lane == line + 128), labels, 0.0).astype(bf16)
 
@@ -229,7 +230,39 @@
         copies[at : at + block.shape[0], :] = block
 
 
-def head_kernel(sz, label_ref, own, mine, theirs, img_grad, txt_grad, images, texts):
+def unpack(sz, got, images, texts):
+    each = sz.half // sz.nz
+    size = 2 * each + sz.nx
+    table = jnp.zeros((sz.nx, 256), f32)
+    for b in range(sz.nz):
+        at, to = b * size, b * each
+        images[to : to + each, :] = got[at : at + each, :]
+        texts[to : to + each, :] = got[at + each : at + 2 * each, :]
+        table = table + got[at + 2 * each : at + size, 0:256].astype(f32)
+    return table
+
+
+def exp_scores(left, right):
+    return jnp.exp(logit_scale * dot(left, right, NT))
+
+
+def first_head_kernel(sz, own, mine, images, texts, table, row_totals, column_totals, strips):
+    half = sz.half
+    table[...] = unpack(sz, mine, images, texts)
+    tile = min(256, half)
+    totals = jnp.zeros((1, half), f32)
+    for at in range(0, half, tile):
+        scores = exp_scores(images[at : at + tile, :], texts[...])
+        row_totals[at : at + tile, :] = jnp.sum(scores, axis=1, keepdims=True)
+        totals = totals + jnp.sum(scores, axis=0, keepdims=True)
+    column_totals[...] = totals
+    strips[...] = exp_scores(own[: sz.part, :], texts[...])
+
+
+def head_kernel(
+    sz, label_ref, own, theirs, images_a, texts_a, table_a, rows_a, columns_a, strip_a,
+    img_grad, txt_grad, images_b, texts_b,
+):
     half = sz.half
     me = lax.axis_index("expert")
     line = lax.axis_index("dp")
@@ -243,38 +276,33 @@
         place = (block * 2 + (x & 1)) * sz.per + (x >> 1)
         return jnp.where(core == my_core, 0, half) + place
 
-    blocks = sz.nz
-    each = half // blocks
-    size = 2 * each + sz.nx
-    names = []
-    for a, got in enumerate((mine, theirs)):
-        table = jnp.zeros((sz.nx, 256), f32)
-        for b in range(blocks):
-            at, to = b * size, a * half + b * each
-            images[to : to + each, :] = got[at : at + each, :]
-            texts[to : to + each, :] = got[at + each : at + 2 * each, :]
-            table = table + got[at + 2 * each : at + size, 0:256].astype(f32)
-        names.append(table)
-
-    total = 2 * half
+    names = [table_a[...], unpack(sz, theirs, images_b, texts_b)]
     near = own[: sz.part, :]
-    row_scores = jnp.exp(logit_scale * dot(near, texts[...], NT))
-    column_scores = jnp.exp(logit_scale * dot(images[...], near, NT))
-    tile = min(256, total)
-    column_totals = jnp.zeros((1, total), f32)
-    row_totals = []
-    for at in range(0, total, tile):
-        scores = jnp.exp(logit_scale * dot(images[at : at + tile, :], texts[...], NT))
-        row_totals.append(jnp.sum(scores, axis=1, keepdims=True))
-        column_totals = column_totals + jnp.sum(scores, axis=0, keepdims=True)
+    tile = min(256, half)
+    columns = [columns_a[...], jnp.zeros((1, half), f32)]
+    rows = [[rows_a[at : at + tile, :] for at in range(0, half, tile)], []]
+    for t, at in enumerate(range(0, half, tile)):
+        scores = exp_scores(images_a[at : at + tile, :], texts_b[...])
+        rows[0][t] = rows[0][t] + jnp.sum(scores, axis=1, keepdims=True)
+        columns[1] = columns[1] + jnp.sum(scores, axis=0, keepdims=True)
+    for at in range(0, half, tile):
+        total = jnp.zeros((tile, 1), f32)
+        for b, texts in enumerate((texts_a, texts_b)):
+            scores = exp_scores(images_b[at : at + tile, :], texts[...])
+            total = total + jnp.sum(scores, axis=1, keepdims=True)
+            columns[b] = columns[b] + jnp.sum(scores, axis=0, keepdims=True)
+        rows[1].append(total)
 
     label = label_ref[0]
     owner = label & (sz.owners - 1)
     target = position(label >> (sz.owners.bit_length() - 1), owner >> 1, owner & 1)
-    match = jnp.where(iota((sz.part, total), 1) == target, 2.0, 0.0)
-    own_rows = jnp.sum(row_scores, axis=1, keepdims=True)
-    scores = row_scores / own_rows + row_scores / column_totals - match
-    grad = dot(scores.astype(bf16), texts[...])
+    strips = [strip_a[...], exp_scores(near, texts_b[...])]
+    own_rows = sum(jnp.sum(strip, axis=1, keepdims=True) for strip in strips)
+    grad = jnp.zeros((sz.part, sz.feat), f32)
+    for b, texts in enumerate((texts_a, texts_b)):
+        match = jnp.where(iota((sz.part, half), 1) + b * half == target, 2.0, 0.0)
+        scores = strips[b] / own_rows + strips[b] / columns[b] - match
+        grad = grad + dot(scores.astype(bf16), texts[...])
     own_row = iota((sz.part, sz.feat), 0) - (my_x >> 1)
     img_grad[...] = jnp.sum(jnp.where(own_row == 0, grad, 0.0), axis=0, keepdims=True)
 
@@ -294,13 +322,15 @@
     found_x = (found[0][1] + found[1][1]).astype(i32)
     found_core = jnp.where(found[1][2] > 0.5, 1 - my_core, my_core)
     named = position(found_line, found_x, found_core)
-    own_columns = jnp.sum(column_scores, axis=0, keepdims=True)
+    strips = [exp_scores(images[...], near) for images in (images_a, images_b)]
+    own_columns = sum(jnp.sum(strip, axis=0, keepdims=True) for strip in strips)
     grad = jnp.zeros((sz.part, sz.feat), f32)
-    for t, at in enumerate(range(0, total, tile)):
-        rows = column_scores[at : at + tile, :]
-        match = jnp.where(iota((tile, sz.part), 0) + at == named, 2.0, 0.0)
-        scores = rows / row_totals[t] + rows / own_columns - match
-        grad = grad + dot(scores.astype(bf16), images[at : at + tile, :], TN)
+    for a, images in enumerate((images_a, images_b)):
+        for t, at in enumerate(range(0, half, tile)):
+            strip = strips[a][at : at + tile, :]
+            match = jnp.where(iota((tile, sz.part), 0) + a * half + at == named, 2.0, 0.0)
+            scores = strip / rows[a][t] + strip / own_columns - match
+            grad = grad + dot(scores.astype(bf16), images[at : at + tile, :], TN)
     txt_grad[...] = jnp.sum(jnp.where(own_row == sz.per, grad, 0.0), axis=0, keepdims=True)
 
 
@@ -385,7 +415,7 @@
             jax.ShapeDtypeStruct((8, feat), f32),
             jax.ShapeDtypeStruct((feat, ff), bf16),
         ),
-        in_specs=[smem, smem] + [hbm] * 11,
+        in_specs=[smem] * 2 + [hbm] * 11,
         out_specs=[vmem] * 3,
         scratch_shapes=[pltpu.VMEM(counts, i32)] * 3
         + [pltpu.VMEM(keys, i32)] * 3
@@ -447,16 +477,29 @@
         cost=(2 * back_rows * (img_tok + txt_tok) * feat, 4 * back_rows * feat, 0),
         name="combine",
     )(*routes, *gates, img, txt, returned)
+    halves = [jax.ShapeDtypeStruct((sz.half, feat), bf16)] * 2
+    first = call(
+        bind(first_head_kernel, sz),
+        (
+            *halves,
+            jax.ShapeDtypeStruct((sz.nx, 256), f32),
+            jax.ShapeDtypeStruct((sz.half, 1), f32),
+            jax.ShapeDtypeStruct((1, sz.half), f32),
+            jax.ShapeDtypeStruct((sz.part, sz.half), f32),
+        ),
+        cost=(2 * sz.half * sz.half * feat, 4 * sz.half * feat, sz.half * sz.half),
+        name="first_head",
+    )(own, mine)
     img_grad, txt_grad = call(
         bind(head_kernel, sz),
         (
             jax.ShapeDtypeStruct((1, feat), f32),
             jax.ShapeDtypeStruct((1, feat), f32),
         ),
-        in_specs=[smem] + [vmem] * 3,
-        scratch_shapes=[pltpu.VMEM((sz.pairs, feat), bf16)] * 2,
+        in_specs=[smem] + [vmem] * 8,
+        scratch_shapes=[pltpu.VMEM((sz.half, feat), bf16)] * 2,
         name="head",
-    )(pair_labels, own, mine, theirs)
+    )(pair_labels, own, theirs, *first)
     return (img_out[None], txt_out[None], img_grad, txt_grad)
 
 

time: 124 us -> 123 us (level)
  transfers between devices with their start and end apart: 1 -> 1, of which waited for: 1 -> 1; matrix products, arithmetic and copies ran while one was open for 0% -> 0% of each run, Pallas kernels for 1% -> 2%
where the time goes in v4:
time: 123 us
  blocking collectives  102 us (83%)
  Pallas kernels  12.9 us (10%)
  starting transfers between devices  5.11 us (4%)
  between operations  2.44 us (2%)
    all_to_all x4, blocking collectives, exchange(): lax.all_to_all(rows, axes, split_axis=0, concat_axis=0, tiled=True, axis_...  102 us
    ppermute x1, starting transfers between devices, per_device(): theirs = lax.ppermute(mine, both, pairs)  5.11 us
    pallas_call x1, Pallas kernels, per_device(): call(bind(expert_kernel, sz), (jax.ShapeDtypeStruct((back_rows, feat), bf...  4.78 us
    pallas_call x1, Pallas kernels, per_device(): call(bind(head_kernel, sz), (jax.ShapeDtypeStruct((1, feat), f32), jax.Sh...  3.32 us
  transfers between devices with their start and end apart: 1, of which 1 were waited for; matrix products, arithmetic and copies ran while one was open for 0% of the time, Pallas kernels for 2%

profile of v4, /device:TPU:1, one launch (start us, length us, event | category | flops | bytes accessed | tf_op | source)
XLA Modules:
  0.0 123.0 jit_solution(2639684048390292196)
XLA Ops:
  0.6 0.0 copy-start
  2.2 2.3 %dispatch.1 = (bf16[384,640]{1,0:T(8,128)(2,1)S(1)}, f32[8,640]{1,0:T(8,128)S(1)}, bf16[640,2560]{1,0:T(8,128)(2,1)S(1)}) custom-call(s32[1]{0:T(128)S(6)} %copy.18.refs_0_, s32[1]{0:T(128)S(6)} %copy.19.refs_1_.refs_0_, s32[1,256]{1,0:T(1,128)} %refs_0_.3, s32[1,256]{1,0:T(1,128)} %refs_1_.2, s32[1,256]{1,0:T(1,128)} %refs_2_.3, s32[1,16]{1,0:T(1,128)} %refs_3_.3, ...), custom_call_target="tpu_custom_call" | custom-call | tf_op jit(solution)/shard_map/dispatch/pallas_call | solution.py:411
  4.5 33.3 %all_to_all.20 = bf16[16,24,640]{2,1,0:T(8,128)(2,1)S(1)} all-to-all(bf16[16,24,640]{2,1,0:T(8,128)(2,1)S(1)} %bitcast.25), channel_id=1, replica_groups=mesh['dp'=64,'expert'=16] {'expert'}, dimensions={0} | all-to-all | bytes 983040 | tf_op jit(solution)/shard_map/all_to_all | solution.py:431
  37.8 0.0 copy-done
  37.8 4.8 %expert.1 = (bf16[512,640]{1,0:T(8,128)(2,1)S(1)}, bf16[8,640]{1,0:T(8,128)(2,1)S(1)}) custom-call(bf16[384,640]{1,0:T(8,128)(2,1)S(1)} %bitcast.20, bf16[640,2560]{1,0:T(8,128)(2,1)S(1)} %get-tuple-element.22.refs_1_, bf16[2560,640]{1,0:T(8,128)(2,1)S(1)} %bitcast.19, f32[8,640]{1,0:T(8,128)S(1)} %get-tuple-element.23.refs_3_), custom_call_target="tpu_custom_call" | custom-call | tf_op jit(solution)/shard_map/expert/pallas_call | solution.py:438
  42.6 0.0 copy-start.1
  42.6 0.0 copy-start.2
  42.6 0.0 copy-start.3
  42.6 0.0 copy-start.4
  42.6 0.0 copy-start.5
  42.6 0.0 copy-start.6
  42.6 0.0 copy-start.7
  42.6 0.0 copy-start.8
  42.7 0.0 copy-start.9
  42.7 0.0 copy-start.10
  42.7 23.1 %all_to_all.21 = bf16[16,32,640]{2,1,0:T(8,128)(2,1)S(1)} all-to-all(bf16[16,32,640]{2,1,0:T(8,128)(2,1)S(1)} %bitcast.24), channel_id=1, replica_groups=mesh['dp'=64,'expert'=16] {'expert'}, dimensions={0} | all-to-all | bytes 1310720 | tf_op jit(solution)/shard_map/all_to_all | solution.py:431
  65.7 0.3 normalize.1
  66.1 17.0 %all_to_all.22 = bf16[16,16,640]{2,1,0:T(8,128)(2,1)S(1)} all-to-all(bf16[16,16,640]{2,1,0:T(8,128)(2,1)S(1)} %bitcast.26), channel_id=1, replica_groups={{0,2,128,130,256,258,384,386,512,514,640,642,768,770,896,898},{4,6,132,..., dimensions={0} | all-to-all | bytes 655360 | tf_op jit(solution)/shard_map/all_to_all | solution.py:431
  83.1 0.3 merge.1
  83.4 28.5 %all_to_all.23 = bf16[8,136,640]{2,1,0:T(8,128)(2,1)S(1)} all-to-all(bf16[8,136,640]{2,1,0:T(8,128)(2,1)S(1)} %bitcast.18), channel_id=1, replica_groups={{0,16,32,48,64,80,96,112},{2,18,34,50,66,82,98,114},{4,20,36,52,68,84,1..., dimensions={0} | all-to-all | bytes 2785280 | tf_op jit(solution)/shard_map/all_to_all | solution.py:431
  111.8 5.1 %collective-permute-start = (bf16[1088,640]{1,0:T(8,128)(2,1)S(1)}, bf16[1088,640]{1,0:T(8,128)(2,1)S(1)}, u32[]{:S(2)}, u32[]{:S(2)}) collective-permute-start(bf16[1088,640]{1,0:T(8,128)(2,1)S(1)} %bitcast.16), channel_id=1, source_target_pairs={{0,1},{1,0},{2,3},{3,2},{4,5},{5,4},{6,7},{7,6},{8,9},{9,8},{10,11... | collective-permute-start | bytes 4177928 | tf_op jit(solution)/shard_map/ppermute | solution.py:470
  117.0 0.0 copy-done.1
  117.0 0.0 copy-done.2
  117.0 0.0 copy-done.3
  117.0 0.0 copy-done.4
  117.0 0.0 copy-done.5
  117.0 0.0 copy-done.6
  117.0 0.0 copy-done.7
  117.0 0.0 copy-done.8
  117.0 0.0 copy-done.9
  117.1 0.0 copy-done.10
  117.1 1.1 combine.1
  118.2 0.8 first_head.1
  119.0 0.8 collective-permute-done.refs_2_
  119.7 3.3 %head.1 = (f32[1,640]{1,0:T(1,128)}, f32[1,640]{1,0:T(1,128)}) custom-call(s32[1]{0:T(128)S(6)} %copy.19.refs_1_.refs_0_, bf16[16,640]{1,0:T(8,128)(2,1)S(1)} %get-tuple-element.28.refs_0_.refs_1_, bf16[1088,640]{1,0:T(8,128)(2,1)S(1)} %collective-permute-done.refs_2_, bf16[512,640]{1,0:T(8,128)(2,1)S(1)} %get-tuple-element.30.refs_3_, ...), custom_call_target="tpu_custom_call" | custom-call | tf_op jit(solution)/shard_map/head/pallas_call | solution.py:493
Async XLA Ops:
  0.6 37.1 %copy-start = (bf16[1,2560,640]{2,1,0:T(8,128)(2,1)S(1)}, bf16[1,2560,640]{2,1,0:T(8,128)(2,1)}, u32[]{:S(2)}) copy-start(bf16[1,2560,640]{2,1,0:T(8,128)(2,1)} %param.27) | copy-start | bytes 9830404
  42.6 74.4 %copy-start.1 = (bf16[1,256,640]{2,1,0:T(8,128)(2,1)S(1)}, bf16[1,256,640]{2,1,0:T(8,128)(2,1)}, u32[]{:S(2)}) copy-start(bf16[1,256,640]{2,1,0:T(8,128)(2,1)} %param.14) | copy-start | bytes 983044
  42.6 74.4 %copy-start.2 = (bf16[1,16,640]{2,1,0:T(8,128)(2,1)S(1)}, bf16[1,16,640]{2,1,0:T(8,128)(2,1)}, u32[]{:S(2)}) copy-start(bf16[1,16,640]{2,1,0:T(8,128)(2,1)} %param.15) | copy-start | bytes 61444
  42.6 74.4 %copy-start.3 = (s32[1,256]{1,0:T(1,128)S(1)}, s32[1,256]{1,0:T(1,128)}, u32[]{:S(2)}) copy-start(s32[1,256]{1,0:T(1,128)} %refs_0_.3) | copy-start | bytes 3076
  42.6 74.4 %copy-start.4 = (s32[1,256]{1,0:T(1,128)S(1)}, s32[1,256]{1,0:T(1,128)}, u32[]{:S(2)}) copy-start(s32[1,256]{1,0:T(1,128)} %refs_1_.2) | copy-start | bytes 3076
  42.6 74.4 %copy-start.5 = (s32[1,256]{1,0:T(1,128)S(1)}, s32[1,256]{1,0:T(1,128)}, u32[]{:S(2)}) copy-start(s32[1,256]{1,0:T(1,128)} %refs_2_.3) | copy-start | bytes 3076
  42.6 74.4 %copy-start.6 = (f32[1,256]{1,0:T(1,128)S(1)}, f32[1,256]{1,0:T(1,128)}, u32[]{:S(2)}) copy-start(f32[1,256]{1,0:T(1,128)} %refs_6_.3) | copy-start | bytes 3076
  42.6 74.4 %copy-start.7 = (s32[1,16]{1,0:T(1,128)S(1)}, s32[1,16]{1,0:T(1,128)}, u32[]{:S(2)}) copy-start(s32[1,16]{1,0:T(1,128)} %refs_3_.3) | copy-start | bytes 196
  42.6 74.4 %copy-start.8 = (s32[1,16]{1,0:T(1,128)S(1)}, s32[1,16]{1,0:T(1,128)}, u32[]{:S(2)}) copy-start(s32[1,16]{1,0:T(1,128)} %refs_4_.3) | copy-start | bytes 196
  42.7 74.4 %copy-start.9 = (s32[1,16]{1,0:T(1,128)S(1)}, s32[1,16]{1,0:T(1,128)}, u32[]{:S(2)}) copy-start(s32[1,16]{1,0:T(1,128)} %refs_5_.3) | copy-start | bytes 196
  42.7 74.4 %copy-start.10 = (f32[1,16]{1,0:T(1,128)S(1)}, f32[1,16]{1,0:T(1,128)}, u32[]{:S(2)}) copy-start(f32[1,16]{1,0:T(1,128)} %refs_7_.3) | copy-start | bytes 196
  111.8 7.9 %collective-permute-start = (bf16[1088,640]{1,0:T(8,128)(2,1)S(1)}, bf16[1088,640]{1,0:T(8,128)(2,1)S(1)}, u32[]{:S(2)}, u32[]{:S(2)}) collective-permute-start(bf16[1088,640]{1,0:T(8,128)(2,1)S(1)} %bitcast.16), channel_id=1, source_target_pairs={{0,1},{1,0},{2,3},{3,2},{4,5},{5,4},{6,7},{7,6},{8,9},{9,8},{10,11... | collective-permute-start | bytes 4177928 | tf_op jit(solution)/shard_map/ppermute | solution.py:470

commit v5 on v4

--- a/solution.py
+++ b/solution.py
@@ -147,9 +147,10 @@
     place = c - block * sz.stride
     is_txt = r & sz.per
     source = source_of(sz, r)
-    r8 = iota((sz.nx, sz.rows), 0)
-    c8 = iota((sz.nx, sz.rows), 1)
-    wanted = (c8 == (r8 * sz.cores + my_core) * sz.stride + sz.slots + 1) & ((r8 & 1) == (my_x & 1))
+    r8 = iota((sz.part, sz.rows), 0)
+    c8 = iota((sz.part, sz.rows), 1)
+    named = (r8 * 2 + (my_x & 1)) * sz.cores + my_core
+    wanted = (c8 == named * sz.stride + sz.slots + 1) & (r8 < sz.per)
     weighing = jnp.where(c == source * sz.stride + sz.slots, 1.0, 0.0)
     labelling = jnp.where(wanted, 1.0, 0.0)
     held = dot(jnp.concatenate([weighing, labelling], 0).astype(bf16), x)
@@ -181,8 +182,9 @@
         group = (e % sz.cores) * 2 + (e // sz.cores) % 2
         blocks.append(pool[group * sz.part : (group + 1) * sz.part, :])
     back_ref[...] = jnp.concatenate(blocks, 0).astype(bf16)
-    lane = iota((sz.nx, sz.feat), 1)
-    label_ref[...] = jnp.where((lane == line) | (lane == line + 128), labels, 0.0).astype(bf16)
+    lane = iota((sz.part, 128), 1)
+    low = jnp.where(lane == line + 64, labels[:, 128:256], 0.0)
+    label_ref[...] = jnp.where(lane == line, labels[:, :128], low).astype(bf16)
 
 
 def normalize_kernel(sz, back, label, out, copies):
@@ -196,8 +198,8 @@
     left = (place == spare) & (owner == source_of(sz, r + group * sz.part))
     pooled = dot(one_hot((place == sz.stride + r) | left), back[...])
     norm = jnp.sqrt(jnp.sum(pooled * pooled, axis=1, keepdims=True) + 1e-06)
-    block = jnp.concatenate([(pooled / norm).astype(bf16), label[...]], 0)
-    out[...] = block
+    out[...] = (pooled / norm).astype(bf16)
+    block = jnp.concatenate([out[...], label[...]], 1)
     for at in range(0, copies.shape[0], block.shape[0]):
         copies[at : at + block.shape[0], :] = block
 
@@ -213,7 +215,7 @@
 
 
 def merge_kernel(sz, got, copies):
-    size = sz.part + sz.nx
+    size = sz.part
     members = got.shape[0] // size
     count = members * sz.per
     bits = sz.per.bit_length() - 1
@@ -222,10 +224,15 @@
     is_txt = jnp.where(r >= count, 1, 0)
     pair = r - is_txt * count
     place = (pair >> bits) * size + is_txt * sz.per + (pair & (sz.per - 1))
-    is_label = r >= 2 * count
-    label = (c & (size - 1)) == r - 2 * count + sz.part
-    chosen = (is_label & label) | (jnp.logical_not(is_label) & (c == place))
-    block = dot(one_hot(chosen), got[...]).astype(bf16)
+    x = r - 2 * count
+    label = ((c & (size - 1)) == (x >> 1)) & (((c >> (bits + 1)) & 1) == (x & 1))
+    chosen = ((r >= 2 * count) & label) | ((r < 2 * count) & (c == place))
+    all_rows = dot(one_hot(chosen), got[...]).astype(bf16)
+    labels = all_rows[2 * count :, sz.feat :]
+    padding = jnp.zeros((sz.nx, sz.feat - 128), bf16)
+    block = jnp.concatenate(
+        [all_rows[: 2 * count, : sz.feat], jnp.concatenate([labels, padding], 1)], 0
+    )
     for at in range(0, copies.shape[0], block.shape[0]):
         copies[at : at + block.shape[0], :] = block
 
@@ -233,12 +240,12 @@
 def unpack(sz, got, images, texts):
     each = sz.half // sz.nz
     size = 2 * each + sz.nx
-    table = jnp.zeros((sz.nx, 256), f32)
+    table = jnp.zeros((sz.nx, 128), f32)
     for b in range(sz.nz):
         at, to = b * size, b * each
         images[to : to + each, :] = got[at : at + each, :]
         texts[to : to + each, :] = got[at + each : at + 2 * each, :]
-        table = table + got[at + 2 * each : at + size, 0:256].astype(f32)
+        table = table + got[at + 2 * each : at + size, 0:128].astype(f32)
     return table
 
 
@@ -256,7 +263,7 @@
         row_totals[at : at + tile, :] = jnp.sum(scores, axis=1, keepdims=True)
         totals = totals + jnp.sum(scores, axis=0, keepdims=True)
     column_totals[...] = totals
-    strips[...] = exp_scores(own[: sz.part, :], texts[...])
+    strips[...] = exp_scores(own[...], texts[...])
 
 
 def head_kernel(
@@ -277,7 +284,7 @@
         return jnp.where(core == my_core, 0, half) + place
 
     names = [table_a[...], unpack(sz, theirs, images_b, texts_b)]
-    near = own[: sz.part, :]
+    near = own[...]
     tile = min(256, half)
     columns = [columns_a[...], jnp.zeros((1, half), f32)]
     rows = [[rows_a[at : at + tile, :] for at in range(0, half, tile)], []]
@@ -306,31 +313,30 @@
     own_row = iota((sz.part, sz.feat), 0) - (my_x >> 1)
     img_grad[...] = jnp.sum(jnp.where(own_row == 0, grad, 0.0), axis=0, keepdims=True)
 
-    lane = iota((sz.nx, 128), 1)
-    sub = iota((sz.nx, 128), 0)
+    lane = iota((sz.nx, 64), 1)
+    sub = iota((sz.nx, 64), 0)
     high, low = (pair >> 5).astype(f32), (pair & 31).astype(f32)
     found = []
     for table in names:
-        hit = (table[:, :128] == high) & (table[:, 128:] == low) & (lane < sz.lines)
+        hit = (table[:, :64] == high) & (table[:, 64:] == low) & (lane < sz.lines)
 
         def summed(value):
             value = jnp.where(hit, value, 0.0)
             return jnp.sum(jnp.sum(value, axis=0, keepdims=True), axis=1, keepdims=True)
 
-        found.append([summed(v) for v in (lane.astype(f32), sub.astype(f32), jnp.ones((sz.nx, 128), f32))])
+        found.append([summed(v) for v in (lane.astype(f32), sub.astype(f32), jnp.ones((sz.nx, 64), f32))])
     found_line = (found[0][0] + found[1][0]).astype(i32)
     found_x = (found[0][1] + found[1][1]).astype(i32)
     found_core = jnp.where(found[1][2] > 0.5, 1 - my_core, my_core)
     named = position(found_line, found_x, found_core)
-    strips = [exp_scores(images[...], near) for images in (images_a, images_b)]
-    own_columns = sum(jnp.sum(strip, axis=0, keepdims=True) for strip in strips)
+    strips = [exp_scores(near, images[...]) for images in (images_a, images_b)]
+    own_columns = sum(jnp.sum(strip, axis=1, keepdims=True) for strip in strips)
     grad = jnp.zeros((sz.part, sz.feat), f32)
     for a, images in enumerate((images_a, images_b)):
-        for t, at in enumerate(range(0, half, tile)):
-            strip = strips[a][at : at + tile, :]
-            match = jnp.where(iota((tile, sz.part), 0) + a * half + at == named, 2.0, 0.0)
-            scores = strip / rows[a][t] + strip / own_columns - match
-            grad = grad + dot(scores.astype(bf16), images[at : at + tile, :], TN)
+        across = [jnp.transpose(jnp.broadcast_to(total, (tile, 128)))[0:1, :] for total in rows[a]]
+        match = jnp.where(iota((sz.part, half), 1) + a * half == named, 2.0, 0.0)
+        scores = strips[a] / jnp.concatenate(across, 1) + strips[a] / own_columns - match
+        grad = grad + dot(scores.astype(bf16), images[...])
     txt_grad[...] = jnp.sum(jnp.where(own_row == sz.per, grad, 0.0), axis=0, keepdims=True)
 
 
@@ -427,11 +433,12 @@
     )(text_counts, pair_labels, *[in_hbm(v) for v in (*routes, *gates, img, txt, w_in[0])])
 
     def exchange(rows, count, axes="expert", groups=None):
-        rows = rows.reshape(count, rows.shape[0] // count, feat)
+        width = rows.shape[1]
+        rows = rows.reshape(count, rows.shape[0] // count, width)
         rows = lax.all_to_all(
             rows, axes, split_axis=0, concat_axis=0, tiled=True, axis_index_groups=groups
         )
-        return rows.reshape(-1, feat)
+        return rows.reshape(-1, width)
 
     received = exchange(packed, sz.owners)
     back_rows = sz.owners * sz.back
@@ -439,7 +446,7 @@
         bind(expert_kernel, sz),
         (
             jax.ShapeDtypeStruct((back_rows, feat), bf16),
-            jax.ShapeDtypeStruct((sz.nx, feat), bf16),
+            jax.ShapeDtypeStruct((sz.part, 128), bf16),
         ),
         in_specs=[vmem, vmem, hbm, vmem],
         scratch_shapes=[pltpu.VMEM((ff, feat), bf16), pltpu.SemaphoreType.DMA],
@@ -448,12 +455,11 @@
     )(received, w_in_held, w_out[0], means)
     returned = exchange(rows, sz.owners)
 
-    size = sz.part + sz.nx
     own, copies = call(
         bind(normalize_kernel, sz),
         (
-            jax.ShapeDtypeStruct((size, feat), bf16),
-            jax.ShapeDtypeStruct((2 * sz.ny * size, feat), bf16),
+            jax.ShapeDtypeStruct((sz.part, feat), bf16),
+            jax.ShapeDtypeStruct((2 * sz.ny * sz.part, feat + 128), bf16),
         ),
         name="normalize",
     )(returned, labels)
@@ -482,7 +488,7 @@
         bind(first_head_kernel, sz),
         (
             *halves,
-            jax.ShapeDtypeStruct((sz.nx, 256), f32),
+            jax.ShapeDtypeStruct((sz.nx, 128), f32),
             jax.ShapeDtypeStruct((sz.half, 1), f32),
             jax.ShapeDtypeStruct((1, sz.half), f32),
             jax.ShapeDtypeStruct((sz.part, sz.half), f32),

time: 123 us -> 122 us (level)
  no operation moved by 1% of the time
where the time goes in v5:
time: 122 us
  blocking collectives  101 us (83%)
  Pallas kernels  12.8 us (10%)
  starting transfers between devices  4.61 us (4%)
  between operations  2.44 us (2%)
    all_to_all x4, blocking collectives, exchange(): lax.all_to_all(rows, axes, split_axis=0, concat_axis=0, tiled=True, axis_...  101 us
    pallas_call x1, Pallas kernels, per_device(): call(bind(expert_kernel, sz), (jax.ShapeDtypeStruct((back_rows, feat), bf...  4.83 us
    ppermute x1, starting transfers between devices, per_device(): theirs = lax.ppermute(mine, both, pairs)  4.61 us
    pallas_call x1, Pallas kernels, per_device(): call(bind(head_kernel, sz), (jax.ShapeDtypeStruct((1, feat), f32), jax.Sh...  3.25 us
  transfers between devices with their start and end apart: 1, of which 1 were waited for; matrix products, arithmetic and copies ran while one was open for 0% of the time, Pallas kernels for 2%

profile of v5, /device:TPU:1, one launch (start us, length us, event | category | flops | bytes accessed | tf_op | source)
XLA Modules:
  0.0 121.7 jit_solution(11340592450741951228)
XLA Ops:
  0.6 0.0 copy-start
  2.2 2.3 %dispatch.1 = (bf16[384,640]{1,0:T(8,128)(2,1)S(1)}, f32[8,640]{1,0:T(8,128)S(1)}, bf16[640,2560]{1,0:T(8,128)(2,1)S(1)}) custom-call(s32[1]{0:T(128)S(6)} %copy.18.refs_0_, s32[1]{0:T(128)S(6)} %copy.19.refs_1_.refs_0_, s32[1,256]{1,0:T(1,128)} %refs_0_.3, s32[1,256]{1,0:T(1,128)} %refs_1_.2, s32[1,256]{1,0:T(1,128)} %refs_2_.3, s32[1,16]{1,0:T(1,128)} %refs_3_.3, ...), custom_call_target="tpu_custom_call" | custom-call | tf_op jit(solution)/shard_map/dispatch/pallas_call | solution.py:417
  4.5 33.3 %all_to_all.20 = bf16[16,24,640]{2,1,0:T(8,128)(2,1)S(1)} all-to-all(bf16[16,24,640]{2,1,0:T(8,128)(2,1)S(1)} %bitcast.25), channel_id=1, replica_groups=mesh['dp'=64,'expert'=16] {'expert'}, dimensions={0} | all-to-all | bytes 983040 | tf_op jit(solution)/shard_map/all_to_all | solution.py:438
  37.8 0.0 copy-done
  37.8 4.8 %expert.1 = (bf16[512,640]{1,0:T(8,128)(2,1)S(1)}, bf16[8,128]{1,0:T(8,128)(2,1)S(1)}) custom-call(bf16[384,640]{1,0:T(8,128)(2,1)S(1)} %bitcast.20, bf16[640,2560]{1,0:T(8,128)(2,1)S(1)} %get-tuple-element.22.refs_1_, bf16[2560,640]{1,0:T(8,128)(2,1)S(1)} %bitcast.19, f32[8,640]{1,0:T(8,128)S(1)} %get-tuple-element.23.refs_3_), custom_call_target="tpu_custom_call" | custom-call | tf_op jit(solution)/shard_map/expert/pallas_call | solution.py:445
  42.6 0.0 copy-start.1
  42.6 0.0 copy-start.2
  42.6 0.0 copy-start.3
  42.6 0.0 copy-start.4
  42.7 0.0 copy-start.5
  42.7 0.0 copy-start.6
  42.7 0.0 copy-start.7
  42.7 0.0 copy-start.8
  42.7 0.0 copy-start.9
  42.7 0.0 copy-start.10
  42.7 23.0 %all_to_all.21 = bf16[16,32,640]{2,1,0:T(8,128)(2,1)S(1)} all-to-all(bf16[16,32,640]{2,1,0:T(8,128)(2,1)S(1)} %bitcast.24), channel_id=1, replica_groups=mesh['dp'=64,'expert'=16] {'expert'}, dimensions={0} | all-to-all | bytes 1310720 | tf_op jit(solution)/shard_map/all_to_all | solution.py:438
  65.8 0.3 normalize.1
  66.1 16.2 %all_to_all.22 = bf16[16,8,768]{2,1,0:T(8,128)(2,1)S(1)} all-to-all(bf16[16,8,768]{2,1,0:T(8,128)(2,1)S(1)} %bitcast.26), channel_id=1, replica_groups={{0,2,128,130,256,258,384,386,512,514,640,642,768,770,896,898},{4,6,132,..., dimensions={0} | all-to-all | bytes 393216 | tf_op jit(solution)/shard_map/all_to_all | solution.py:438
  82.3 0.2 merge.1
  82.5 28.5 %all_to_all.23 = bf16[8,136,640]{2,1,0:T(8,128)(2,1)S(1)} all-to-all(bf16[8,136,640]{2,1,0:T(8,128)(2,1)S(1)} %bitcast.18), channel_id=1, replica_groups={{0,16,32,48,64,80,96,112},{2,18,34,50,66,82,98,114},{4,20,36,52,68,84,1..., dimensions={0} | all-to-all | bytes 2785280 | tf_op jit(solution)/shard_map/all_to_all | solution.py:438
  111.0 4.6 %collective-permute-start = (bf16[1088,640]{1,0:T(8,128)(2,1)S(1)}, bf16[1088,640]{1,0:T(8,128)(2,1)S(1)}, u32[]{:S(2)}, u32[]{:S(2)}) collective-permute-start(bf16[1088,640]{1,0:T(8,128)(2,1)S(1)} %bitcast.16), channel_id=1, source_target_pairs={{0,1},{1,0},{2,3},{3,2},{4,5},{5,4},{6,7},{7,6},{8,9},{9,8},{10,11... | collective-permute-start | bytes 4177928 | tf_op jit(solution)/shard_map/ppermute | solution.py:476
  115.7 0.0 copy-done.1
  115.7 0.0 copy-done.2
  115.7 0.0 copy-done.3
  115.7 0.0 copy-done.4
  115.7 0.0 copy-done.5
  115.7 0.0 copy-done.6
  115.7 0.0 copy-done.7
  115.7 0.0 copy-done.8
  115.7 0.0 copy-done.9
  115.7 0.0 copy-done.10
  115.8 1.1 combine.1
  116.9 0.8 first_head.1
  117.7 0.8 collective-permute-done.refs_2_
  118.4 3.2 %head.1 = (f32[1,640]{1,0:T(1,128)}, f32[1,640]{1,0:T(1,128)}) custom-call(s32[1]{0:T(128)S(6)} %copy.19.refs_1_.refs_0_, bf16[8,640]{1,0:T(8,128)(2,1)S(1)} %get-tuple-element.28.refs_0_.refs_1_, bf16[1088,640]{1,0:T(8,128)(2,1)S(1)} %collective-permute-done.refs_2_, bf16[512,640]{1,0:T(8,128)(2,1)S(1)} %get-tuple-element.30.refs_3_, ...), custom_call_target="tpu_custom_call" | custom-call | tf_op jit(solution)/shard_map/head/pallas_call | solution.py:499
Async XLA Ops:
  0.6 37.1 %copy-start = (bf16[1,2560,640]{2,1,0:T(8,128)(2,1)S(1)}, bf16[1,2560,640]{2,1,0:T(8,128)(2,1)}, u32[]{:S(2)}) copy-start(bf16[1,2560,640]{2,1,0:T(8,128)(2,1)} %param.27) | copy-start | bytes 9830404
  42.6 73.0 %copy-start.1 = (bf16[1,256,640]{2,1,0:T(8,128)(2,1)S(1)}, bf16[1,256,640]{2,1,0:T(8,128)(2,1)}, u32[]{:S(2)}) copy-start(bf16[1,256,640]{2,1,0:T(8,128)(2,1)} %param.14) | copy-start | bytes 983044
  42.6 73.0 %copy-start.2 = (bf16[1,16,640]{2,1,0:T(8,128)(2,1)S(1)}, bf16[1,16,640]{2,1,0:T(8,128)(2,1)}, u32[]{:S(2)}) copy-start(bf16[1,16,640]{2,1,0:T(8,128)(2,1)} %param.15) | copy-start | bytes 61444
  42.6 73.0 %copy-start.3 = (s32[1,256]{1,0:T(1,128)S(1)}, s32[1,256]{1,0:T(1,128)}, u32[]{:S(2)}) copy-start(s32[1,256]{1,0:T(1,128)} %refs_0_.3) | copy-start | bytes 3076
  42.6 73.0 %copy-start.4 = (s32[1,256]{1,0:T(1,128)S(1)}, s32[1,256]{1,0:T(1,128)}, u32[]{:S(2)}) copy-start(s32[1,256]{1,0:T(1,128)} %refs_1_.2) | copy-start | bytes 3076
  42.7 73.0 %copy-start.5 = (s32[1,256]{1,0:T(1,128)S(1)}, s32[1,256]{1,0:T(1,128)}, u32[]{:S(2)}) copy-start(s32[1,256]{1,0:T(1,128)} %refs_2_.3) | copy-start | bytes 3076
  42.7 73.0 %copy-start.6 = (f32[1,256]{1,0:T(1,128)S(1)}, f32[1,256]{1,0:T(1,128)}, u32[]{:S(2)}) copy-start(f32[1,256]{1,0:T(1,128)} %refs_6_.3) | copy-start | bytes 3076
  42.7 73.0 %copy-start.7 = (s32[1,16]{1,0:T(1,128)S(1)}, s32[1,16]{1,0:T(1,128)}, u32[]{:S(2)}) copy-start(s32[1,16]{1,0:T(1,128)} %refs_3_.3) | copy-start | bytes 196
  42.7 73.0 %copy-start.8 = (s32[1,16]{1,0:T(1,128)S(1)}, s32[1,16]{1,0:T(1,128)}, u32[]{:S(2)}) copy-start(s32[1,16]{1,0:T(1,128)} %refs_4_.3) | copy-start | bytes 196
  42.7 73.0 %copy-start.9 = (s32[1,16]{1,0:T(1,128)S(1)}, s32[1,16]{1,0:T(1,128)}, u32[]{:S(2)}) copy-start(s32[1,16]{1,0:T(1,128)} %refs_5_.3) | copy-start | bytes 196
  42.7 73.0 %copy-start.10 = (f32[1,16]{1,0:T(1,128)S(1)}, f32[1,16]{1,0:T(1,128)}, u32[]{:S(2)}) copy-start(f32[1,16]{1,0:T(1,128)} %refs_7_.3) | copy-start | bytes 196
  111.0 7.4 %collective-permute-start = (bf16[1088,640]{1,0:T(8,128)(2,1)S(1)}, bf16[1088,640]{1,0:T(8,128)(2,1)S(1)}, u32[]{:S(2)}, u32[]{:S(2)}) collective-permute-start(bf16[1088,640]{1,0:T(8,128)(2,1)S(1)} %bitcast.16), channel_id=1, source_target_pairs={{0,1},{1,0},{2,3},{3,2},{4,5},{5,4},{6,7},{7,6},{8,9},{9,8},{10,11... | collective-permute-start | bytes 4177928 | tf_op jit(solution)/shard_map/ppermute | solution.py:476

commit v6 on v5

--- a/solution.py
+++ b/solution.py
@@ -72,9 +72,13 @@
 def dispatch_kernel(sz, count_ref, label_ref, *refs):
     sources, (packed, means, weights_ref) = refs[:11], refs[11:14]
     held, sems = refs[14:24], refs[24]
+    pairs = list(zip(sources, held))
+    rows = weights_ref.shape[0] // 4
+    for at in range(0, weights_ref.shape[0], rows):
+        pairs.append((sources[10].at[at : at + rows, :], weights_ref.at[at : at + rows, :]))
     copies = [
         pltpu.make_async_copy(source, target, sems.at[i])
-        for i, (source, target) in enumerate(zip(sources, held + (weights_ref,)))
+        for i, (source, target) in enumerate(pairs)
     ]
     for copy in copies:
         copy.start()
@@ -116,7 +120,8 @@
     counted = one_hot(iota((8, sz.txt_tok), 1) < count)
     txt_mean = dot(counted, txt[...]) / count_f
     means[...] = jnp.where(iota((8, sz.feat), 0) == 0, img_mean, txt_mean)
-    copies[10].wait()
+    for copy in copies[10:]:
+        copy.wait()
 
 
 def source_of(sz, r):
@@ -228,24 +233,23 @@
     label = ((c & (size - 1)) == (x >> 1)) & (((c >> (bits + 1)) & 1) == (x & 1))
     chosen = ((r >= 2 * count) & label) | ((r < 2 * count) & (c == place))
     all_rows = dot(one_hot(chosen), got[...]).astype(bf16)
-    labels = all_rows[2 * count :, sz.feat :]
-    padding = jnp.zeros((sz.nx, sz.feat - 128), bf16)
-    block = jnp.concatenate(
-        [all_rows[: 2 * count, : sz.feat], jnp.concatenate([labels, padding], 1)], 0
-    )
+    slabs = [all_rows[: 2 * count, at : at + 128] for at in range(0, sz.feat, 128)]
+    block = jnp.concatenate(slabs + [all_rows[2 * count :, sz.feat :]], 0)
     for at in range(0, copies.shape[0], block.shape[0]):
         copies[at : at + block.shape[0], :] = block
 
 
 def unpack(sz, got, images, texts):
     each = sz.half // sz.nz
-    size = 2 * each + sz.nx
+    size = got.shape[0] // sz.nz
     table = jnp.zeros((sz.nx, 128), f32)
     for b in range(sz.nz):
         at, to = b * size, b * each
-        images[to : to + each, :] = got[at : at + each, :]
-        texts[to : to + each, :] = got[at + each : at + 2 * each, :]
-        table = table + got[at + 2 * each : at + size, 0:128].astype(f32)
+        for lane in range(0, sz.feat, 128):
+            images[to : to + each, lane : lane + 128] = got[at : at + each, :]
+            texts[to : to + each, lane : lane + 128] = got[at + each : at + 2 * each, :]
+            at += 2 * each
+        table = table + got[at : at + sz.nx, :].astype(f32)
     return table
 
 
@@ -253,7 +257,7 @@
     return jnp.exp(logit_scale * dot(left, right, NT))
 
 
-def first_head_kernel(sz, own, mine, images, texts, table, row_totals, column_totals, strips):
+def first_head_kernel(sz, own, mine, images, texts, table, row_totals, column_totals, image_strip, text_strip):
     half = sz.half
     table[...] = unpack(sz, mine, images, texts)
     tile = min(256, half)
@@ -263,11 +267,12 @@
         row_totals[at : at + tile, :] = jnp.sum(scores, axis=1, keepdims=True)
         totals = totals + jnp.sum(scores, axis=0, keepdims=True)
     column_totals[...] = totals
-    strips[...] = exp_scores(own[...], texts[...])
+    image_strip[...] = exp_scores(own[...], texts[...])
+    text_strip[...] = exp_scores(own[...], images[...])
 
 
 def head_kernel(
-    sz, label_ref, own, theirs, images_a, texts_a, table_a, rows_a, columns_a, strip_a,
+    sz, label_ref, own, theirs, images_a, texts_a, table_a, rows_a, columns_a, strip_a, text_strip_a,
     img_grad, txt_grad, images_b, texts_b,
 ):
     half = sz.half
@@ -329,7 +334,7 @@
     found_x = (found[0][1] + found[1][1]).astype(i32)
     found_core = jnp.where(found[1][2] > 0.5, 1 - my_core, my_core)
     named = position(found_line, found_x, found_core)
-    strips = [exp_scores(near, images[...]) for images in (images_a, images_b)]
+    strips = [text_strip_a[...], exp_scores(near, images_b[...])]
     own_columns = sum(jnp.sum(strip, axis=1, keepdims=True) for strip in strips)
     grad = jnp.zeros((sz.part, sz.feat), f32)
     for a, images in enumerate((images_a, images_b)):
@@ -427,7 +432,7 @@
         + [pltpu.VMEM(keys, i32)] * 3
         + [pltpu.VMEM(counts, f32), pltpu.VMEM(keys, f32)]
         + [pltpu.VMEM((img_tok, feat), bf16), pltpu.VMEM((txt_tok, feat), bf16)]
-        + [pltpu.SemaphoreType.DMA((11,))],
+        + [pltpu.SemaphoreType.DMA((14,))],
         limit=16,
         name="dispatch",
     )(text_counts, pair_labels, *[in_hbm(v) for v in (*routes, *gates, img, txt, w_in[0])])
@@ -465,10 +470,10 @@
     )(returned, labels)
     both = ("dp", "expert")
     got = exchange(copies, 2 * sz.ny, both, split_groups(sz, True))
-    size = 2 * sz.ny * sz.nx + sz.nx
+    size = 2 * sz.ny * sz.nx * (feat // 128) + sz.nx
     copies = call(
         bind(merge_kernel, sz),
-        jax.ShapeDtypeStruct((sz.nz * size, feat), bf16),
+        jax.ShapeDtypeStruct((sz.nz * size, 128), bf16),
         name="merge",
     )(got)
     mine = exchange(copies, sz.nz, both, split_groups(sz, False))
@@ -492,6 +497,7 @@
             jax.ShapeDtypeStruct((sz.half, 1), f32),
             jax.ShapeDtypeStruct((1, sz.half), f32),
             jax.ShapeDtypeStruct((sz.part, sz.half), f32),
+            jax.ShapeDtypeStruct((sz.part, sz.half), f32),
         ),
         cost=(2 * sz.half * sz.half * feat, 4 * sz.half * feat, sz.half * sz.half),
         name="first_head",
@@ -502,7 +508,7 @@
             jax.ShapeDtypeStruct((1, feat), f32),
             jax.ShapeDtypeStruct((1, feat), f32),
         ),
-        in_specs=[smem] + [vmem] * 8,
+        in_specs=[smem] + [vmem] * 9,
         scratch_shapes=[pltpu.VMEM((sz.half, feat), bf16)] * 2,
         name="head",
     )(pair_labels, own, theirs, *first)

time: 122 us -> 121 us (level)
  no operation moved by 1% of the time
where the time goes in v6:
time: 121 us
  blocking collectives  100 us (83%)
  Pallas kernels  12.8 us (11%)
  starting transfers between devices  4.61 us (4%)
  between operations  2.44 us (2%)
    all_to_all x4, blocking collectives, exchange(): lax.all_to_all(rows, axes, split_axis=0, concat_axis=0, tiled=True, axis_...  100 us
    pallas_call x1, Pallas kernels, per_device(): call(bind(expert_kernel, sz), (jax.ShapeDtypeStruct((back_rows, feat), bf...  4.83 us
    ppermute x1, starting transfers between devices, per_device(): theirs = lax.ppermute(mine, both, pairs)  4.61 us
    pallas_call x1, Pallas kernels, per_device(): call(bind(head_kernel, sz), (jax.ShapeDtypeStruct((1, feat), f32), jax.Sh...  3.11 us
  transfers between devices with their start and end apart: 1, of which 1 were waited for; matrix products, arithmetic and copies ran while one was open for 0% of the time, Pallas kernels for 2%

profile of v6, /device:TPU:1, one launch (start us, length us, event | category | flops | bytes accessed | tf_op | source)
XLA Modules:
  0.0 120.7 jit_solution(4407216705293269134)
XLA Ops:
  0.6 0.0 copy-start
  2.2 2.2 %dispatch.1 = (bf16[384,640]{1,0:T(8,128)(2,1)S(1)}, f32[8,640]{1,0:T(8,128)S(1)}, bf16[640,2560]{1,0:T(8,128)(2,1)S(1)}) custom-call(s32[1]{0:T(128)S(6)} %copy.18.refs_0_, s32[1]{0:T(128)S(6)} %copy.19.refs_1_.refs_0_, s32[1,256]{1,0:T(1,128)} %refs_0_.3, s32[1,256]{1,0:T(1,128)} %refs_1_.2, s32[1,256]{1,0:T(1,128)} %refs_2_.3, s32[1,16]{1,0:T(1,128)} %refs_3_.3, ...), custom_call_target="tpu_custom_call" | custom-call | tf_op jit(solution)/shard_map/dispatch/pallas_call | solution.py:422
  4.5 33.3 %all_to_all.20 = bf16[16,24,640]{2,1,0:T(8,128)(2,1)S(1)} all-to-all(bf16[16,24,640]{2,1,0:T(8,128)(2,1)S(1)} %bitcast.25), channel_id=1, replica_groups=mesh['dp'=64,'expert'=16] {'expert'}, dimensions={0} | all-to-all | bytes 983040 | tf_op jit(solution)/shard_map/all_to_all | solution.py:443
  37.8 0.0 copy-done
  37.8 4.8 %expert.1 = (bf16[512,640]{1,0:T(8,128)(2,1)S(1)}, bf16[8,128]{1,0:T(8,128)(2,1)S(1)}) custom-call(bf16[384,640]{1,0:T(8,128)(2,1)S(1)} %bitcast.20, bf16[640,2560]{1,0:T(8,128)(2,1)S(1)} %get-tuple-element.23.refs_1_, bf16[2560,640]{1,0:T(8,128)(2,1)S(1)} %bitcast.19, f32[8,640]{1,0:T(8,128)S(1)} %get-tuple-element.24.refs_3_), custom_call_target="tpu_custom_call" | custom-call | tf_op jit(solution)/shard_map/expert/pallas_call | solution.py:450
  42.6 0.0 copy-start.1
  42.6 0.0 copy-start.2
  42.6 0.0 copy-start.3
  42.6 0.0 copy-start.4
  42.6 0.0 copy-start.5
  42.7 0.0 copy-start.6
  42.7 0.0 copy-start.7
  42.7 0.0 copy-start.8
  42.7 0.0 copy-start.9
  42.7 0.0 copy-start.10
  42.7 23.0 %all_to_all.21 = bf16[16,32,640]{2,1,0:T(8,128)(2,1)S(1)} all-to-all(bf16[16,32,640]{2,1,0:T(8,128)(2,1)S(1)} %bitcast.24), channel_id=1, replica_groups=mesh['dp'=64,'expert'=16] {'expert'}, dimensions={0} | all-to-all | bytes 1310720 | tf_op jit(solution)/shard_map/all_to_all | solution.py:443
  65.8 0.3 normalize.1
  66.1 16.2 %all_to_all.22 = bf16[16,8,768]{2,1,0:T(8,128)(2,1)S(1)} all-to-all(bf16[16,8,768]{2,1,0:T(8,128)(2,1)S(1)} %bitcast.26), channel_id=1, replica_groups={{0,2,128,130,256,258,384,386,512,514,640,642,768,770,896,898},{4,6,132,..., dimensions={0} | all-to-all | bytes 393216 | tf_op jit(solution)/shard_map/all_to_all | solution.py:443
  82.2 0.2 merge.1
  82.5 27.8 %all_to_all.23 = bf16[8,648,128]{2,1,0:T(8,128)(2,1)S(1)} all-to-all(bf16[8,648,128]{2,1,0:T(8,128)(2,1)S(1)} %bitcast.18), channel_id=1, replica_groups={{0,16,32,48,64,80,96,112},{2,18,34,50,66,82,98,114},{4,20,36,52,68,84,1..., dimensions={0} | all-to-all | bytes 2654208 | tf_op jit(solution)/shard_map/all_to_all | solution.py:443
  110.3 4.6 %collective-permute-start = (bf16[5184,128]{1,0:T(8,128)(2,1)S(1)}, bf16[5184,128]{1,0:T(8,128)(2,1)S(1)}, u32[]{:S(2)}, u32[]{:S(2)}) collective-permute-start(bf16[5184,128]{1,0:T(8,128)(2,1)S(1)} %bitcast.16), channel_id=1, source_target_pairs={{0,1},{1,0},{2,3},{3,2},{4,5},{5,4},{6,7},{7,6},{8,9},{9,8},{10,11... | collective-permute-start | bytes 3981320 | tf_op jit(solution)/shard_map/ppermute | solution.py:481
  114.9 0.0 copy-done.1
  114.9 0.0 copy-done.2
  114.9 0.0 copy-done.3
  114.9 0.0 copy-done.4
  115.0 0.0 copy-done.5
  115.0 0.0 copy-done.6
  115.0 0.0 copy-done.7
  115.0 0.0 copy-done.8
  115.0 0.0 copy-done.9
  115.0 0.0 copy-done.10
  115.0 1.2 combine.1
  116.2 1.0 first_head.1
  117.1 0.4 collective-permute-done.refs_2_
  117.6 3.1 %head.1 = (f32[1,640]{1,0:T(1,128)}, f32[1,640]{1,0:T(1,128)}) custom-call(s32[1]{0:T(128)S(6)} %copy.19.refs_1_.refs_0_, bf16[8,640]{1,0:T(8,128)(2,1)S(1)} %get-tuple-element.29.refs_0_.refs_1_, bf16[5184,128]{1,0:T(8,128)(2,1)S(1)} %collective-permute-done.refs_2_, bf16[512,640]{1,0:T(8,128)(2,1)S(1)} %get-tuple-element.31.refs_3_, ...), custom_call_target="tpu_custom_call" | custom-call | tf_op jit(solution)/shard_map/head/pallas_call | solution.py:505
Async XLA Ops:
  0.6 37.1 %copy-start = (bf16[1,2560,640]{2,1,0:T(8,128)(2,1)S(1)}, bf16[1,2560,640]{2,1,0:T(8,128)(2,1)}, u32[]{:S(2)}) copy-start(bf16[1,2560,640]{2,1,0:T(8,128)(2,1)} %param.27) | copy-start | bytes 9830404
  42.6 72.3 %copy-start.1 = (bf16[1,256,640]{2,1,0:T(8,128)(2,1)S(1)}, bf16[1,256,640]{2,1,0:T(8,128)(2,1)}, u32[]{:S(2)}) copy-start(bf16[1,256,640]{2,1,0:T(8,128)(2,1)} %param.14) | copy-start | bytes 983044
  42.6 72.3 %copy-start.2 = (bf16[1,16,640]{2,1,0:T(8,128)(2,1)S(1)}, bf16[1,16,640]{2,1,0:T(8,128)(2,1)}, u32[]{:S(2)}) copy-start(bf16[1,16,640]{2,1,0:T(8,128)(2,1)} %param.15) | copy-start | bytes 61444
  42.6 72.3 %copy-start.3 = (s32[1,256]{1,0:T(1,128)S(1)}, s32[1,256]{1,0:T(1,128)}, u32[]{:S(2)}) copy-start(s32[1,256]{1,0:T(1,128)} %refs_0_.3) | copy-start | bytes 3076
  42.6 72.3 %copy-start.4 = (s32[1,256]{1,0:T(1,128)S(1)}, s32[1,256]{1,0:T(1,128)}, u32[]{:S(2)}) copy-start(s32[1,256]{1,0:T(1,128)} %refs_1_.2) | copy-start | bytes 3076
  42.6 72.3 %copy-start.5 = (s32[1,256]{1,0:T(1,128)S(1)}, s32[1,256]{1,0:T(1,128)}, u32[]{:S(2)}) copy-start(s32[1,256]{1,0:T(1,128)} %refs_2_.3) | copy-start | bytes 3076
  42.7 72.3 %copy-start.6 = (f32[1,256]{1,0:T(1,128)S(1)}, f32[1,256]{1,0:T(1,128)}, u32[]{:S(2)}) copy-start(f32[1,256]{1,0:T(1,128)} %refs_6_.3) | copy-start | bytes 3076
  42.7 72.3 %copy-start.7 = (s32[1,16]{1,0:T(1,128)S(1)}, s32[1,16]{1,0:T(1,128)}, u32[]{:S(2)}) copy-start(s32[1,16]{1,0:T(1,128)} %refs_3_.3) | copy-start | bytes 196
  42.7 72.3 %copy-start.8 = (s32[1,16]{1,0:T(1,128)S(1)}, s32[1,16]{1,0:T(1,128)}, u32[]{:S(2)}) copy-start(s32[1,16]{1,0:T(1,128)} %refs_4_.3) | copy-start | bytes 196
  42.7 72.3 %copy-start.9 = (s32[1,16]{1,0:T(1,128)S(1)}, s32[1,16]{1,0:T(1,128)}, u32[]{:S(2)}) copy-start(s32[1,16]{1,0:T(1,128)} %refs_5_.3) | copy-start | bytes 196
  42.7 72.3 %copy-start.10 = (f32[1,16]{1,0:T(1,128)S(1)}, f32[1,16]{1,0:T(1,128)}, u32[]{:S(2)}) copy-start(f32[1,16]{1,0:T(1,128)} %refs_7_.3) | copy-start | bytes 196
  110.3 7.3 %collective-permute-start = (bf16[5184,128]{1,0:T(8,128)(2,1)S(1)}, bf16[5184,128]{1,0:T(8,128)(2,1)S(1)}, u32[]{:S(2)}, u32[]{:S(2)}) collective-permute-start(bf16[5184,128]{1,0:T(8,128)(2,1)S(1)} %bitcast.16), channel_id=1, source_target_pairs={{0,1},{1,0},{2,3},{3,2},{4,5},{5,4},{6,7},{7,6},{8,9},{9,8},{10,11... | collective-permute-start | bytes 3981320 | tf_op jit(solution)/shard_map/ppermute | solution.py:481

commit v7 on v6

--- a/solution.py
+++ b/solution.py
@@ -134,12 +134,9 @@
     return 0.5 * x * (1.0 + lax.erf(x * np.float32(np.sqrt(0.5))))
 
 
-def expert_kernel(sz, x_ref, w_in, w_out_source, means, back_ref, label_ref, w_out, sem):
-    copy = pltpu.make_async_copy(w_out_source, w_out, sem)
-    copy.start()
+def expert_kernel(sz, x_ref, w_in, w_out, means, back_ref, label_ref):
     x = x_ref[...]
     hidden = gelu(dot(x, w_in[...])).astype(bf16)
-    copy.wait()
     total = dot(hidden, w_out[...])
     out = total.astype(bf16)
     me = lax.axis_index("expert")
@@ -257,6 +254,11 @@
     return jnp.exp(logit_scale * dot(left, right, NT))
 
 
+def along_lanes(column):
+    tall = jnp.broadcast_to(column, (column.shape[0], 128))
+    return jnp.transpose(tall)[0:1, :]
+
+
 def first_head_kernel(sz, own, mine, images, texts, table, row_totals, column_totals, image_strip, text_strip):
     half = sz.half
     table[...] = unpack(sz, mine, images, texts)
@@ -291,24 +293,31 @@
     names = [table_a[...], unpack(sz, theirs, images_b, texts_b)]
     near = own[...]
     tile = min(256, half)
-    columns = [columns_a[...], jnp.zeros((1, half), f32)]
-    rows = [[rows_a[at : at + tile, :] for at in range(0, half, tile)], []]
-    for t, at in enumerate(range(0, half, tile)):
-        scores = exp_scores(images_a[at : at + tile, :], texts_b[...])
-        rows[0][t] = rows[0][t] + jnp.sum(scores, axis=1, keepdims=True)
-        columns[1] = columns[1] + jnp.sum(scores, axis=0, keepdims=True)
-    for at in range(0, half, tile):
-        total = jnp.zeros((tile, 1), f32)
-        for b, texts in enumerate((texts_a, texts_b)):
-            scores = exp_scores(images_b[at : at + tile, :], texts[...])
-            total = total + jnp.sum(scores, axis=1, keepdims=True)
-            columns[b] = columns[b] + jnp.sum(scores, axis=0, keepdims=True)
-        rows[1].append(total)
+
+    def against(left_halves, right):
+        across, down = [], []
+        for left in left_halves:
+            total = jnp.zeros((1, half), f32)
+            for at in range(0, half, tile):
+                rows = left[at : at + tile, :]
+                last = left is left_halves[-1] and at + tile == half
+                scores = exp_scores(jnp.concatenate([rows, near], 0) if last else rows, right[...])
+                own_scores = scores[tile:, :]
+                scores = scores[:tile, :]
+                across.append(along_lanes(jnp.sum(scores, axis=1, keepdims=True)))
+                total = total + jnp.sum(scores, axis=0, keepdims=True)
+            down.append(total)
+        return jnp.concatenate(across, 1), down, own_scores
+
+    rows_ab, (columns_ab,), strip_b = against([images_a], texts_b)
+    columns_b, (rows_ba, rows_bb), text_strip_b = against([texts_a, texts_b], images_b)
+    columns = [columns_a[...] + columns_b[:, :half], columns_ab + columns_b[:, half:]]
+    rows = [along_lanes(rows_a[...]) + rows_ab, rows_ba + rows_bb]
 
     label = label_ref[0]
     owner = label & (sz.owners - 1)
     target = position(label >> (sz.owners.bit_length() - 1), owner >> 1, owner & 1)
-    strips = [strip_a[...], exp_scores(near, texts_b[...])]
+    strips = [strip_a[...], strip_b]
     own_rows = sum(jnp.sum(strip, axis=1, keepdims=True) for strip in strips)
     grad = jnp.zeros((sz.part, sz.feat), f32)
     for b, texts in enumerate((texts_a, texts_b)):
@@ -334,13 +343,12 @@
     found_x = (found[0][1] + found[1][1]).astype(i32)
     found_core = jnp.where(found[1][2] > 0.5, 1 - my_core, my_core)
     named = position(found_line, found_x, found_core)
-    strips = [text_strip_a[...], exp_scores(near, images_b[...])]
+    strips = [text_strip_a[...], text_strip_b]
     own_columns = sum(jnp.sum(strip, axis=1, keepdims=True) for strip in strips)
     grad = jnp.zeros((sz.part, sz.feat), f32)
     for a, images in enumerate((images_a, images_b)):
-        across = [jnp.transpose(jnp.broadcast_to(total, (tile, 128)))[0:1, :] for total in rows[a]]
         match = jnp.where(iota((sz.part, half), 1) + a * half == named, 2.0, 0.0)
-        scores = strips[a] / jnp.concatenate(across, 1) + strips[a] / own_columns - match
+        scores = strips[a] / rows[a] + strips[a] / own_columns - match
         grad = grad + dot(scores.astype(bf16), images[...])
     txt_grad[...] = jnp.sum(jnp.where(own_row == sz.per, grad, 0.0), axis=0, keepdims=True)
 
@@ -453,8 +461,7 @@
             jax.ShapeDtypeStruct((back_rows, feat), bf16),
             jax.ShapeDtypeStruct((sz.part, 128), bf16),
         ),
-        in_specs=[vmem, vmem, hbm, vmem],
-        scratch_shapes=[pltpu.VMEM((ff, feat), bf16), pltpu.SemaphoreType.DMA],
+        in_specs=[vmem] * 4,
         limit=28,
         name="expert",
     )(received, w_in_held, w_out[0], means)

time: 121 us -> 119 us (0.983)
  Pallas kernels: 12.8 us -> 11.3 us
    pallas_call x1, Pallas kernels: 4.83 us -> 3.62 us  [per_device(): call(bind(expert_kernel, sz), (jax.ShapeDtypeStruct((back_rows, feat), bf...]
where the time goes in v7:
time: 119 us
  blocking collectives  100 us (84%)
  Pallas kernels  11.3 us (9%)
  starting transfers between devices  4.61 us (4%)
  between operations  2.44 us (2%)
    all_to_all x4, blocking collectives, exchange(): lax.all_to_all(rows, axes, split_axis=0, concat_axis=0, tiled=True, axis_...  100 us
    ppermute x1, starting transfers between devices, per_device(): theirs = lax.ppermute(mine, both, pairs)  4.61 us
    pallas_call x1, Pallas kernels, per_device(): call(bind(expert_kernel, sz), (jax.ShapeDtypeStruct((back_rows, feat), bf...  3.62 us
    pallas_call x1, Pallas kernels, per_device(): call(bind(head_kernel, sz), (jax.ShapeDtypeStruct((1, feat), f32), jax.Sh...  2.75 us
  transfers between devices with their start and end apart: 1, of which 1 were waited for; matrix products, arithmetic and copies ran while one was open for 0% of the time, Pallas kernels for 2%

profile of v7, /device:TPU:1, one launch (start us, length us, event | category | flops | bytes accessed | tf_op | source)
XLA Modules:
  0.0 119.1 jit_solution(13009005358085749670)
XLA Ops:
  0.6 0.0 copy-start
  2.2 2.2 %dispatch.1 = (bf16[384,640]{1,0:T(8,128)(2,1)S(1)}, f32[8,640]{1,0:T(8,128)S(1)}, bf16[640,2560]{1,0:T(8,128)(2,1)S(1)}) custom-call(s32[1]{0:T(128)S(6)} %copy.18.refs_0_, s32[1]{0:T(128)S(6)} %copy.19.refs_1_.refs_0_, s32[1,256]{1,0:T(1,128)} %refs_0_.3, s32[1,256]{1,0:T(1,128)} %refs_1_.2, s32[1,256]{1,0:T(1,128)} %refs_2_.3, s32[1,16]{1,0:T(1,128)} %refs_3_.3, ...), custom_call_target="tpu_custom_call" | custom-call | tf_op jit(solution)/shard_map/dispatch/pallas_call | solution.py:430
  4.5 33.3 %all_to_all.20 = bf16[16,24,640]{2,1,0:T(8,128)(2,1)S(1)} all-to-all(bf16[16,24,640]{2,1,0:T(8,128)(2,1)S(1)} %bitcast.25), channel_id=1, replica_groups=mesh['dp'=64,'expert'=16] {'expert'}, dimensions={0} | all-to-all | bytes 983040 | tf_op jit(solution)/shard_map/all_to_all | solution.py:451
  37.8 0.0 copy-done
  37.8 3.6 %expert.1 = (bf16[512,640]{1,0:T(8,128)(2,1)S(1)}, bf16[8,128]{1,0:T(8,128)(2,1)S(1)}) custom-call(bf16[384,640]{1,0:T(8,128)(2,1)S(1)} %bitcast.20, bf16[640,2560]{1,0:T(8,128)(2,1)S(1)} %get-tuple-element.23.refs_1_, bf16[2560,640]{1,0:T(8,128)(2,1)S(1)} %bitcast.19, f32[8,640]{1,0:T(8,128)S(1)} %get-tuple-element.24.refs_3_), custom_call_target="tpu_custom_call" | custom-call | tf_op jit(solution)/shard_map/expert/pallas_call | solution.py:458
  41.4 0.0 copy-start.1
  41.4 0.0 copy-start.2
  41.4 0.0 copy-start.3
  41.4 0.0 copy-start.4
  41.4 0.0 copy-start.5
  41.4 0.0 copy-start.6
  41.5 0.0 copy-start.7
  41.5 0.0 copy-start.8
  41.5 0.0 copy-start.9
  41.5 0.0 copy-start.10
  41.5 23.1 %all_to_all.21 = bf16[16,32,640]{2,1,0:T(8,128)(2,1)S(1)} all-to-all(bf16[16,32,640]{2,1,0:T(8,128)(2,1)S(1)} %bitcast.24), channel_id=1, replica_groups=mesh['dp'=64,'expert'=16] {'expert'}, dimensions={0} | all-to-all | bytes 1310720 | tf_op jit(solution)/shard_map/all_to_all | solution.py:451
  64.6 0.3 normalize.1
  64.9 16.2 %all_to_all.22 = bf16[16,8,768]{2,1,0:T(8,128)(2,1)S(1)} all-to-all(bf16[16,8,768]{2,1,0:T(8,128)(2,1)S(1)} %bitcast.26), channel_id=1, replica_groups={{0,2,128,130,256,258,384,386,512,514,640,642,768,770,896,898},{4,6,132,..., dimensions={0} | all-to-all | bytes 393216 | tf_op jit(solution)/shard_map/all_to_all | solution.py:451
  81.0 0.2 merge.1
  81.3 27.8 %all_to_all.23 = bf16[8,648,128]{2,1,0:T(8,128)(2,1)S(1)} all-to-all(bf16[8,648,128]{2,1,0:T(8,128)(2,1)S(1)} %bitcast.18), channel_id=1, replica_groups={{0,16,32,48,64,80,96,112},{2,18,34,50,66,82,98,114},{4,20,36,52,68,84,1..., dimensions={0} | all-to-all | bytes 2654208 | tf_op jit(solution)/shard_map/all_to_all | solution.py:451
  109.1 4.6 %collective-permute-start = (bf16[5184,128]{1,0:T(8,128)(2,1)S(1)}, bf16[5184,128]{1,0:T(8,128)(2,1)S(1)}, u32[]{:S(2)}, u32[]{:S(2)}) collective-permute-start(bf16[5184,128]{1,0:T(8,128)(2,1)S(1)} %bitcast.16), channel_id=1, source_target_pairs={{0,1},{1,0},{2,3},{3,2},{4,5},{5,4},{6,7},{7,6},{8,9},{9,8},{10,11... | collective-permute-start | bytes 3981320 | tf_op jit(solution)/shard_map/ppermute | solution.py:488
  113.7 0.0 copy-done.1
  113.7 0.0 copy-done.2
  113.7 0.0 copy-done.3
  113.7 0.0 copy-done.4
  113.7 0.0 copy-done.5
  113.8 0.0 copy-done.6
  113.8 0.0 copy-done.7
  113.8 0.0 copy-done.8
  113.8 0.0 copy-done.9
  113.8 0.0 copy-done.10
  113.8 1.2 combine.1
  115.0 1.0 first_head.1
  115.9 0.4 collective-permute-done.refs_2_
  116.4 2.7 %head.1 = (f32[1,640]{1,0:T(1,128)}, f32[1,640]{1,0:T(1,128)}) custom-call(s32[1]{0:T(128)S(6)} %copy.19.refs_1_.refs_0_, bf16[8,640]{1,0:T(8,128)(2,1)S(1)} %get-tuple-element.29.refs_0_.refs_1_, bf16[5184,128]{1,0:T(8,128)(2,1)S(1)} %collective-permute-done.refs_2_, bf16[512,640]{1,0:T(8,128)(2,1)S(1)} %get-tuple-element.31.refs_3_, ...), custom_call_target="tpu_custom_call" | custom-call | tf_op jit(solution)/shard_map/head/pallas_call | solution.py:512
Async XLA Ops:
  0.6 37.1 %copy-start = (bf16[1,2560,640]{2,1,0:T(8,128)(2,1)S(1)}, bf16[1,2560,640]{2,1,0:T(8,128)(2,1)}, u32[]{:S(2)}) copy-start(bf16[1,2560,640]{2,1,0:T(8,128)(2,1)} %param.27) | copy-start | bytes 9830404
  41.4 72.3 %copy-start.1 = (bf16[1,256,640]{2,1,0:T(8,128)(2,1)S(1)}, bf16[1,256,640]{2,1,0:T(8,128)(2,1)}, u32[]{:S(2)}) copy-start(bf16[1,256,640]{2,1,0:T(8,128)(2,1)} %param.14) | copy-start | bytes 983044
  41.4 72.3 %copy-start.2 = (bf16[1,16,640]{2,1,0:T(8,128)(2,1)S(1)}, bf16[1,16,640]{2,1,0:T(8,128)(2,1)}, u32[]{:S(2)}) copy-start(bf16[1,16,640]{2,1,0:T(8,128)(2,1)} %param.15) | copy-start | bytes 61444
  41.4 72.3 %copy-start.3 = (s32[1,256]{1,0:T(1,128)S(1)}, s32[1,256]{1,0:T(1,128)}, u32[]{:S(2)}) copy-start(s32[1,256]{1,0:T(1,128)} %refs_0_.3) | copy-start | bytes 3076
  41.4 72.3 %copy-start.4 = (s32[1,256]{1,0:T(1,128)S(1)}, s32[1,256]{1,0:T(1,128)}, u32[]{:S(2)}) copy-start(s32[1,256]{1,0:T(1,128)} %refs_1_.2) | copy-start | bytes 3076
  41.4 72.3 %copy-start.5 = (s32[1,256]{1,0:T(1,128)S(1)}, s32[1,256]{1,0:T(1,128)}, u32[]{:S(2)}) copy-start(s32[1,256]{1,0:T(1,128)} %refs_2_.3) | copy-start | bytes 3076
  41.4 72.3 %copy-start.6 = (f32[1,256]{1,0:T(1,128)S(1)}, f32[1,256]{1,0:T(1,128)}, u32[]{:S(2)}) copy-start(f32[1,256]{1,0:T(1,128)} %refs_6_.3) | copy-start | bytes 3076
  41.5 72.3 %copy-start.7 = (s32[1,16]{1,0:T(1,128)S(1)}, s32[1,16]{1,0:T(1,128)}, u32[]{:S(2)}) copy-start(s32[1,16]{1,0:T(1,128)} %refs_3_.3) | copy-start | bytes 196
  41.5 72.3 %copy-start.8 = (s32[1,16]{1,0:T(1,128)S(1)}, s32[1,16]{1,0:T(1,128)}, u32[]{:S(2)}) copy-start(s32[1,16]{1,0:T(1,128)} %refs_4_.3) | copy-start | bytes 196
  41.5 72.3 %copy-start.9 = (s32[1,16]{1,0:T(1,128)S(1)}, s32[1,16]{1,0:T(1,128)}, u32[]{:S(2)}) copy-start(s32[1,16]{1,0:T(1,128)} %refs_5_.3) | copy-start | bytes 196
  41.5 72.3 %copy-start.10 = (f32[1,16]{1,0:T(1,128)S(1)}, f32[1,16]{1,0:T(1,128)}, u32[]{:S(2)}) copy-start(f32[1,16]{1,0:T(1,128)} %refs_7_.3) | copy-start | bytes 196
  109.1 7.3 %collective-permute-start = (bf16[5184,128]{1,0:T(8,128)(2,1)S(1)}, bf16[5184,128]{1,0:T(8,128)(2,1)S(1)}, u32[]{:S(2)}, u32[]{:S(2)}) collective-permute-start(bf16[5184,128]{1,0:T(8,128)(2,1)S(1)} %bitcast.16), channel_id=1, source_target_pairs={{0,1},{1,0},{2,3},{3,2},{4,5},{5,4},{6,7},{7,6},{8,9},{9,8},{10,11... | collective-permute-start | bytes 3981320 | tf_op jit(solution)/shard_map/ppermute | solution.py:488
